TPU v7x, 32 devices: a whole 2x2x4 slice. The times are simulated.
32 devices in a mesh: expert: 8 (over z, y), slot: 4 (over x, core).
Axes of the slice: x: 2, y: 2, z: 4, core: 2. Of those that a mesh axis runs over, the one named last changes fastest.
Arguments:
- tokens: bfloat16 [4096, 2048], P(('expert', 'slot')), may hold values from -6 to 6
- out_grad: bfloat16 [4096, 2048], P(('expert', 'slot')), may hold values from -6 to 6
- routing: int32 [4096, 1], P(('expert', 'slot')), may hold values from 0 to 7; in each aligned block of 128 rows (0 to 127, 128 to 255, ...) at most 32 rows name the same one
- plan: int32 [8], replicated, may hold values from 0 to 5, as said below
- gate_weight: bfloat16 [8, 2048, 768], P('expert', None, 'slot'), as said below
- up_weight: bfloat16 [8, 2048, 768], P('expert', None, 'slot'), as said below
- down_weight: bfloat16 [8, 768, 2048], P('expert', 'slot'), as said below
- master: float32 [6, 768, 2048], P(None, ('slot', 'expert'))
- moment: float32 [6, 768, 2048], P(None, ('slot', 'expert')), may hold values from -24 to 24
- second: float32 [6, 768, 2048], P(None, ('slot', 'expert')), may hold values from 1 to 400
Outputs:
- token_grad: bfloat16 [4096, 2048], P(('expert', 'slot'))
- new_master: float32 [6, 768, 2048], P(None, ('slot', 'expert'))
- new_moment: float32 [6, 768, 2048], P(None, ('slot', 'expert'))
- new_second: float32 [6, 768, 2048], P(None, ('slot', 'expert'))
- new_down: bfloat16 [8, 768, 2048], P('expert', 'slot')
Inputs may be any that keep to these rules, and one draw needn't show every extreme that they name: `routing`: in the rows of one device no slot is named more than 32 times, a bound that some block reaches. `plan`: every expert 0 to 5 is held by at least one slot. `gate_weight`: slots holding the same expert have equal gate and up projections. `up_weight`: slots holding the same expert have equal gate and up projections. down_weight[k] is master[plan[k]] rounded to bfloat16.
All inputs are finite; a program needn't handle non-finite values.
Results may differ from a plain program's by a relative error of at most 0.012.
Values may be sent and summed in bfloat16 or wider, within the bound.
No kernel may reach another device: no remote copies, remote signals or barrier semaphores. Data moves between devices by JAX's collectives and lax.ppermute only.
A program may use at most 128 MiB of HBM per device.

v0:
```python
import jax
import jax.numpy as jnp
from jax import lax
from jax.sharding import PartitionSpec as P


def adam_update(folded, master, moment, second):
    new_moment = 0.9 * moment + 0.1 * folded
    new_second = 0.95 * second + 0.05 * folded * folded
    first_hat = new_moment / (1.0 - 0.9**10)
    second_hat = new_second / (1.0 - 0.95**10)
    new_master = master - 0.01 * (first_hat / (jnp.sqrt(second_hat) + 1e-08) + 0.1 * master)
    return (new_master, new_moment, new_second)


def body(
    tokens, out_grad, routing, plan, gate_weight, up_weight, down_weight, master, moment, second
):
    slot_count = lax.axis_size("expert")
    owned = tokens.shape[0]
    width = tokens.shape[1]
    capacity = 2 * owned // slot_count
    route = routing[:, 0]
    onehot = (route[:, None] == jnp.arange(slot_count, dtype=jnp.int32)[None, :]).astype(jnp.int32)
    rank = jnp.sum(jnp.cumsum(onehot, axis=0) * onehot, axis=1) - 1
    position = route * capacity + rank
    send_x = jnp.zeros((slot_count * capacity, width), jnp.bfloat16).at[position].set(tokens)
    send_g = jnp.zeros((slot_count * capacity, width), jnp.bfloat16).at[position].set(out_grad)
    send_x = send_x.reshape(slot_count, capacity, width)
    send_g = send_g.reshape(slot_count, capacity, width)
    got_x, got_g = (
        lax.all_to_all(send_x, "expert", split_axis=0, concat_axis=0, tiled=True),
        lax.all_to_all(send_g, "expert", split_axis=0, concat_axis=0, tiled=True),
    )
    all_x, all_g = (
        lax.all_gather(got_x[None], "slot", axis=0, tiled=True),
        lax.all_gather(got_g[None], "slot", axis=0, tiled=True),
    )
    rows_x = all_x.reshape(-1, width)
    rows_g = all_g.reshape(-1, width)
    quarter = gate_weight.shape[2]
    joined = jnp.concatenate((gate_weight[0], up_weight[0]), axis=1)
    both = jnp.dot(rows_x, joined, preferred_element_type=jnp.float32)
    gate = both[:, :quarter]
    up = both[:, quarter:]
    sig = jax.nn.sigmoid(gate)
    silu_gate = gate * sig
    hidden = (silu_gate * up).astype(jnp.bfloat16)
    d_hidden = lax.dot_general(
        rows_g, down_weight[0], (((1,), (1,)), ((), ())), preferred_element_type=jnp.float32
    )
    d_gate = (d_hidden * up * sig * (1.0 + gate * (1.0 - sig))).astype(jnp.bfloat16)
    d_up = (d_hidden * silu_gate).astype(jnp.bfloat16)
    backward = jnp.concatenate((d_gate, d_up), axis=1)
    grad = lax.dot_general(
        hidden, rows_g, (((0,), (0,)), ((), ())), preferred_element_type=jnp.float32
    )
    summed = lax.psum_scatter(
        lax.dot_general(
            backward, joined, (((1,), (1,)), ((), ())), preferred_element_type=jnp.float32
        ).astype(jnp.bfloat16),
        "slot",
        scatter_dimension=0,
        tiled=True,
    )
    dx_rows = summed.reshape(slot_count, capacity, width)
    returned = lax.all_to_all(dx_rows, "expert", split_axis=0, concat_axis=0, tiled=True).reshape(
        slot_count * capacity, width
    )
    token_grad = jnp.take(returned, position, axis=0)
    pieces = grad.reshape(slot_count, -1, width)
    arrived = lax.all_to_all(
        pieces.astype(jnp.bfloat16), "expert", split_axis=0, concat_axis=0, tiled=True
    ).astype(pieces.dtype)
    primaries = master.shape[0]
    select = (plan[None, :] == jnp.arange(primaries, dtype=jnp.int32)[:, None]).astype(jnp.float32)
    folded = jnp.einsum("ps,sfd->pfd", select, arrived, precision=lax.Precision.HIGHEST)
    new_master, new_moment, new_second = adam_update(folded, master, moment, second)
    outgoing = jnp.take(new_master.astype(jnp.bfloat16), plan, axis=0)
    fresh = lax.all_to_all(outgoing, "expert", split_axis=0, concat_axis=0, tiled=True).reshape(
        1, -1, width
    )
    return (token_grad, new_master, new_moment, new_second, fresh)


def solution(mesh):
    placed = (
        P(("expert", "slot"), None),
        P(("expert", "slot"), None),
        P(("expert", "slot"), None),
        P(),
        P("expert", None, "slot"),
        P("expert", None, "slot"),
        P("expert", "slot", None),
        P(None, ("slot", "expert"), None),
        P(None, ("slot", "expert"), None),
        P(None, ("slot", "expert"), None),
    )
    return jax.shard_map(
        body,
        mesh=mesh,
        in_specs=placed,
        out_specs=(
            P(("expert", "slot"), None),
            P(None, ("slot", "expert"), None),
            P(None, ("slot", "expert"), None),
            P(None, ("slot", "expert"), None),
            P("expert", "slot", None),
        ),
        check_vma=False,
    )
```

profile of v0, /device:TPU:0, one launch (start us, length us, event | category | flops | bytes accessed | tf_op | source)
XLA Modules:
  0.0 222.8 jit_solution(1653720906243507989)
XLA Ops:
  7.2 0.0 all-gather.7.cloned.1.call-start
  7.2 0.8 fusion.15
  8.0 0.2 reduce_window_sum.11
  8.2 0.8 select_reduce_fusion
  9.0 0.7 and_bitcast_fusion
  9.7 2.2 scatter_custom_fusion.1
  11.9 33.0 %all_to_all.25 = bf16[8,32,2048]{2,1,0:T(8,128)(2,1)} all-to-all(bf16[8,32,2048]{2,1,0:T(8,128)(2,1)S(1)} %bitcast.38), channel_id=1, replica_groups=mesh['expert'=8,'slot'=4] {'expert'}, dimensions={0} | all-to-all | bytes 2097152 | tf_op jit(solution)/shard_map/all_to_all | solution.py:32
  44.9 0.0 all-gather.7.cloned.1.call-update
  44.9 0.0 all-gather.5.cloned.1.call-start
  45.0 2.2 scatter_custom_fusion
  47.2 29.1 %all_to_all.26 = bf16[8,32,2048]{2,1,0:T(8,128)(2,1)} all-to-all(bf16[8,32,2048]{2,1,0:T(8,128)(2,1)S(1)} %bitcast.37), channel_id=1, replica_groups=mesh['expert'=8,'slot'=4] {'expert'}, dimensions={0} | all-to-all | bytes 2097152 | tf_op jit(solution)/shard_map/all_to_all | solution.py:33
  76.3 0.0 reduce-scatter.2.cloned.1.call-start
  76.4 2.2 all-gather.7.cloned.1.call-done
  78.6 5.2 %fusion.1 = f32[1024,384]{0,1:T(8,128)} fusion(bf16[1024,2048]{1,0:T(8,128)(2,1)} %bitcast.48, bf16[2048,192]{0,1:T(8,128)(2,1)S(1)} %bitcast.49, bf16[2048,192]{0,1:T(8,128)(2,1)S(1)} %bitcast.51), kind=kOutput, calls=%fused_computation.11 | convolution fusion | flops 1613758464 | bytes 7340032 | tf_op jit(solution)/shard_map/dot_general | solution.py:43
  83.8 30.9 %all-gather.5.cloned.1.call-done = bf16[32,32,2048]{2,1,0:T(8,128)(2,1)} async-done(((bf16[8,32,2048]{2,1,0:T(8,128)(2,1)}), bf16[32,32,2048]{2,1,0:T(8,128)(2,1)}) %all-gather.5.cloned.1.call-update) | async-done | bytes 4194320 | tf_op jit(solution)/shard_map/all_gather | solution.py:37
  114.6 4.4 %multiply_convert_fusion.2 = (bf16[1024,192]{0,1:T(8,128)(2,1)S(1)}, bf16[1024,192]{0,1:T(8,128)(2,1)S(1)}, bf16[1024,192]{0,1:T(8,128)(2,1)S(1)}) fusion(f32[1024,384]{0,1:T(8,128)} %fusion.1, bf16[1024,2048]{1,0:T(8,128)(2,1)} %bitcast.46, bf16[1,192,2048]{2,1,0:T(8,128)(2,1)S(1)} %copy-done), kind=kOutput, calls=%fused_computation.21 | convolution fusion | flops 808255488 | bytes 7733248 | tf_op jit(solution)/shard_map/dot_general | solution.py:49
  119.0 4.4 %convolution_convert_fusion = bf16[1024,2048]{1,0:T(8,128)(2,1)} fusion(bf16[2048,192]{0,1:T(8,128)(2,1)S(1)} %bitcast.50, bf16[2048,192]{0,1:T(8,128)(2,1)S(1)} %bitcast.52, bf16[1024,192]{0,1:T(8,128)(2,1)S(1)} %get-tuple-element.27, bf16[1024,192]{0,1:T(8,128)(2,1)S(1)} %get-tuple-element.26), kind=kOutput, calls=%fused_computation.4 | convolution fusion | flops 1617428480 | bytes 6553600 | tf_op jit(solution)/shard_map/dot_general | solution.py:59
  123.4 3.3 %convolution_convert_fusion.1 = bf16[8,24,2048]{2,0,1:T(8,128)(2,1)S(1)} fusion(bf16[1024,2048,1]{1,0,2:T(8,128)(2,1)} %bitcast.47, bf16[8,24,1024]{2,1,0:T(8,128)(2,1)S(1)} %bitcast.53), kind=kOutput, calls=%fused_computation.5 | convolution fusion | flops 805699584 | bytes 5373952 | tf_op jit(solution)/shard_map/dot_general | solution.py:55
  126.7 1.3 copy.42
  128.0 5.5 %all-to-all-start.3 = ((bf16[8,24,2048]{2,1,0:T(8,128)(2,1)}), bf16[8,24,2048]{2,1,0:T(8,128)(2,1)S(1)}, u32[]{:S(2)}, u32[]{:S(2)}) async-start(bf16[8,24,2048]{2,1,0:T(8,128)(2,1)} %copy.42), calls=%async_computation.4 | async-start | bytes 1572864 | tf_op jit(solution)/shard_map/all_to_all | solution.py:72
  133.6 20.5 %all-to-all-done.3 = bf16[8,24,2048]{2,1,0:T(8,128)(2,1)S(1)} async-done(((bf16[8,24,2048]{2,1,0:T(8,128)(2,1)}), bf16[8,24,2048]{2,1,0:T(8,128)(2,1)S(1)}, u32[]{:S(2)}, u32[]{:S(2)}) %all-to-all-start.3) | async-done | bytes 786464 | tf_op jit(solution)/shard_map/all_to_all | solution.py:72
  154.1 0.6 fusion.7
  154.7 0.6 copy-done.2
  155.4 4.4 %fusion.21 = (bf16[6,24,2048]{2,1,0:T(8,128)(2,1)S(1)}, f32[6,24,2048]{2,1,0:T(8,128)}, f32[6,24,2048]{2,1,0:T(8,128)}, f32[6,24,2048]{2,1,0:T(8,128)}) fusion(f32[6,24,2048]{2,1,0:T(8,128)S(1)} %copy-done.1, f32[6,24,2048]{2,0,1:T(8,128)S(1)} %fusion.7, f32[6,24,2048]{2,1,0:T(8,128)S(1)} %copy-done.2, f32[6,24,2048]{2,1,0:T(8,128)} %param.19), kind=kLoop, calls=%fused_computation.46 | loop fusion | flops 4718592 | bytes 8847360 | tf_op jit(solution)/shard_map/convert_element_type | solution.py:79
  159.8 0.6 gather_fusion.1
  160.4 0.1 broadcast_select_fusion
  160.6 23.7 %all_to_all.27 = bf16[8,24,2048]{2,1,0:T(8,128)(2,1)S(1)} all-to-all(bf16[8,24,2048]{2,1,0:T(8,128)(2,1)S(1)} %broadcast_select_fusion), channel_id=1, replica_groups=mesh['expert'=8,'slot'=4] {'expert'}, dimensions={0} | all-to-all | bytes 1572864 | tf_op jit(solution)/shard_map/all_to_all | solution.py:80
  184.3 3.6 %all-to-all-start.2 = ((bf16[8,32,2048]{2,1,0:T(8,128)(2,1)}), bf16[8,32,2048]{2,1,0:T(8,128)(2,1)S(1)}, u32[]{:S(2)}, u32[]{:S(2)}) async-start(bf16[8,32,2048]{2,1,0:T(8,128)(2,1)} %bitcast.40), calls=%async_computation.3 | async-start | bytes 2097152 | tf_op jit(solution)/shard_map/all_to_all | solution.py:67
  187.9 25.6 %all-to-all-done.2 = bf16[8,32,2048]{2,1,0:T(8,128)(2,1)S(1)} async-done(((bf16[8,32,2048]{2,1,0:T(8,128)(2,1)}), bf16[8,32,2048]{2,1,0:T(8,128)(2,1)S(1)}, u32[]{:S(2)}, u32[]{:S(2)}) %all-to-all-start.2) | async-done | bytes 1048608 | tf_op jit(solution)/shard_map/all_to_all | solution.py:67
  213.5 0.9 gather_fusion
  214.5 0.9 broadcast_select_fusion.1
  215.4 0.9 copy.56
  (18 shorter events, 0.1 us)
Async XLA Ops:
  7.2 107.5 %copy-start = (bf16[1,192,2048]{2,1,0:T(8,128)(2,1)S(1)}, bf16[1,192,2048]{2,1,0:T(8,128)(2,1)}, u32[]{:S(2)}) copy-start(bf16[1,192,2048]{2,1,0:T(8,128)(2,1)} %param.16) | copy-start | bytes 2359300
  7.2 71.4 %all-gather.7.cloned.1.call-start = ((), (), s32[]{:S(2)}) async-start(), calls=%async_computation.8 | async-start | bytes 5242880 | tf_op jit(solution)/shard_map/all_gather | solution.py:36
  44.9 69.7 %all-gather.5.cloned.1.call-start = ((), (), s32[]{:S(2)}) async-start(), calls=%async_computation.7 | async-start | bytes 5242880 | tf_op jit(solution)/shard_map/all_gather | solution.py:37
  47.2 31.4 %copy-start.4 = (bf16[1,2048,192]{1,2,0:T(8,128)(2,1)S(1)}, bf16[1,2048,192]{1,2,0:T(8,128)(2,1)}, u32[]{:S(2)}) copy-start(bf16[1,2048,192]{1,2,0:T(8,128)(2,1)} %param.15) | copy-start | bytes 2359300
  47.2 31.4 %copy-start.5 = (bf16[1,2048,192]{1,2,0:T(8,128)(2,1)S(1)}, bf16[1,2048,192]{1,2,0:T(8,128)(2,1)}, u32[]{:S(2)}) copy-start(bf16[1,2048,192]{1,2,0:T(8,128)(2,1)} %param.14) | copy-start | bytes 2359300
  76.3 108.0 %reduce-scatter.2.cloned.1.call-start = ((), (), s32[]{:S(2)}) async-start(), calls=%async_computation.6 | async-start | bytes 5242880 | tf_op jit(solution)/shard_map/reduce_scatter | solution.py:58
  126.7 6.8 %copy-start.3 = (s32[8]{0:T(128)S(1)}, s32[8]{0:T(128)}, u32[]{:S(2)}) copy-start(s32[8]{0:T(128)} %param.13) | copy-start | bytes 100
  128.0 26.1 %all-to-all-start.3 = ((bf16[8,24,2048]{2,1,0:T(8,128)(2,1)}), bf16[8,24,2048]{2,1,0:T(8,128)(2,1)S(1)}, u32[]{:S(2)}, u32[]{:S(2)}) async-start(bf16[8,24,2048]{2,1,0:T(8,128)(2,1)} %copy.42), calls=%async_computation.4 | async-start | bytes 1572864 | tf_op jit(solution)/shard_map/all_to_all | solution.py:72
  133.5 21.2 %copy-start.1 = (f32[6,24,2048]{2,1,0:T(8,128)S(1)}, f32[6,24,2048]{2,1,0:T(8,128)}, u32[]{:S(2)}) copy-start(f32[6,24,2048]{2,1,0:T(8,128)} %param.17) | copy-start | bytes 3538948
  154.1 1.3 copy-start.2
  184.3 29.2 %all-to-all-start.2 = ((bf16[8,32,2048]{2,1,0:T(8,128)(2,1)}), bf16[8,32,2048]{2,1,0:T(8,128)(2,1)S(1)}, u32[]{:S(2)}, u32[]{:S(2)}) async-start(bf16[8,32,2048]{2,1,0:T(8,128)(2,1)} %bitcast.40), calls=%async_computation.3 | async-start | bytes 2097152 | tf_op jit(solution)/shard_map/all_to_all | solution.py:67
Sparse Core Ops, SparseCore 0:
  45.0 33.4 all-gather.6
  80.1 34.4 all-gather.4
  123.5 44.4 reduce-scatter.1
where the time goes:
time: 223 us
  blocking collectives  85.8 us (38%)
  waiting for transfers between devices  79.2 us (36%)
  matrix products  17.9 us (8%)
  between operations  13.9 us (6%)
  starting transfers between devices  9.28 us (4%)
  local copies, waits for them, and re-layouts  8.82 us (4%)
  other arithmetic  7.98 us (4%)
    all_to_all x1, blocking collectives, body(): lax.all_to_all(send_x, 'expert', split_axis=0, concat_axis=0, tiled=True)  33 us
    all_gather x1, waiting for transfers between devices, body(): lax.all_gather(got_g[None], 'slot', axis=0, tiled=True)  30.9 us
    all_to_all x1, blocking collectives, body(): lax.all_to_all(send_g, 'expert', split_axis=0, concat_axis=0, tiled=True)  29.1 us
    all_to_all x1, waiting for transfers between devices, body(): lax.all_to_all(dx_rows, 'expert', split_axis=0, concat_axis=0, tiled=True)  25.6 us
    all_to_all x1, blocking collectives, body(): lax.all_to_all(outgoing, 'expert', split_axis=0, concat_axis=0, tiled=True)  23.7 us
    all_to_all x1, waiting for transfers between devices, body(): lax.all_to_all(pieces.astype(jnp.bfloat16), 'expert', split_axis=0, conca...  20.5 us
    all_to_all x1, starting transfers between devices, body(): lax.all_to_all(pieces.astype(jnp.bfloat16), 'expert', split_axis=0, conca...  5.52 us
    dot_general x1, matrix products, body(): both = jnp.dot(rows_x, joined, preferred_element_type=jnp.float32)  5.21 us
  transfers between devices with their start and end apart: 5, of which 4 were waited for; matrix products, arithmetic and copies ran while one was open for 8% of the time, Pallas kernels for 0%

commit v1 on v0

v1 whole, which is shorter than its diff:
```python
import functools

import jax
import jax.numpy as jnp
from jax import lax
from jax.experimental import pallas as pl
from jax.experimental.pallas import tpu as pltpu
from jax.sharding import PartitionSpec as P

BF16 = jnp.bfloat16
F32 = jnp.float32
NT = (((1,), (1,)), ((), ()))
TN = (((0,), (0,)), ((), ()))
NN = (((1,), (0,)), ((), ()))
COLUMNS = 512


def dot(a, b, dims):
    return lax.dot_general(a, b, dims, preferred_element_type=F32)


def call(kernel, outs, args, scratch=(), smem=(), name=None, mib=40, flops=0):
    moved = sum(a.size * a.dtype.itemsize for a in args) + sum(
        o.size * o.dtype.itemsize for o in outs
    )
    return pl.pallas_call(
        kernel,
        out_shape=tuple(outs),
        in_specs=[
            pl.BlockSpec(memory_space=pltpu.SMEM if i in smem else pltpu.VMEM)
            for i in range(len(args))
        ],
        out_specs=tuple(pl.BlockSpec(memory_space=pltpu.VMEM) for _ in outs),
        scratch_shapes=list(scratch),
        compiler_params=pltpu.CompilerParams(vmem_limit_bytes=mib * 2**20),
        cost_estimate=pl.CostEstimate(flops=flops, bytes_accessed=moved, transcendentals=0),
        name=name,
    )(*args)


def columns(width):
    step = min(COLUMNS, width)
    return [slice(c, c + step) for c in range(0, width, step)]


def pack_kernel(n, capacity, joint, r_ref, x_ref, g_ref, place_ref, *outs):
    e = lax.axis_index("expert")
    owned, width = x_ref.shape
    rel = r_ref[...] ^ e
    lane = lax.broadcasted_iota(jnp.int32, (owned, n), 1)
    match = (rel == lane).astype(F32)
    lower = lax.broadcasted_iota(jnp.int32, (owned, owned), 0) >= lax.broadcasted_iota(
        jnp.int32, (owned, owned), 1
    )
    count = dot(lower.astype(BF16), match.astype(BF16), NN)
    pos = jnp.sum(match * (count - 1.0 + (lane * capacity).astype(F32)), axis=1, keepdims=True)
    spot = lax.broadcasted_iota(jnp.int32, (owned, n * capacity), 1)
    place = (pos.astype(jnp.int32) == spot).astype(BF16)
    place_ref[...] = place
    for cols in columns(width):
        for half, ref in enumerate((x_ref, g_ref)):
            packed = dot(place, ref[:, cols], TN).astype(BF16)
            if joint:
                for d in range(n):
                    outs[d][half * capacity : (half + 1) * capacity, cols] = packed[
                        d * capacity : (d + 1) * capacity
                    ]
            else:
                outs[half][:, cols] = packed


def turn_kernel(gate_ref, up_ref, out_ref):
    part = gate_ref.shape[2]
    out_ref[:part] = gate_ref[0].T
    out_ref[part:] = up_ref[0].T


def halves(blocks, half):
    parts = []
    for ref in blocks:
        rows = ref.shape[0] // 2
        parts.append(ref[half * rows : (half + 1) * rows])
    return parts[0] if len(parts) == 1 else jnp.concatenate(parts, axis=0)


def hidden_kernel(nb, m, *refs):
    blocks, weights = refs[:nb], refs[nb : nb + m]
    hidden_ref, a_ref, b_ref = refs[nb + m :]
    x = halves(blocks, 0)
    part = weights[0].shape[0] // 2
    for r in range(m):
        gate = dot(weights[r][:part], x, NT)
        up = dot(weights[r][part:], x, NT)
        sig = jax.nn.sigmoid(gate)
        silu = gate * sig
        hidden_ref[r] = (silu * up).astype(BF16)
        a_ref[r] = up * sig * (1.0 + gate * (1.0 - sig))
        b_ref[r] = silu


def grad_kernel(nb, m, *refs):
    blocks, hidden_ref = refs[:nb], refs[nb]
    send_ref, keep_ref = refs[nb + 1 :]
    part = hidden_ref.shape[1]
    g = halves(blocks, 1)
    for r in range(m):
        rows = slice(r // 2 * part, (r // 2 + 1) * part)
        for cols in columns(g.shape[1]):
            value = dot(hidden_ref[r], g[:, cols], NN)
            if r % 2:
                send_ref[rows, cols] = value.astype(BF16)
            else:
                keep_ref[rows, cols] = value


def back_kernel(nb, m, *refs):
    blocks, weights, down = refs[:nb], refs[nb : nb + m], refs[nb + m : nb + 2 * m]
    a_ref, b_ref = refs[nb + 2 * m : nb + 2 * m + 2]
    outs, (total, turned) = refs[nb + 2 * m + 2 : -2], refs[-2:]
    g = halves(blocks, 1)
    part = down[0].shape[0]
    for r in range(m):
        dh = dot(down[r][...], g, NT)
        turned[r, :part] = (dh * a_ref[r]).astype(BF16)
        turned[r, part:] = (dh * b_ref[r]).astype(BF16)
    for cols in columns(g.shape[1]):
        acc = dot(turned[0], weights[0][:, cols], TN)
        for r in range(1, m):
            acc = acc + dot(turned[r], weights[r][:, cols], TN)
        acc = acc.astype(BF16)
        start = 0
        for out in outs:
            out[:, cols] = acc[start : start + out.shape[0]]
            start += out.shape[0]


def add_kernel(keep_ref, got_ref, first_ref, *rest):
    part = first_ref.shape[0]
    first_ref[...] = keep_ref[:part] + got_ref[:part].astype(F32)
    for i, out in enumerate(rest, 1):
        rows = slice(i * part, (i + 1) * part)
        out[...] = (keep_ref[rows] + got_ref[rows].astype(F32)).astype(BF16)


def cut_kernel(count, first_ref, *refs):
    got, outs, sums = refs[:count], refs[count:-1], refs[-1]
    e = lax.axis_index("expert")
    total = first_ref[...]
    for ref in got:
        total = total + ref[...].astype(F32)
    if len(outs) == 1:
        outs[0][...] = total.astype(BF16)
        return
    sums[...] = total
    rows = outs[0].shape[0]
    for d, out in enumerate(outs):
        out[...] = sums[pl.ds(pl.multiple_of((e ^ d) * rows, 8), rows)].astype(BF16)


def adam_kernel(n, pieces_in, *refs):
    plan_ref = refs[0]
    pieces, (master_ref, moment_ref, second_ref) = refs[1 : 1 + pieces_in], refs[
        1 + pieces_in : 4 + pieces_in
    ]
    new_master, new_moment, new_second = refs[4 + pieces_in : 7 + pieces_in]
    outs, folded = refs[7 + pieces_in : -1], refs[-1]
    e = lax.axis_index("expert")
    primaries = master_ref.shape[0]
    folded[...] = jnp.zeros_like(folded)
    for d in range(n):
        p = plan_ref[e ^ d]
        piece = pieces[0][d] if pieces_in == 1 else pieces[d][...]
        folded[p] = folded[p] + piece.astype(F32)
    for p in range(primaries):
        total = folded[p]
        moment = 0.9 * moment_ref[p] + 0.1 * total
        second = 0.95 * second_ref[p] + 0.05 * total * total
        new_moment[p] = moment
        new_second[p] = second
        master = master_ref[p]
        first_hat = moment / (1.0 - 0.9**10)
        second_hat = second / (1.0 - 0.95**10)
        new_master[p] = master - 0.01 * (
            first_hat / (jnp.sqrt(second_hat) + 1e-08) + 0.1 * master
        )
    for d in range(n):
        row = new_master[plan_ref[e ^ d]].astype(BF16)
        if len(outs) == 1:
            outs[0][d] = row
        else:
            outs[d][...] = row


def unpack_kernel(place_ref, *refs):
    blocks, out_ref = refs[:-1], refs[-1]
    place = place_ref[...]
    for cols in columns(out_ref.shape[1]):
        parts = [b[:, cols] for b in blocks]
        rows = parts[0] if len(parts) == 1 else jnp.concatenate(parts, axis=0)
        out_ref[:, cols] = dot(place, rows, NN).astype(BF16)


def swap(x, axis, mask):
    size = lax.axis_size(axis)
    return lax.ppermute(x, axis, [(i, i ^ mask) for i in range(size)])


def order(n):
    return sorted(range(1, n), key=lambda d: -(d >> 1))


def exchange(blocks):
    n = len(blocks)
    got = {0: blocks[0]}
    for d in order(n):
        got[d] = swap(blocks[d], "expert", d)
    return [got[d] for d in range(n)]


def exchange_whole(x):
    n = x.shape[0]
    turn = jnp.arange(n, dtype=jnp.int32) ^ lax.axis_index("expert")
    x = jnp.take(x, turn, axis=0)
    x = lax.all_to_all(x, "expert", split_axis=0, concat_axis=0, tiled=True)
    return jnp.take(x, turn, axis=0)


def gather_slot(x):
    m = lax.axis_size("slot")
    have = {0: x}
    mask = m // 2
    while mask:
        for r in sorted(have):
            have[r | mask] = swap(have[r], "slot", mask)
        mask //= 2
    return [have[r] for r in range(m)]


def body(
    tokens, out_grad, routing, plan, gate_weight, up_weight, down_weight, master, moment, second
):
    n, m = lax.axis_size("expert"), lax.axis_size("slot")
    owned, width = tokens.shape
    capacity = 2 * owned // n
    part = down_weight.shape[1]
    rows = n * capacity
    few = capacity % 16 == 0
    turn = jnp.arange(n, dtype=jnp.int32) ^ lax.axis_index("expert")
    shape = jax.ShapeDtypeStruct

    outs = [shape((owned, rows), BF16)]
    outs += [shape((2 * capacity, width), BF16)] * n if few else [shape((rows, width), BF16)] * 2
    place, *packed = call(
        functools.partial(pack_kernel, n, capacity, few),
        outs,
        (routing, tokens, out_grad),
        name="pack_rows",
        flops=4 * owned * rows * width,
    )
    (joined,) = call(
        turn_kernel, [shape((2 * part, width), BF16)], (gate_weight, up_weight), name="turn_weights"
    )
    if few:
        blocks = exchange(packed)
    else:
        x, g = (
            exchange_whole(p.reshape(n, capacity, width)).reshape(rows, width) for p in packed
        )
        blocks = [jnp.concatenate((x, g), axis=0)]
    nb = len(blocks)
    joined = gather_slot(joined)
    down = gather_slot(down_weight[0])

    hidden, a, b = call(
        functools.partial(hidden_kernel, nb, m),
        [shape((m, part, rows), BF16), shape((m, part, rows), F32), shape((m, part, rows), F32)],
        (*blocks, *joined),
        name="hidden_units",
        flops=4 * rows * width * part * m,
    )
    send, keep = call(
        functools.partial(grad_kernel, nb, m),
        [shape((m // 2 * part, width), BF16), shape((m // 2 * part, width), F32)],
        (*blocks, hidden),
        name="down_gradient",
        flops=2 * rows * width * part * m,
    )
    dx = call(
        functools.partial(back_kernel, nb, m),
        [shape((r.shape[0] // 2, width), BF16) for r in blocks],
        (*blocks, *joined, *down, a, b),
        scratch=[pltpu.VMEM((8, 128), F32), pltpu.VMEM((m, 2 * part, rows), BF16)],
        name="input_gradient",
        flops=6 * rows * width * part * m,
    )
    got = swap(send, "slot", 1)
    first, *rest = call(
        add_kernel,
        [shape((part, width), F32)] + [shape((part, width), BF16)] * (m // 2 - 1),
        (keep, got),
        name="add_pair",
    )
    if few:
        returned = exchange(dx)
    else:
        returned = [exchange_whole(dx[0].reshape(n, capacity, width)).reshape(rows, width)]
    rest = [swap(r, "slot", 2 * i) for i, r in enumerate(rest, 1)]
    owner = part // n
    pieces = call(
        functools.partial(cut_kernel, len(rest)),
        [shape((owner, width), BF16)] * n if few else [shape((part, width), BF16)],
        (first, *rest),
        scratch=[pltpu.VMEM((part, width), F32)],
        name="cut_gradient",
    )
    if few:
        arrived = exchange(pieces)
    else:
        arrived = [exchange_whole(jnp.take(pieces[0].reshape(n, owner, width), turn, axis=0))]
    new_master, new_moment, new_second, *outgoing = call(
        functools.partial(adam_kernel, n, len(arrived)),
        [shape(master.shape, F32)] * 3
        + ([shape((owner, width), BF16)] * n if few else [shape((n, owner, width), BF16)]),
        (plan, *arrived, master, moment, second),
        scratch=[pltpu.VMEM(master.shape, F32)],
        smem=(0,),
        name="adam",
    )
    (token_grad,) = call(
        unpack_kernel,
        [shape((owned, width), BF16)],
        (place, *returned),
        name="unpack_rows",
        flops=2 * owned * rows * width,
    )
    if few:
        fresh = jnp.take(jnp.stack(exchange(outgoing)), turn, axis=0)
    else:
        fresh = exchange_whole(outgoing[0])
    return (token_grad, new_master, new_moment, new_second, fresh.reshape(1, part, width))


def solution(mesh):
    rows, state = P(("expert", "slot"), None), P(None, ("slot", "expert"), None)
    split, held = P("expert", None, "slot"), P("expert", "slot", None)
    return jax.shard_map(
        body,
        mesh=mesh,
        in_specs=(rows, rows, rows, P(), split, split, held, state, state, state),
        out_specs=(rows, state, state, state, held),
        check_vma=False,
    )
```

time: 223 us -> 213 us (0.955)
  blocking collectives: 85.8 us -> 0 us
  starting transfers between devices: 9.28 us -> 74.1 us
  waiting for transfers between devices: 79.2 us -> 104 us
  Pallas kernels: 0 us -> 21.4 us
  matrix products: 17.9 us -> 0 us
  between operations: 13.9 us -> 0.87 us
  other arithmetic: 7.98 us -> 1.04 us
    ppermute x0 -> x36, waiting for transfers between devices: none -> 104 us  [swap(): return lax.ppermute(x, axis, [(i, i ^ mask) for i in range(size)])]
    all_to_all x3 -> x0, blocking collectives: 85.8 us -> none  [the longest x1 33 us: body(): lax.all_to_all(send_x, 'expert', split_axis=0, concat_axis=0, tiled=True)]
    ppermute x0 -> x36, starting transfers between devices: none -> 74.1 us  [swap(): return lax.ppermute(x, axis, [(i, i ^ mask) for i in range(size)])]
    all_to_all x2 -> x0, waiting for transfers between devices: 46.1 us -> none  [the longest x1 25.6 us: body(): lax.all_to_all(dx_rows, 'expert', split_axis=0, concat_axis=0, tiled=True)]
    all_gather x2 -> x0, waiting for transfers between devices: 33 us -> none  [the longest x1 30.9 us: body(): lax.all_gather(got_g[None], 'slot', axis=0, tiled=True)]
    pallas_call x0 -> x9, Pallas kernels: none -> 21.4 us  [call(): pl.pallas_call(kernel, out_shape=tuple(outs), in_specs=[pl.BlockSpec(memo...]
    dot_general x5 -> x0, matrix products: 17.9 us -> none  [the longest x1 5.21 us: body(): both = jnp.dot(rows_x, joined, preferred_element_type=jnp.float32)]
    all_to_all x2 -> x0, starting transfers between devices: 9.15 us -> none  [the longest x1 5.52 us: body(): lax.all_to_all(pieces.astype(jnp.bfloat16), 'expert', split_axis=0, conca...]
  transfers between devices with their start and end apart: 5 -> 36, of which waited for: 4 -> 10; matrix products, arithmetic and copies ran while one was open for 8% -> 0% of each run, Pallas kernels for 0% -> 5%
where the time goes in v1:
time: 213 us
  waiting for transfers between devices  104 us (49%)
  starting transfers between devices  74.1 us (35%)
  Pallas kernels  21.4 us (10%)
  local copies, waits for them, and re-layouts  11 us (5%)
    ppermute x36, waiting for transfers between devices, swap(): return lax.ppermute(x, axis, [(i, i ^ mask) for i in range(size)])  104 us
    ppermute x36, starting transfers between devices, swap(): return lax.ppermute(x, axis, [(i, i ^ mask) for i in range(size)])  74.1 us
    pallas_call x9, Pallas kernels, call(): pl.pallas_call(kernel, out_shape=tuple(outs), in_specs=[pl.BlockSpec(memo...  21.4 us
    unnamed x38, local copies, waits for them, and re-layouts  10.2 us
  transfers between devices with their start and end apart: 36, of which 10 were waited for; matrix products, arithmetic and copies ran while one was open for 0% of the time, Pallas kernels for 5%

profile of v1, /device:TPU:0, one launch (start us, length us, event | category | flops | bytes accessed | tf_op | source)
XLA Modules:
  0.0 212.5 jit_solution(8369222499590744508)
XLA Ops:
  5.3 3.0 %collective-permute-start.8 = (bf16[384,2048]{1,0:T(8,128)(2,1)S(1)}, bf16[384,2048]{1,0:T(8,128)(2,1)S(1)}, u32[]{:S(2)}, u32[]{:S(2)}) collective-permute-start(bf16[384,2048]{1,0:T(8,128)(2,1)S(1)} %turn_weights.1.refs_8_), channel_id=1, source_target_pairs={{0,2},{1,3},{2,0},{3,1},{4,6},{5,7},{6,4},{7,5},{8,10},{9,11},{10,... | collective-permute-start | bytes 4718600 | tf_op jit(solution)/shard_map/ppermute | solution.py:205
  8.3 34.4 %collective-permute-done.8.refs_10_ = bf16[384,2048]{1,0:T(8,128)(2,1)S(1)} collective-permute-done((bf16[384,2048]{1,0:T(8,128)(2,1)S(1)}, bf16[384,2048]{1,0:T(8,128)(2,1)S(1)}, u32[]{:S(2)}, u32[]{:S(2)}) %collective-permute-start.8) | collective-permute-done | bytes 1572896 | tf_op jit(solution)/shard_map/ppermute | solution.py:205
  45.9 1.8 collective-permute-start
  47.7 1.6 collective-permute-start.1
  49.5 5.3 %collective-permute-done.refs_1_ = bf16[64,2048]{1,0:T(8,128)(2,1)S(1)} collective-permute-done((bf16[64,2048]{1,0:T(8,128)(2,1)S(1)}, bf16[64,2048]{1,0:T(8,128)(2,1)S(1)}, u32[]{:S(2)}, u32[]{:S(2)}) %collective-permute-start) | collective-permute-done | bytes 262176 | tf_op jit(solution)/shard_map/ppermute | solution.py:205
  54.7 2.8 %collective-permute-start.3 = (bf16[64,2048]{1,0:T(8,128)(2,1)S(1)}, bf16[64,2048]{1,0:T(8,128)(2,1)S(1)}, u32[]{:S(2)}, u32[]{:S(2)}) collective-permute-start(bf16[64,2048]{1,0:T(8,128)(2,1)S(1)} %get-tuple-element.53), channel_id=1, source_target_pairs={{0,16},{4,20},{8,24},{12,28},{16,0},{20,4},{24,8},{28,12},{1,17},{... | collective-permute-start | bytes 786440 | tf_op jit(solution)/shard_map/ppermute | solution.py:205
  57.5 1.9 collective-permute-start.4
  59.4 6.9 %collective-permute-done.2.refs_3_ = bf16[64,2048]{1,0:T(8,128)(2,1)S(1)} collective-permute-done((bf16[64,2048]{1,0:T(8,128)(2,1)S(1)}, bf16[64,2048]{1,0:T(8,128)(2,1)S(1)}, u32[]{:S(2)}, u32[]{:S(2)}) %collective-permute-start.2) | collective-permute-done | bytes 262176 | tf_op jit(solution)/shard_map/ppermute | solution.py:205
  67.8 13.9 %collective-permute-done.3.refs_4_ = bf16[64,2048]{1,0:T(8,128)(2,1)S(1)} collective-permute-done((bf16[64,2048]{1,0:T(8,128)(2,1)S(1)}, bf16[64,2048]{1,0:T(8,128)(2,1)S(1)}, u32[]{:S(2)}, u32[]{:S(2)}) %collective-permute-start.3) | collective-permute-done | bytes 262176 | tf_op jit(solution)/shard_map/ppermute | solution.py:205
  81.7 4.8 %collective-permute-start.6 = (bf16[64,2048]{1,0:T(8,128)(2,1)S(1)}, bf16[64,2048]{1,0:T(8,128)(2,1)S(1)}, u32[]{:S(2)}, u32[]{:S(2)}) collective-permute-start(bf16[64,2048]{1,0:T(8,128)(2,1)S(1)} %get-tuple-element.56), channel_id=1, source_target_pairs={{0,28},{4,24},{8,20},{12,16},{16,12},{20,8},{24,4},{28,0},{1,29},{... | collective-permute-start | bytes 786440 | tf_op jit(solution)/shard_map/ppermute | solution.py:205
  86.5 7.6 %collective-permute-done.4.refs_5_ = bf16[64,2048]{1,0:T(8,128)(2,1)S(1)} collective-permute-done((bf16[64,2048]{1,0:T(8,128)(2,1)S(1)}, bf16[64,2048]{1,0:T(8,128)(2,1)S(1)}, u32[]{:S(2)}, u32[]{:S(2)}) %collective-permute-start.4) | collective-permute-done | bytes 262176 | tf_op jit(solution)/shard_map/ppermute | solution.py:205
  94.1 4.8 %hidden_units.1 = (bf16[4,192,256]{2,1,0:T(8,128)(2,1)S(1)}, f32[4,192,256]{2,1,0:T(8,128)S(1)}, f32[4,192,256]{2,1,0:T(8,128)S(1)}) custom-call(bf16[64,2048]{1,0:T(8,128)(2,1)S(1)} %get-tuple-element.49.refs_0_, bf16[64,2048]{1,0:T(8,128)(2,1)S(1)} %collective-permute-done.refs_1_, bf16[64,2048]{1,0:T(8,128)(2,1)S(1)} %collective-permute-done.1.refs_2_, ...), custom_call_target="tpu_custom_call" | custom-call | flops 1610612736 | bytes 10354688 | tf_op jit(solution)/shard_map/hidden_units/pallas_call | solution.py:26
  101.7 18.2 %collective-permute-done.11.refs_14_ = bf16[192,2048]{1,0:T(8,128)(2,1)S(1)} collective-permute-done((bf16[192,2048]{1,0:T(8,128)(2,1)S(1)}, bf16[192,2048]{1,0:T(8,128)(2,1)S(1)}, u32[]{:S(2)}, u32[]{:S(2)}) %collective-permute-start.11) | collective-permute-done | bytes 786464 | tf_op jit(solution)/shard_map/ppermute | solution.py:205
  123.8 6.3 %input_gradient.1 = (bf16[32,2048]{1,0:T(8,128)(2,1)S(1)}, bf16[32,2048]{1,0:T(8,128)(2,1)}, bf16[32,2048]{1,0:T(8,128)(2,1)}, bf16[32,2048]{1,0:T(8,128)(2,1)},...) custom-call(bf16[64,2048]{1,0:T(8,128)(2,1)S(1)} %get-tuple-element., ...), custom_call_target="tpu_custom_call" | custom-call | flops 2415919104 | bytes 14155776 | tf_op jit(solution)/shard_map/input_gradient/pallas_call | solution.py:26
  131.9 10.8 %collective-permute-start.14 = (bf16[32,2048]{1,0:T(8,128)(2,1)}, bf16[32,2048]{1,0:T(8,128)(2,1)S(1)}, u32[]{:S(2)}, u32[]{:S(2)}) collective-permute-start(bf16[32,2048]{1,0:T(8,128)(2,1)} %get-tuple-element.61), channel_id=1, source_target_pairs={{0,8},{4,12},{8,0},{12,4},{16,24},{20,28},{24,16},{28,20},{1,9},{5... | collective-permute-start | bytes 393224 | tf_op jit(solution)/shard_map/ppermute | solution.py:205
  143.4 4.2 %collective-permute-start.16 = (bf16[32,2048]{1,0:T(8,128)(2,1)}, bf16[32,2048]{1,0:T(8,128)(2,1)S(1)}, u32[]{:S(2)}, u32[]{:S(2)}) collective-permute-start(bf16[32,2048]{1,0:T(8,128)(2,1)} %get-tuple-element.63), channel_id=1, source_target_pairs={{0,16},{4,20},{8,24},{12,28},{16,0},{20,4},{24,8},{28,12},{1,17},{... | collective-permute-start | bytes 393224 | tf_op jit(solution)/shard_map/ppermute | solution.py:205
  147.6 2.3 %collective-permute-start.17 = (bf16[32,2048]{1,0:T(8,128)(2,1)}, bf16[32,2048]{1,0:T(8,128)(2,1)S(1)}, u32[]{:S(2)}, u32[]{:S(2)}) collective-permute-start(bf16[32,2048]{1,0:T(8,128)(2,1)} %copy-done.11), channel_id=1, source_target_pairs={{0,20},{4,16},{8,28},{12,24},{16,4},{20,0},{24,12},{28,8},{1,21},{... | collective-permute-start | bytes 393224 | tf_op jit(solution)/shard_map/ppermute | solution.py:205
  150.4 4.4 %collective-permute-start.19 = (bf16[32,2048]{1,0:T(8,128)(2,1)S(1)}, bf16[32,2048]{1,0:T(8,128)(2,1)S(1)}, u32[]{:S(2)}, u32[]{:S(2)}) collective-permute-start(bf16[32,2048]{1,0:T(8,128)(2,1)S(1)} %get-tuple-element.66), channel_id=1, source_target_pairs={{0,28},{4,24},{8,20},{12,16},{16,12},{20,8},{24,4},{28,0},{1,29},{... | collective-permute-start | bytes 393224 | tf_op jit(solution)/shard_map/ppermute | solution.py:205
  156.4 1.5 cut_gradient.1
  158.6 4.5 %collective-permute-start.23 = (bf16[24,2048]{1,0:T(8,128)(2,1)S(1)}, bf16[24,2048]{1,0:T(8,128)(2,1)S(1)}, u32[]{:S(2)}, u32[]{:S(2)}) collective-permute-start(bf16[24,2048]{1,0:T(8,128)(2,1)S(1)} %get-tuple-element.74), channel_id=1, source_target_pairs={{0,8},{4,12},{8,0},{12,4},{16,24},{20,28},{24,16},{28,20},{1,9},{5... | collective-permute-start | bytes 294920 | tf_op jit(solution)/shard_map/ppermute | solution.py:205
  163.1 3.8 %collective-permute-done.17.refs_5_ = bf16[32,2048]{1,0:T(8,128)(2,1)S(1)} collective-permute-done((bf16[32,2048]{1,0:T(8,128)(2,1)}, bf16[32,2048]{1,0:T(8,128)(2,1)S(1)}, u32[]{:S(2)}, u32[]{:S(2)}) %collective-permute-start.17) | collective-permute-done | bytes 131104 | tf_op jit(solution)/shard_map/ppermute | solution.py:205
  166.9 3.6 %collective-permute-start.25 = (bf16[24,2048]{1,0:T(8,128)(2,1)S(1)}, bf16[24,2048]{1,0:T(8,128)(2,1)S(1)}, u32[]{:S(2)}, u32[]{:S(2)}) collective-permute-start(bf16[24,2048]{1,0:T(8,128)(2,1)S(1)} %get-tuple-element.76), channel_id=1, source_target_pairs={{0,16},{4,20},{8,24},{12,28},{16,0},{20,4},{24,8},{28,12},{1,17},{... | collective-permute-start | bytes 294920 | tf_op jit(solution)/shard_map/ppermute | solution.py:205
  170.5 4.8 %collective-permute-start.26 = (bf16[24,2048]{1,0:T(8,128)(2,1)S(1)}, bf16[24,2048]{1,0:T(8,128)(2,1)S(1)}, u32[]{:S(2)}, u32[]{:S(2)}) collective-permute-start(bf16[24,2048]{1,0:T(8,128)(2,1)S(1)} %get-tuple-element.77), channel_id=1, source_target_pairs={{0,20},{4,16},{8,28},{12,24},{16,4},{20,0},{24,12},{28,8},{1,21},{... | collective-permute-start | bytes 294920 | tf_op jit(solution)/shard_map/ppermute | solution.py:205
  176.4 2.7 %collective-permute-start.28 = (bf16[24,2048]{1,0:T(8,128)(2,1)S(1)}, bf16[24,2048]{1,0:T(8,128)(2,1)S(1)}, u32[]{:S(2)}, u32[]{:S(2)}) collective-permute-start(bf16[24,2048]{1,0:T(8,128)(2,1)S(1)} %get-tuple-element.79), channel_id=1, source_target_pairs={{0,28},{4,24},{8,20},{12,16},{16,12},{20,8},{24,4},{28,0},{1,29},{... | collective-permute-start | bytes 294920 | tf_op jit(solution)/shard_map/ppermute | solution.py:205
  180.2 4.9 %collective-permute-done.26.refs_6_ = bf16[24,2048]{1,0:T(8,128)(2,1)S(1)} collective-permute-done((bf16[24,2048]{1,0:T(8,128)(2,1)S(1)}, bf16[24,2048]{1,0:T(8,128)(2,1)S(1)}, u32[]{:S(2)}, u32[]{:S(2)}) %collective-permute-start.26) | collective-permute-done | bytes 98336 | tf_op jit(solution)/shard_map/ppermute | solution.py:205
  185.2 3.9 %adam.1 = (f32[6,24,2048]{2,1,0:T(8,128)}, f32[6,24,2048]{2,1,0:T(8,128)}, f32[6,24,2048]{2,1,0:T(8,128)}, bf16[24,2048]{1,0:T(8,128)(2,1)S(1)}, bf16[24,2048]{1...) custom-call(s32[8]{0:T(128)S(1)} %copy-done.9, ...), custom_call_target="tpu_custom_call" | custom-call | bytes 8650784 | tf_op jit(solution)/shard_map/adam/pallas_call | solution.py:26
  189.6 3.8 %collective-permute-start.30 = (bf16[24,2048]{1,0:T(8,128)(2,1)S(1)}, bf16[24,2048]{1,0:T(8,128)(2,1)S(1)}, u32[]{:S(2)}, u32[]{:S(2)}) collective-permute-start(bf16[24,2048]{1,0:T(8,128)(2,1)S(1)} %get-tuple-element.85), channel_id=1, source_target_pairs={{0,8},{4,12},{8,0},{12,4},{16,24},{20,28},{24,16},{28,20},{1,9},{5... | collective-permute-start | bytes 294920 | tf_op jit(solution)/shard_map/ppermute | solution.py:205
  193.9 2.4 %collective-permute-start.32 = (bf16[24,2048]{1,0:T(8,128)(2,1)S(1)}, bf16[24,2048]{1,0:T(8,128)(2,1)S(1)}, u32[]{:S(2)}, u32[]{:S(2)}) collective-permute-start(bf16[24,2048]{1,0:T(8,128)(2,1)S(1)} %get-tuple-element.87), channel_id=1, source_target_pairs={{0,16},{4,20},{8,24},{12,28},{16,0},{20,4},{24,8},{28,12},{1,17},{... | collective-permute-start | bytes 294920 | tf_op jit(solution)/shard_map/ppermute | solution.py:205
  197.3 2.4 %collective-permute-start.34 = (bf16[24,2048]{1,0:T(8,128)(2,1)S(1)}, bf16[24,2048]{1,0:T(8,128)(2,1)S(1)}, u32[]{:S(2)}, u32[]{:S(2)}) collective-permute-start(bf16[24,2048]{1,0:T(8,128)(2,1)S(1)} %get-tuple-element.89), channel_id=1, source_target_pairs={{0,24},{4,28},{8,16},{12,20},{16,8},{20,12},{24,0},{28,4},{1,25},{... | collective-permute-start | bytes 294920 | tf_op jit(solution)/shard_map/ppermute | solution.py:205
  199.7 1.9 collective-permute-start.35
  201.7 6.0 %collective-permute-done.32 = bf16[24,2048]{1,0:T(8,128)(2,1)S(1)} collective-permute-done((bf16[24,2048]{1,0:T(8,128)(2,1)S(1)}, bf16[24,2048]{1,0:T(8,128)(2,1)S(1)}, u32[]{:S(2)}, u32[]{:S(2)}) %collective-permute-start.32) | collective-permute-done | bytes 98336 | tf_op jit(solution)/shard_map/ppermute | solution.py:205
  207.7 3.1 %collective-permute-done.33 = bf16[24,2048]{1,0:T(8,128)(2,1)S(1)} collective-permute-done((bf16[24,2048]{1,0:T(8,128)(2,1)S(1)}, bf16[24,2048]{1,0:T(8,128)(2,1)S(1)}, u32[]{:S(2)}, u32[]{:S(2)}) %collective-permute-start.33) | collective-permute-done | bytes 98336 | tf_op jit(solution)/shard_map/ppermute | solution.py:205
  (95 shorter events, 27.3 us)
Async XLA Ops:
  5.3 37.4 %collective-permute-start.8 = (bf16[384,2048]{1,0:T(8,128)(2,1)S(1)}, bf16[384,2048]{1,0:T(8,128)(2,1)S(1)}, u32[]{:S(2)}, u32[]{:S(2)}) collective-permute-start(bf16[384,2048]{1,0:T(8,128)(2,1)S(1)} %turn_weights.1.refs_8_), channel_id=1, source_target_pairs={{0,2},{1,3},{2,0},{3,1},{4,6},{5,7},{6,4},{7,5},{8,10},{9,11},{10,... | collective-permute-start | bytes 4718600 | tf_op jit(solution)/shard_map/ppermute | solution.py:205
  8.3 85.8 %collective-permute-start.7 = (bf16[384,2048]{1,0:T(8,128)(2,1)S(1)}, bf16[384,2048]{1,0:T(8,128)(2,1)}, u32[]{:S(2)}, u32[]{:S(2)}) collective-permute-start(bf16[384,2048]{1,0:T(8,128)(2,1)S(1)} %turn_weights.1.refs_8_), channel_id=1, source_target_pairs={{0,1},{1,0},{2,3},{3,2},{4,5},{5,4},{6,7},{7,6},{8,9},{9,8},{10,11... | collective-permute-start | bytes 4718600 | tf_op jit(solution)/shard_map/ppermute | solution.py:205
  42.7 51.4 %collective-permute-start.9 = (bf16[384,2048]{1,0:T(8,128)(2,1)S(1)}, bf16[384,2048]{1,0:T(8,128)(2,1)}, u32[]{:S(2)}, u32[]{:S(2)}) collective-permute-start(bf16[384,2048]{1,0:T(8,128)(2,1)S(1)} %collective-permute-done.8.refs_10_), channel_id=1, source_target_pairs={{0,1},{1,0},{2,3},{3,2},{4,5},{5,4},{6,7},{7,6},{8,9},{9,8},{10,11... | collective-permute-start | bytes 4718600 | tf_op jit(solution)/shard_map/ppermute | solution.py:205
  45.9 8.8 %collective-permute-start = (bf16[64,2048]{1,0:T(8,128)(2,1)S(1)}, bf16[64,2048]{1,0:T(8,128)(2,1)S(1)}, u32[]{:S(2)}, u32[]{:S(2)}) collective-permute-start(bf16[64,2048]{1,0:T(8,128)(2,1)S(1)} %get-tuple-element.50), channel_id=1, source_target_pairs={{0,4},{4,0},{8,12},{12,8},{16,20},{20,16},{24,28},{28,24},{1,5},{5... | collective-permute-start | bytes 786440 | tf_op jit(solution)/shard_map/ppermute | solution.py:205
  47.7 9.8 %collective-permute-start.1 = (bf16[64,2048]{1,0:T(8,128)(2,1)S(1)}, bf16[64,2048]{1,0:T(8,128)(2,1)S(1)}, u32[]{:S(2)}, u32[]{:S(2)}) collective-permute-start(bf16[64,2048]{1,0:T(8,128)(2,1)S(1)} %get-tuple-element.51), channel_id=1, source_target_pairs={{0,8},{4,12},{8,0},{12,4},{16,24},{20,28},{24,16},{28,20},{1,9},{5... | collective-permute-start | bytes 786440 | tf_op jit(solution)/shard_map/ppermute | solution.py:205
  49.3 17.0 %collective-permute-start.2 = (bf16[64,2048]{1,0:T(8,128)(2,1)S(1)}, bf16[64,2048]{1,0:T(8,128)(2,1)S(1)}, u32[]{:S(2)}, u32[]{:S(2)}) collective-permute-start(bf16[64,2048]{1,0:T(8,128)(2,1)S(1)} %get-tuple-element.52), channel_id=1, source_target_pairs={{0,12},{4,8},{8,4},{12,0},{16,28},{20,24},{24,20},{28,16},{1,13},{... | collective-permute-start | bytes 786440 | tf_op jit(solution)/shard_map/ppermute | solution.py:205
  54.7 26.9 %collective-permute-start.3 = (bf16[64,2048]{1,0:T(8,128)(2,1)S(1)}, bf16[64,2048]{1,0:T(8,128)(2,1)S(1)}, u32[]{:S(2)}, u32[]{:S(2)}) collective-permute-start(bf16[64,2048]{1,0:T(8,128)(2,1)S(1)} %get-tuple-element.53), channel_id=1, source_target_pairs={{0,16},{4,20},{8,24},{12,28},{16,0},{20,4},{24,8},{28,12},{1,17},{... | collective-permute-start | bytes 786440 | tf_op jit(solution)/shard_map/ppermute | solution.py:205
  57.5 36.6 %collective-permute-start.4 = (bf16[64,2048]{1,0:T(8,128)(2,1)S(1)}, bf16[64,2048]{1,0:T(8,128)(2,1)S(1)}, u32[]{:S(2)}, u32[]{:S(2)}) collective-permute-start(bf16[64,2048]{1,0:T(8,128)(2,1)S(1)} %get-tuple-element.54), channel_id=1, source_target_pairs={{0,20},{4,16},{8,28},{12,24},{16,4},{20,0},{24,12},{28,8},{1,21},{... | collective-permute-start | bytes 786440 | tf_op jit(solution)/shard_map/ppermute | solution.py:205
  66.3 27.8 %collective-permute-start.5 = (bf16[64,2048]{1,0:T(8,128)(2,1)S(1)}, bf16[64,2048]{1,0:T(8,128)(2,1)S(1)}, u32[]{:S(2)}, u32[]{:S(2)}) collective-permute-start(bf16[64,2048]{1,0:T(8,128)(2,1)S(1)} %get-tuple-element.55), channel_id=1, source_target_pairs={{0,24},{4,28},{8,16},{12,20},{16,8},{20,12},{24,0},{28,4},{1,25},{... | collective-permute-start | bytes 786440 | tf_op jit(solution)/shard_map/ppermute | solution.py:205
  81.7 12.4 %collective-permute-start.6 = (bf16[64,2048]{1,0:T(8,128)(2,1)S(1)}, bf16[64,2048]{1,0:T(8,128)(2,1)S(1)}, u32[]{:S(2)}, u32[]{:S(2)}) collective-permute-start(bf16[64,2048]{1,0:T(8,128)(2,1)S(1)} %get-tuple-element.56), channel_id=1, source_target_pairs={{0,28},{4,24},{8,20},{12,16},{16,12},{20,8},{24,4},{28,0},{1,29},{... | collective-permute-start | bytes 786440 | tf_op jit(solution)/shard_map/ppermute | solution.py:205
  99.9 20.0 %collective-permute-start.20 = (bf16[384,2048]{1,0:T(8,128)(2,1)S(1)}, bf16[384,2048]{1,0:T(8,128)(2,1)S(1)}, u32[]{:S(2)}, u32[]{:S(2)}) collective-permute-start(bf16[384,2048]{1,0:T(8,128)(2,1)S(1)} %get-tuple-element.69), channel_id=1, source_target_pairs={{0,1},{1,0},{2,3},{3,2},{4,5},{5,4},{6,7},{7,6},{8,9},{9,8},{10,11... | collective-permute-start | bytes 4718600 | tf_op jit(solution)/shard_map/ppermute | solution.py:205
  100.0 19.9 %collective-permute-start.11 = (bf16[192,2048]{1,0:T(8,128)(2,1)S(1)}, bf16[192,2048]{1,0:T(8,128)(2,1)S(1)}, u32[]{:S(2)}, u32[]{:S(2)}) collective-permute-start(bf16[192,2048]{1,0:T(8,128)(2,1)S(1)} %bitcast.22), channel_id=1, source_target_pairs={{0,2},{1,3},{2,0},{3,1},{4,6},{5,7},{6,4},{7,5},{8,10},{9,11},{10,... | collective-permute-start | bytes 2359304 | tf_op jit(solution)/shard_map/ppermute | solution.py:205
  101.6 22.2 %collective-permute-start.10 = (bf16[192,2048]{1,0:T(8,128)(2,1)S(1)}, bf16[192,2048]{1,0:T(8,128)(2,1)S(1)}, u32[]{:S(2)}, u32[]{:S(2)}) collective-permute-start(bf16[192,2048]{1,0:T(8,128)(2,1)S(1)} %bitcast.23), channel_id=1, source_target_pairs={{0,1},{1,0},{2,3},{3,2},{4,5},{5,4},{6,7},{7,6},{8,9},{9,8},{10,11... | collective-permute-start | bytes 2359304 | tf_op jit(solution)/shard_map/ppermute | solution.py:205
  122.3 28.1 %collective-permute-start.21 = (bf16[192,2048]{1,0:T(8,128)(2,1)}, bf16[192,2048]{1,0:T(8,128)(2,1)}, u32[]{:S(2)}, u32[]{:S(2)}) collective-permute-start(bf16[192,2048]{1,0:T(8,128)(2,1)} %get-tuple-element.71), channel_id=1, source_target_pairs={{0,2},{1,3},{2,0},{3,1},{4,6},{5,7},{6,4},{7,5},{8,10},{9,11},{10,... | collective-permute-start | bytes 2359304 | tf_op jit(solution)/shard_map/ppermute | solution.py:205
  131.4 16.2 %collective-permute-start.13 = (bf16[32,2048]{1,0:T(8,128)(2,1)}, bf16[32,2048]{1,0:T(8,128)(2,1)S(1)}, u32[]{:S(2)}, u32[]{:S(2)}) collective-permute-start(bf16[32,2048]{1,0:T(8,128)(2,1)} %get-tuple-element.60), channel_id=1, source_target_pairs={{0,4},{4,0},{8,12},{12,8},{16,20},{20,16},{24,28},{28,24},{1,5},{5... | collective-permute-start | bytes 393224 | tf_op jit(solution)/shard_map/ppermute | solution.py:205
  131.9 18.0 %collective-permute-start.14 = (bf16[32,2048]{1,0:T(8,128)(2,1)}, bf16[32,2048]{1,0:T(8,128)(2,1)S(1)}, u32[]{:S(2)}, u32[]{:S(2)}) collective-permute-start(bf16[32,2048]{1,0:T(8,128)(2,1)} %get-tuple-element.61), channel_id=1, source_target_pairs={{0,8},{4,12},{8,0},{12,4},{16,24},{20,28},{24,16},{28,20},{1,9},{5... | collective-permute-start | bytes 393224 | tf_op jit(solution)/shard_map/ppermute | solution.py:205
  142.7 15.2 %collective-permute-start.15 = (bf16[32,2048]{1,0:T(8,128)(2,1)}, bf16[32,2048]{1,0:T(8,128)(2,1)S(1)}, u32[]{:S(2)}, u32[]{:S(2)}) collective-permute-start(bf16[32,2048]{1,0:T(8,128)(2,1)} %get-tuple-element.62), channel_id=1, source_target_pairs={{0,12},{4,8},{8,4},{12,0},{16,28},{20,24},{24,20},{28,16},{1,13},{... | collective-permute-start | bytes 393224 | tf_op jit(solution)/shard_map/ppermute | solution.py:205
  143.4 15.2 %collective-permute-start.16 = (bf16[32,2048]{1,0:T(8,128)(2,1)}, bf16[32,2048]{1,0:T(8,128)(2,1)S(1)}, u32[]{:S(2)}, u32[]{:S(2)}) collective-permute-start(bf16[32,2048]{1,0:T(8,128)(2,1)} %get-tuple-element.63), channel_id=1, source_target_pairs={{0,16},{4,20},{8,24},{12,28},{16,0},{20,4},{24,8},{28,12},{1,17},{... | collective-permute-start | bytes 393224 | tf_op jit(solution)/shard_map/ppermute | solution.py:205
  147.6 19.3 %collective-permute-start.17 = (bf16[32,2048]{1,0:T(8,128)(2,1)}, bf16[32,2048]{1,0:T(8,128)(2,1)S(1)}, u32[]{:S(2)}, u32[]{:S(2)}) collective-permute-start(bf16[32,2048]{1,0:T(8,128)(2,1)} %copy-done.11), channel_id=1, source_target_pairs={{0,20},{4,16},{8,28},{12,24},{16,4},{20,0},{24,12},{28,8},{1,21},{... | collective-permute-start | bytes 393224 | tf_op jit(solution)/shard_map/ppermute | solution.py:205
  149.9 17.0 %collective-permute-start.18 = (bf16[32,2048]{1,0:T(8,128)(2,1)}, bf16[32,2048]{1,0:T(8,128)(2,1)S(1)}, u32[]{:S(2)}, u32[]{:S(2)}) collective-permute-start(bf16[32,2048]{1,0:T(8,128)(2,1)} %copy-done.10), channel_id=1, source_target_pairs={{0,24},{4,28},{8,16},{12,20},{16,8},{20,12},{24,0},{28,4},{1,25},{... | collective-permute-start | bytes 393224 | tf_op jit(solution)/shard_map/ppermute | solution.py:205
  150.4 20.2 %collective-permute-start.19 = (bf16[32,2048]{1,0:T(8,128)(2,1)S(1)}, bf16[32,2048]{1,0:T(8,128)(2,1)S(1)}, u32[]{:S(2)}, u32[]{:S(2)}) collective-permute-start(bf16[32,2048]{1,0:T(8,128)(2,1)S(1)} %get-tuple-element.66), channel_id=1, source_target_pairs={{0,28},{4,24},{8,20},{12,16},{16,12},{20,8},{24,4},{28,0},{1,29},{... | collective-permute-start | bytes 393224 | tf_op jit(solution)/shard_map/ppermute | solution.py:205
  157.9 17.4 %collective-permute-start.22 = (bf16[24,2048]{1,0:T(8,128)(2,1)S(1)}, bf16[24,2048]{1,0:T(8,128)(2,1)S(1)}, u32[]{:S(2)}, u32[]{:S(2)}) collective-permute-start(bf16[24,2048]{1,0:T(8,128)(2,1)S(1)} %get-tuple-element.73), channel_id=1, source_target_pairs={{0,4},{4,0},{8,12},{12,8},{16,20},{20,16},{24,28},{28,24},{1,5},{5... | collective-permute-start | bytes 294920 | tf_op jit(solution)/shard_map/ppermute | solution.py:205
  158.6 17.9 %collective-permute-start.23 = (bf16[24,2048]{1,0:T(8,128)(2,1)S(1)}, bf16[24,2048]{1,0:T(8,128)(2,1)S(1)}, u32[]{:S(2)}, u32[]{:S(2)}) collective-permute-start(bf16[24,2048]{1,0:T(8,128)(2,1)S(1)} %get-tuple-element.74), channel_id=1, source_target_pairs={{0,8},{4,12},{8,0},{12,4},{16,24},{20,28},{24,16},{28,20},{1,9},{5... | collective-permute-start | bytes 294920 | tf_op jit(solution)/shard_map/ppermute | solution.py:205
  166.9 13.4 %collective-permute-start.24 = (bf16[24,2048]{1,0:T(8,128)(2,1)S(1)}, bf16[24,2048]{1,0:T(8,128)(2,1)S(1)}, u32[]{:S(2)}, u32[]{:S(2)}) collective-permute-start(bf16[24,2048]{1,0:T(8,128)(2,1)S(1)} %get-tuple-element.75), channel_id=1, source_target_pairs={{0,12},{4,8},{8,4},{12,0},{16,28},{20,24},{24,20},{28,16},{1,13},{... | collective-permute-start | bytes 294920 | tf_op jit(solution)/shard_map/ppermute | solution.py:205
  166.9 13.3 %collective-permute-start.25 = (bf16[24,2048]{1,0:T(8,128)(2,1)S(1)}, bf16[24,2048]{1,0:T(8,128)(2,1)S(1)}, u32[]{:S(2)}, u32[]{:S(2)}) collective-permute-start(bf16[24,2048]{1,0:T(8,128)(2,1)S(1)} %get-tuple-element.76), channel_id=1, source_target_pairs={{0,16},{4,20},{8,24},{12,28},{16,0},{20,4},{24,8},{28,12},{1,17},{... | collective-permute-start | bytes 294920 | tf_op jit(solution)/shard_map/ppermute | solution.py:205
  170.5 14.6 %collective-permute-start.26 = (bf16[24,2048]{1,0:T(8,128)(2,1)S(1)}, bf16[24,2048]{1,0:T(8,128)(2,1)S(1)}, u32[]{:S(2)}, u32[]{:S(2)}) collective-permute-start(bf16[24,2048]{1,0:T(8,128)(2,1)S(1)} %get-tuple-element.77), channel_id=1, source_target_pairs={{0,20},{4,16},{8,28},{12,24},{16,4},{20,0},{24,12},{28,8},{1,21},{... | collective-permute-start | bytes 294920 | tf_op jit(solution)/shard_map/ppermute | solution.py:205
  175.3 9.9 %collective-permute-start.27 = (bf16[24,2048]{1,0:T(8,128)(2,1)S(1)}, bf16[24,2048]{1,0:T(8,128)(2,1)S(1)}, u32[]{:S(2)}, u32[]{:S(2)}) collective-permute-start(bf16[24,2048]{1,0:T(8,128)(2,1)S(1)} %get-tuple-element.78), channel_id=1, source_target_pairs={{0,24},{4,28},{8,16},{12,20},{16,8},{20,12},{24,0},{28,4},{1,25},{... | collective-permute-start | bytes 294920 | tf_op jit(solution)/shard_map/ppermute | solution.py:205
  189.6 10.1 %collective-permute-start.30 = (bf16[24,2048]{1,0:T(8,128)(2,1)S(1)}, bf16[24,2048]{1,0:T(8,128)(2,1)S(1)}, u32[]{:S(2)}, u32[]{:S(2)}) collective-permute-start(bf16[24,2048]{1,0:T(8,128)(2,1)S(1)} %get-tuple-element.85), channel_id=1, source_target_pairs={{0,8},{4,12},{8,0},{12,4},{16,24},{20,28},{24,16},{28,20},{1,9},{5... | collective-permute-start | bytes 294920 | tf_op jit(solution)/shard_map/ppermute | solution.py:205
  193.9 13.8 %collective-permute-start.32 = (bf16[24,2048]{1,0:T(8,128)(2,1)S(1)}, bf16[24,2048]{1,0:T(8,128)(2,1)S(1)}, u32[]{:S(2)}, u32[]{:S(2)}) collective-permute-start(bf16[24,2048]{1,0:T(8,128)(2,1)S(1)} %get-tuple-element.87), channel_id=1, source_target_pairs={{0,16},{4,20},{8,24},{12,28},{16,0},{20,4},{24,8},{28,12},{1,17},{... | collective-permute-start | bytes 294920 | tf_op jit(solution)/shard_map/ppermute | solution.py:205
  196.4 14.5 %collective-permute-start.33 = (bf16[24,2048]{1,0:T(8,128)(2,1)S(1)}, bf16[24,2048]{1,0:T(8,128)(2,1)S(1)}, u32[]{:S(2)}, u32[]{:S(2)}) collective-permute-start(bf16[24,2048]{1,0:T(8,128)(2,1)S(1)} %get-tuple-element.88), channel_id=1, source_target_pairs={{0,20},{4,16},{8,28},{12,24},{16,4},{20,0},{24,12},{28,8},{1,21},{... | collective-permute-start | bytes 294920 | tf_op jit(solution)/shard_map/ppermute | solution.py:205
  197.3 13.5 %collective-permute-start.34 = (bf16[24,2048]{1,0:T(8,128)(2,1)S(1)}, bf16[24,2048]{1,0:T(8,128)(2,1)S(1)}, u32[]{:S(2)}, u32[]{:S(2)}) collective-permute-start(bf16[24,2048]{1,0:T(8,128)(2,1)S(1)} %get-tuple-element.89), channel_id=1, source_target_pairs={{0,24},{4,28},{8,16},{12,20},{16,8},{20,12},{24,0},{28,4},{1,25},{... | collective-permute-start | bytes 294920 | tf_op jit(solution)/shard_map/ppermute | solution.py:205
  199.7 11.1 %collective-permute-start.35 = (bf16[24,2048]{1,0:T(8,128)(2,1)S(1)}, bf16[24,2048]{1,0:T(8,128)(2,1)S(1)}, u32[]{:S(2)}, u32[]{:S(2)}) collective-permute-start(bf16[24,2048]{1,0:T(8,128)(2,1)S(1)} %get-tuple-element.90), channel_id=1, source_target_pairs={{0,28},{4,24},{8,20},{12,16},{16,12},{20,8},{24,4},{28,0},{1,29},{... | collective-permute-start | bytes 294920 | tf_op jit(solution)/shard_map/ppermute | solution.py:205
  (18 other events, 192.0 us)

commit v2 on v1

--- a/solution.py
+++ b/solution.py
@@ -19,7 +19,9 @@
     return lax.dot_general(a, b, dims, preferred_element_type=F32)
 
 
-def call(kernel, outs, args, scratch=(), smem=(), name=None, mib=40, flops=0):
+def call(
+    kernel, outs, args, scratch=(), smem=(), far=(), far_out=(), name=None, mib=40, flops=0
+):
     moved = sum(a.size * a.dtype.itemsize for a in args) + sum(
         o.size * o.dtype.itemsize for o in outs
     )
@@ -27,10 +29,15 @@
         kernel,
         out_shape=tuple(outs),
         in_specs=[
-            pl.BlockSpec(memory_space=pltpu.SMEM if i in smem else pltpu.VMEM)
+            pl.BlockSpec(
+                memory_space=pltpu.SMEM if i in smem else pl.ANY if i in far else pltpu.VMEM
+            )
             for i in range(len(args))
         ],
-        out_specs=tuple(pl.BlockSpec(memory_space=pltpu.VMEM) for _ in outs),
+        out_specs=tuple(
+            pl.BlockSpec(memory_space=pl.ANY if i in far_out else pltpu.VMEM)
+            for i in range(len(outs))
+        ),
         scratch_shapes=list(scratch),
         compiler_params=pltpu.CompilerParams(vmem_limit_bytes=mib * 2**20),
         cost_estimate=pl.CostEstimate(flops=flops, bytes_accessed=moved, transcendentals=0),
@@ -43,7 +50,17 @@
     return [slice(c, c + step) for c in range(0, width, step)]
 
 
-def pack_kernel(n, capacity, joint, r_ref, x_ref, g_ref, place_ref, *outs):
+def pack_kernel(
+    n, capacity, joint, r_ref, x_ref, g_ref, gate_ref, up_ref, place_ref, joined_ref, *rest
+):
+    outs, sem = rest[:-1], rest[-1]
+    part = gate_ref.shape[0]
+    copies = [
+        pltpu.make_async_copy(ref, joined_ref.at[i * part : (i + 1) * part], sem.at[i])
+        for i, ref in enumerate((gate_ref, up_ref))
+    ]
+    for copy in copies:
+        copy.start()
     e = lax.axis_index("expert")
     owned, width = x_ref.shape
     rel = r_ref[...] ^ e
@@ -67,12 +84,8 @@
                     ]
             else:
                 outs[half][:, cols] = packed
-
-
-def turn_kernel(gate_ref, up_ref, out_ref):
-    part = gate_ref.shape[2]
-    out_ref[:part] = gate_ref[0].T
-    out_ref[part:] = up_ref[0].T
+    for copy in copies:
+        copy.wait()
 
 
 def halves(blocks, half):
@@ -83,30 +96,33 @@
     return parts[0] if len(parts) == 1 else jnp.concatenate(parts, axis=0)
 
 
+def fetch(pairs, sem):
+    copies = [pltpu.make_async_copy(src, dst, sem.at[i]) for i, (src, dst) in enumerate(pairs)]
+    for copy in copies:
+        copy.start()
+    return copies
+
+
 def hidden_kernel(nb, m, *refs):
     blocks, weights = refs[:nb], refs[nb : nb + m]
-    hidden_ref, a_ref, b_ref = refs[nb + m :]
+    send_ref, keep_ref, a_ref, b_ref, held, hidden, sem = refs[nb + m :]
+    copies = fetch([(w, held.at[r]) for r, w in enumerate(weights)], sem)
     x = halves(blocks, 0)
     part = weights[0].shape[0] // 2
     for r in range(m):
-        gate = dot(weights[r][:part], x, NT)
-        up = dot(weights[r][part:], x, NT)
+        copies[r].wait()
+        gate = dot(held[r, :part], x, NT)
+        up = dot(held[r, part:], x, NT)
         sig = jax.nn.sigmoid(gate)
         silu = gate * sig
-        hidden_ref[r] = (silu * up).astype(BF16)
+        hidden[r] = (silu * up).astype(BF16)
         a_ref[r] = up * sig * (1.0 + gate * (1.0 - sig))
         b_ref[r] = silu
-
-
-def grad_kernel(nb, m, *refs):
-    blocks, hidden_ref = refs[:nb], refs[nb]
-    send_ref, keep_ref = refs[nb + 1 :]
-    part = hidden_ref.shape[1]
     g = halves(blocks, 1)
     for r in range(m):
         rows = slice(r // 2 * part, (r // 2 + 1) * part)
         for cols in columns(g.shape[1]):
-            value = dot(hidden_ref[r], g[:, cols], NN)
+            value = dot(hidden[r], g[:, cols], NN)
             if r % 2:
                 send_ref[rows, cols] = value.astype(BF16)
             else:
@@ -116,17 +132,22 @@
 def back_kernel(nb, m, *refs):
     blocks, weights, down = refs[:nb], refs[nb : nb + m], refs[nb + m : nb + 2 * m]
     a_ref, b_ref = refs[nb + 2 * m : nb + 2 * m + 2]
-    outs, (total, turned) = refs[nb + 2 * m + 2 : -2], refs[-2:]
+    outs, (held, low, turned, sem) = refs[nb + 2 * m + 2 : -4], refs[-4:]
+    pairs = [(d, low.at[r]) for r, d in enumerate(down)]
+    copies = fetch(pairs + [(w, held.at[r]) for r, w in enumerate(weights)], sem)
     g = halves(blocks, 1)
     part = down[0].shape[0]
     for r in range(m):
-        dh = dot(down[r][...], g, NT)
+        copies[r].wait()
+        dh = dot(low[r], g, NT)
         turned[r, :part] = (dh * a_ref[r]).astype(BF16)
         turned[r, part:] = (dh * b_ref[r]).astype(BF16)
+    for r in range(m):
+        copies[m + r].wait()
     for cols in columns(g.shape[1]):
-        acc = dot(turned[0], weights[0][:, cols], TN)
+        acc = dot(turned[0], held[0, :, cols], TN)
         for r in range(1, m):
-            acc = acc + dot(turned[r], weights[r][:, cols], TN)
+            acc = acc + dot(turned[r], held[r, :, cols], TN)
         acc = acc.astype(BF16)
         start = 0
         for out in outs:
@@ -200,6 +221,12 @@
         out_ref[:, cols] = dot(place, rows, NN).astype(BF16)
 
 
+def order_kernel(n, *refs):
+    e = lax.axis_index("expert")
+    for d in range(n):
+        refs[n][e ^ d] = refs[d][...]
+
+
 def swap(x, axis, mask):
     size = lax.axis_size(axis)
     return lax.ppermute(x, axis, [(i, i ^ mask) for i in range(size)])
@@ -225,15 +252,28 @@
     return jnp.take(x, turn, axis=0)
 
 
-def gather_slot(x):
-    m = lax.axis_size("slot")
+def far_steps(m):
+    masks = [1 << i for i in range(m.bit_length() - 1)]
+    return masks[:0:-1]
+
+
+def gather_far(x, m):
     have = {0: x}
-    mask = m // 2
-    while mask:
+    for mask in far_steps(m):
         for r in sorted(have):
             have[r | mask] = swap(have[r], "slot", mask)
-        mask //= 2
+    return have
+
+
+def gather_near(have, m):
+    have = dict(have)
+    for r in sorted(have):
+        have[r | 1] = swap(have[r], "slot", 1)
     return [have[r] for r in range(m)]
+
+
+def after(x, *others):
+    return lax.optimization_barrier((x, *others))
 
 
 def body(
@@ -248,18 +288,20 @@
     turn = jnp.arange(n, dtype=jnp.int32) ^ lax.axis_index("expert")
     shape = jax.ShapeDtypeStruct
 
-    outs = [shape((owned, rows), BF16)]
+    outs = [shape((owned, rows), BF16), shape((2 * part, width), BF16)]
     outs += [shape((2 * capacity, width), BF16)] * n if few else [shape((rows, width), BF16)] * 2
-    place, *packed = call(
+    gate_rows, up_rows = (jnp.swapaxes(w, 1, 2)[0] for w in (gate_weight, up_weight))
+    place, joined, *packed = call(
         functools.partial(pack_kernel, n, capacity, few),
         outs,
-        (routing, tokens, out_grad),
+        (routing, tokens, out_grad, gate_rows, up_rows),
+        scratch=[pltpu.SemaphoreType.DMA((2,))],
+        far=(3, 4),
+        far_out=(1,),
         name="pack_rows",
         flops=4 * owned * rows * width,
     )
-    (joined,) = call(
-        turn_kernel, [shape((2 * part, width), BF16)], (gate_weight, up_weight), name="turn_weights"
-    )
+    joined = gather_far(joined, m)
     if few:
         blocks = exchange(packed)
     else:
@@ -268,32 +310,46 @@
         )
         blocks = [jnp.concatenate((x, g), axis=0)]
     nb = len(blocks)
-    joined = gather_slot(joined)
-    down = gather_slot(down_weight[0])
-
-    hidden, a, b = call(
+    down, blocks[nb // 2] = after(down_weight[0], blocks[nb // 2])
+    down = gather_far(down, m)
+    blocks, joined = lax.optimization_barrier((blocks, joined))
+    joined = gather_near(joined, m)
+
+    send, keep, a, b = call(
         functools.partial(hidden_kernel, nb, m),
-        [shape((m, part, rows), BF16), shape((m, part, rows), F32), shape((m, part, rows), F32)],
+        [
+            shape((m // 2 * part, width), BF16),
+            shape((m // 2 * part, width), F32),
+            shape((m, part, rows), F32),
+            shape((m, part, rows), F32),
+        ],
         (*blocks, *joined),
+        scratch=[
+            pltpu.VMEM((m, 2 * part, width), BF16),
+            pltpu.VMEM((m, part, rows), BF16),
+            pltpu.SemaphoreType.DMA((m,)),
+        ],
+        far=range(nb, nb + m),
         name="hidden_units",
-        flops=4 * rows * width * part * m,
-    )
-    send, keep = call(
-        functools.partial(grad_kernel, nb, m),
-        [shape((m // 2 * part, width), BF16), shape((m // 2 * part, width), F32)],
-        (*blocks, hidden),
-        name="down_gradient",
-        flops=2 * rows * width * part * m,
-    )
+        flops=6 * rows * width * part * m,
+    )
+    send, down = lax.optimization_barrier((send, down))
+    got = swap(send, "slot", 1)
+    down = gather_near(down, m)
     dx = call(
         functools.partial(back_kernel, nb, m),
         [shape((r.shape[0] // 2, width), BF16) for r in blocks],
         (*blocks, *joined, *down, a, b),
-        scratch=[pltpu.VMEM((8, 128), F32), pltpu.VMEM((m, 2 * part, rows), BF16)],
+        scratch=[
+            pltpu.VMEM((m, 2 * part, width), BF16),
+            pltpu.VMEM((m, part, width), BF16),
+            pltpu.VMEM((m, 2 * part, rows), BF16),
+            pltpu.SemaphoreType.DMA((2 * m,)),
+        ],
+        far=range(nb, nb + 2 * m),
         name="input_gradient",
         flops=6 * rows * width * part * m,
     )
-    got = swap(send, "slot", 1)
     first, *rest = call(
         add_kernel,
         [shape((part, width), F32)] + [shape((part, width), BF16)] * (m // 2 - 1),
@@ -334,7 +390,12 @@
         flops=2 * owned * rows * width,
     )
     if few:
-        fresh = jnp.take(jnp.stack(exchange(outgoing)), turn, axis=0)
+        (fresh,) = call(
+            functools.partial(order_kernel, n),
+            [shape((n, owner, width), BF16)],
+            exchange(outgoing),
+            name="order_rows",
+        )
     else:
         fresh = exchange_whole(outgoing[0])
     return (token_grad, new_master, new_moment, new_second, fresh.reshape(1, part, width))

time: 213 us -> 170 us (0.80)
  waiting for transfers between devices: 104 us -> 64.6 us
  local copies, waits for them, and re-layouts: 11 us -> 7.09 us
  starting transfers between devices: 74.1 us -> 76.4 us
    ppermute x36, waiting for transfers between devices: 104 us -> 64.6 us  [swap(): return lax.ppermute(x, axis, [(i, i ^ mask) for i in range(size)])]
    unnamed x38 -> x21, local copies, waits for them, and re-layouts: 10.2 us -> 7.09 us
    ppermute x36, starting transfers between devices: 74.1 us -> 76.4 us  [swap(): return lax.ppermute(x, axis, [(i, i ^ mask) for i in range(size)])]
    pallas_call x9 -> x8, Pallas kernels: 21.4 us -> 20 us  [call(): pl.pallas_call(kernel, out_shape=tuple(outs), in_specs=[pl.BlockSpec(memo...]
  transfers between devices with their start and end apart: 36 -> 36, of which waited for: 10 -> 13; matrix products, arithmetic and copies ran while one was open for 0% -> 0% of each run, Pallas kernels for 5% -> 11%
where the time goes in v2:
time: 170 us; the launch traced here: 169 us
  starting transfers between devices  76.4 us (45%)
  waiting for transfers between devices  64.6 us (38%)
  Pallas kernels  20 us (12%)
  local copies, waits for them, and re-layouts  7.09 us (4%)
    ppermute x36, starting transfers between devices, swap(): return lax.ppermute(x, axis, [(i, i ^ mask) for i in range(size)])  76.4 us
    ppermute x36, waiting for transfers between devices, swap(): return lax.ppermute(x, axis, [(i, i ^ mask) for i in range(size)])  64.6 us
    pallas_call x8, Pallas kernels, call(): pl.pallas_call(kernel, out_shape=tuple(outs), in_specs=[pl.BlockSpec(memo...  20 us
    unnamed x21, local copies, waits for them, and re-layouts  7.09 us
  transfers between devices with their start and end apart: 36, of which 13 were waited for; matrix products, arithmetic and copies ran while one was open for 0% of the time, Pallas kernels for 11%

profile of v2, /device:TPU:0, one launch (start us, length us, event | category | flops | bytes accessed | tf_op | source)
XLA Modules:
  0.0 168.9 jit_solution(4322349376422428035)
XLA Ops:
  7.0 3.0 %collective-permute-start.7 = (bf16[384,2048]{1,0:T(8,128)(2,1)S(1)}, bf16[384,2048]{1,0:T(8,128)(2,1)S(1)}, u32[]{:S(2)}, u32[]{:S(2)}) collective-permute-start(bf16[384,2048]{1,0:T(8,128)(2,1)S(1)} %get-tuple-element.82.refs_8_), channel_id=1, source_target_pairs={{0,2},{1,3},{2,0},{3,1},{4,6},{5,7},{6,4},{7,5},{8,10},{9,11},{10,... | collective-permute-start | bytes 4718600 | tf_op jit(solution)/shard_map/ppermute | solution.py:232
  10.0 2.6 %collective-permute-start.3 = (bf16[64,2048]{1,0:T(8,128)(2,1)S(1)}, bf16[64,2048]{1,0:T(8,128)(2,1)S(1)}, u32[]{:S(2)}, u32[]{:S(2)}) collective-permute-start(bf16[64,2048]{1,0:T(8,128)(2,1)S(1)} %get-tuple-element.68), channel_id=1, source_target_pairs={{0,16},{4,20},{8,24},{12,28},{16,0},{20,4},{24,8},{28,12},{1,17},{... | collective-permute-start | bytes 786440 | tf_op jit(solution)/shard_map/ppermute | solution.py:232
  12.6 1.5 collective-permute-start
  14.1 1.6 collective-permute-start.1
  16.1 8.3 %collective-permute-done.3.refs_4_ = bf16[64,2048]{1,0:T(8,128)(2,1)S(1)} collective-permute-done((bf16[64,2048]{1,0:T(8,128)(2,1)S(1)}, bf16[64,2048]{1,0:T(8,128)(2,1)S(1)}, u32[]{:S(2)}, u32[]{:S(2)}) %collective-permute-start.3) | collective-permute-done | bytes 262176 | tf_op jit(solution)/shard_map/ppermute | solution.py:232
  24.8 3.5 %collective-permute-start.5 = (bf16[64,2048]{1,0:T(8,128)(2,1)S(1)}, bf16[64,2048]{1,0:T(8,128)(2,1)S(1)}, u32[]{:S(2)}, u32[]{:S(2)}) collective-permute-start(bf16[64,2048]{1,0:T(8,128)(2,1)S(1)} %get-tuple-element.71), channel_id=1, source_target_pairs={{0,24},{4,28},{8,16},{12,20},{16,8},{20,12},{24,0},{28,4},{1,25},{... | collective-permute-start | bytes 786440 | tf_op jit(solution)/shard_map/ppermute | solution.py:232
  30.2 5.1 %collective-permute-done.2.refs_3_ = bf16[64,2048]{1,0:T(8,128)(2,1)S(1)} collective-permute-done((bf16[64,2048]{1,0:T(8,128)(2,1)S(1)}, bf16[64,2048]{1,0:T(8,128)(2,1)S(1)}, u32[]{:S(2)}, u32[]{:S(2)}) %collective-permute-start.2) | collective-permute-done | bytes 262176 | tf_op jit(solution)/shard_map/ppermute | solution.py:232
  35.3 17.0 %collective-permute-done.4.refs_5_ = bf16[64,2048]{1,0:T(8,128)(2,1)S(1)} collective-permute-done((bf16[64,2048]{1,0:T(8,128)(2,1)S(1)}, bf16[64,2048]{1,0:T(8,128)(2,1)S(1)}, u32[]{:S(2)}, u32[]{:S(2)}) %collective-permute-start.4) | collective-permute-done | bytes 262176 | tf_op jit(solution)/shard_map/ppermute | solution.py:232
  53.3 2.4 %collective-permute-done.8.refs_9_ = bf16[384,2048]{1,0:T(8,128)(2,1)S(1)} collective-permute-done((bf16[384,2048]{1,0:T(8,128)(2,1)S(1)}, bf16[384,2048]{1,0:T(8,128)(2,1)S(1)}, u32[]{:S(2)}, u32[]{:S(2)}) %collective-permute-start.8) | collective-permute-done | bytes 1572896 | tf_op jit(solution)/shard_map/ppermute | solution.py:232
  55.8 2.2 %collective-permute-done.9.refs_11_ = bf16[384,2048]{1,0:T(8,128)(2,1)S(1)} collective-permute-done((bf16[384,2048]{1,0:T(8,128)(2,1)S(1)}, bf16[384,2048]{1,0:T(8,128)(2,1)S(1)}, u32[]{:S(2)}, u32[]{:S(2)}) %collective-permute-start.9) | collective-permute-done | bytes 1572896 | tf_op jit(solution)/shard_map/ppermute | solution.py:232
  58.0 6.2 %hidden_units.1 = (bf16[384,2048]{1,0:T(8,128)(2,1)S(1)}, f32[384,2048]{1,0:T(8,128)}, f32[4,192,256]{2,1,0:T(8,128)S(1)}, f32[4,192,256]{2,1,0:T(8,128)S(1)}) custom-call(bf16[64,2048]{1,0:T(8,128)(2,1)S(1)} %get-tuple-element.74.refs_0_, bf16[64,2048]{1,0:T(8,128)(2,1)S(1)} %collective-permute-done.refs_1_, ...), custom_call_target="tpu_custom_call" | custom-call | flops 2415919104 | bytes 14680064 | tf_op jit(solution)/shard_map/hidden_units/pallas_call | solution.py:28
  64.2 8.2 %collective-permute-done.10.refs_14_ = bf16[192,2048]{1,0:T(8,128)(2,1)S(1)} collective-permute-done((bf16[192,2048]{1,0:T(8,128)(2,1)S(1)}, bf16[192,2048]{1,0:T(8,128)(2,1)S(1)}, u32[]{:S(2)}, u32[]{:S(2)}) %collective-permute-start.10) | collective-permute-done | bytes 786464 | tf_op jit(solution)/shard_map/ppermute | solution.py:232
  72.9 2.9 %collective-permute-done.20.got_ref = bf16[384,2048]{1,0:T(8,128)(2,1)S(1)} collective-permute-done((bf16[384,2048]{1,0:T(8,128)(2,1)S(1)}, bf16[384,2048]{1,0:T(8,128)(2,1)S(1)}, u32[]{:S(2)}, u32[]{:S(2)}) %collective-permute-start.20) | collective-permute-done | bytes 1572896 | tf_op jit(solution)/shard_map/ppermute | solution.py:232
  75.8 1.9 %copy-done = f32[384,2048]{1,0:T(8,128)S(1)} copy-done((f32[384,2048]{1,0:T(8,128)S(1)}, f32[384,2048]{1,0:T(8,128)}, u32[]{:S(2)}) %copy-start) | copy-done | bytes 3145752
  78.5 6.2 %input_gradient.1 = (bf16[32,2048]{1,0:T(8,128)(2,1)S(1)}, bf16[32,2048]{1,0:T(8,128)(2,1)S(1)}, bf16[32,2048]{1,0:T(8,128)(2,1)S(1)}, bf16[32,2048]{1,0:T(8,128...) custom-call(bf16[64,2048]{1,0:T(8,128)(2,1)S(1)} %get-tuple-element., ...), custom_call_target="tpu_custom_call" | custom-call | flops 2415919104 | bytes 14155776 | tf_op jit(solution)/shard_map/input_gradient/pallas_call | solution.py:28
  84.8 1.5 collective-permute-start.13
  86.3 9.9 %collective-permute-start.14 = (bf16[32,2048]{1,0:T(8,128)(2,1)S(1)}, bf16[32,2048]{1,0:T(8,128)(2,1)S(1)}, u32[]{:S(2)}, u32[]{:S(2)}) collective-permute-start(bf16[32,2048]{1,0:T(8,128)(2,1)S(1)} %get-tuple-element.92), channel_id=1, source_target_pairs={{0,8},{4,12},{8,0},{12,4},{16,24},{20,28},{24,16},{28,20},{1,9},{5... | collective-permute-start | bytes 393224 | tf_op jit(solution)/shard_map/ppermute | solution.py:232
  99.3 9.9 %collective-permute-start.23 = (bf16[24,2048]{1,0:T(8,128)(2,1)S(1)}, bf16[24,2048]{1,0:T(8,128)(2,1)S(1)}, u32[]{:S(2)}, u32[]{:S(2)}) collective-permute-start(bf16[24,2048]{1,0:T(8,128)(2,1)S(1)} %get-tuple-element.104), channel_id=1, source_target_pairs={{0,8},{4,12},{8,0},{12,4},{16,24},{20,28},{24,16},{28,20},{1,9},{5... | collective-permute-start | bytes 294920 | tf_op jit(solution)/shard_map/ppermute | solution.py:232
  110.0 4.0 %collective-permute-start.25 = (bf16[24,2048]{1,0:T(8,128)(2,1)S(1)}, bf16[24,2048]{1,0:T(8,128)(2,1)S(1)}, u32[]{:S(2)}, u32[]{:S(2)}) collective-permute-start(bf16[24,2048]{1,0:T(8,128)(2,1)S(1)} %get-tuple-element.106), channel_id=1, source_target_pairs={{0,16},{4,20},{8,24},{12,28},{16,0},{20,4},{24,8},{28,12},{1,17},{... | collective-permute-start | bytes 294920 | tf_op jit(solution)/shard_map/ppermute | solution.py:232
  114.9 2.3 %collective-permute-start.27 = (bf16[24,2048]{1,0:T(8,128)(2,1)S(1)}, bf16[24,2048]{1,0:T(8,128)(2,1)S(1)}, u32[]{:S(2)}, u32[]{:S(2)}) collective-permute-start(bf16[24,2048]{1,0:T(8,128)(2,1)S(1)} %get-tuple-element.108), channel_id=1, source_target_pairs={{0,24},{4,28},{8,16},{12,20},{16,8},{20,12},{24,0},{28,4},{1,25},{... | collective-permute-start | bytes 294920 | tf_op jit(solution)/shard_map/ppermute | solution.py:232
  117.2 1.6 collective-permute-start.28
  119.3 3.2 %collective-permute-start.16 = (bf16[32,2048]{1,0:T(8,128)(2,1)S(1)}, bf16[32,2048]{1,0:T(8,128)(2,1)S(1)}, u32[]{:S(2)}, u32[]{:S(2)}) collective-permute-start(bf16[32,2048]{1,0:T(8,128)(2,1)S(1)} %get-tuple-element.94), channel_id=1, source_target_pairs={{0,16},{4,20},{8,24},{12,28},{16,0},{20,4},{24,8},{28,12},{1,17},{... | collective-permute-start | bytes 393224 | tf_op jit(solution)/shard_map/ppermute | solution.py:232
  122.5 7.7 %collective-permute-done.26.refs_6_ = bf16[24,2048]{1,0:T(8,128)(2,1)S(1)} collective-permute-done((bf16[24,2048]{1,0:T(8,128)(2,1)S(1)}, bf16[24,2048]{1,0:T(8,128)(2,1)S(1)}, u32[]{:S(2)}, u32[]{:S(2)}) %collective-permute-start.26) | collective-permute-done | bytes 98336 | tf_op jit(solution)/shard_map/ppermute | solution.py:232
  130.2 8.8 %collective-permute-start.18 = (bf16[32,2048]{1,0:T(8,128)(2,1)S(1)}, bf16[32,2048]{1,0:T(8,128)(2,1)S(1)}, u32[]{:S(2)}, u32[]{:S(2)}) collective-permute-start(bf16[32,2048]{1,0:T(8,128)(2,1)S(1)} %get-tuple-element.96), channel_id=1, source_target_pairs={{0,24},{4,28},{8,16},{12,20},{16,8},{20,12},{24,0},{28,4},{1,25},{... | collective-permute-start | bytes 393224 | tf_op jit(solution)/shard_map/ppermute | solution.py:232
  139.1 3.9 %adam.1 = (f32[6,24,2048]{2,1,0:T(8,128)}, f32[6,24,2048]{2,1,0:T(8,128)}, f32[6,24,2048]{2,1,0:T(8,128)}, bf16[24,2048]{1,0:T(8,128)(2,1)S(1)}, bf16[24,2048]{1...) custom-call(s32[8]{0:T(128)S(1)} %copy-done.9, ...), custom_call_target="tpu_custom_call" | custom-call | bytes 8650784 | tf_op jit(solution)/shard_map/adam/pallas_call | solution.py:28
  144.4 1.8 %collective-permute-done.16.refs_4_ = bf16[32,2048]{1,0:T(8,128)(2,1)S(1)} collective-permute-done((bf16[32,2048]{1,0:T(8,128)(2,1)S(1)}, bf16[32,2048]{1,0:T(8,128)(2,1)S(1)}, u32[]{:S(2)}, u32[]{:S(2)}) %collective-permute-start.16) | collective-permute-done | bytes 131104 | tf_op jit(solution)/shard_map/ppermute | solution.py:232
  146.2 2.0 %collective-permute-start.30 = (bf16[24,2048]{1,0:T(8,128)(2,1)S(1)}, bf16[24,2048]{1,0:T(8,128)(2,1)S(1)}, u32[]{:S(2)}, u32[]{:S(2)}) collective-permute-start(bf16[24,2048]{1,0:T(8,128)(2,1)S(1)} %get-tuple-element.115), channel_id=1, source_target_pairs={{0,8},{4,12},{8,0},{12,4},{16,24},{20,28},{24,16},{28,20},{1,9},{5... | collective-permute-start | bytes 294920 | tf_op jit(solution)/shard_map/ppermute | solution.py:232
  149.5 3.2 %collective-permute-start.32 = (bf16[24,2048]{1,0:T(8,128)(2,1)S(1)}, bf16[24,2048]{1,0:T(8,128)(2,1)S(1)}, u32[]{:S(2)}, u32[]{:S(2)}) collective-permute-start(bf16[24,2048]{1,0:T(8,128)(2,1)S(1)} %get-tuple-element.117), channel_id=1, source_target_pairs={{0,16},{4,20},{8,24},{12,28},{16,0},{20,4},{24,8},{28,12},{1,17},{... | collective-permute-start | bytes 294920 | tf_op jit(solution)/shard_map/ppermute | solution.py:232
  152.7 4.5 %collective-permute-start.33 = (bf16[24,2048]{1,0:T(8,128)(2,1)S(1)}, bf16[24,2048]{1,0:T(8,128)(2,1)S(1)}, u32[]{:S(2)}, u32[]{:S(2)}) collective-permute-start(bf16[24,2048]{1,0:T(8,128)(2,1)S(1)} %get-tuple-element.118), channel_id=1, source_target_pairs={{0,20},{4,16},{8,28},{12,24},{16,4},{20,0},{24,12},{28,8},{1,21},{... | collective-permute-start | bytes 294920 | tf_op jit(solution)/shard_map/ppermute | solution.py:232
  157.2 2.5 %collective-permute-start.34 = (bf16[24,2048]{1,0:T(8,128)(2,1)S(1)}, bf16[24,2048]{1,0:T(8,128)(2,1)S(1)}, u32[]{:S(2)}, u32[]{:S(2)}) collective-permute-start(bf16[24,2048]{1,0:T(8,128)(2,1)S(1)} %get-tuple-element.119), channel_id=1, source_target_pairs={{0,24},{4,28},{8,16},{12,20},{16,8},{20,12},{24,0},{28,4},{1,25},{... | collective-permute-start | bytes 294920 | tf_op jit(solution)/shard_map/ppermute | solution.py:232
  159.7 2.3 %collective-permute-start.35 = (bf16[24,2048]{1,0:T(8,128)(2,1)S(1)}, bf16[24,2048]{1,0:T(8,128)(2,1)S(1)}, u32[]{:S(2)}, u32[]{:S(2)}) collective-permute-start(bf16[24,2048]{1,0:T(8,128)(2,1)S(1)} %get-tuple-element.120), channel_id=1, source_target_pairs={{0,28},{4,24},{8,20},{12,16},{16,12},{20,8},{24,4},{28,0},{1,29},{... | collective-permute-start | bytes 294920 | tf_op jit(solution)/shard_map/ppermute | solution.py:232
  163.1 4.8 %collective-permute-done.33.refs_5_ = bf16[24,2048]{1,0:T(8,128)(2,1)S(1)} collective-permute-done((bf16[24,2048]{1,0:T(8,128)(2,1)S(1)}, bf16[24,2048]{1,0:T(8,128)(2,1)S(1)}, u32[]{:S(2)}, u32[]{:S(2)}) %collective-permute-start.33) | collective-permute-done | bytes 98336 | tf_op jit(solution)/shard_map/ppermute | solution.py:232
  (69 shorter events, 21.6 us)
Async XLA Ops:
  7.0 45.3 %collective-permute-start.7 = (bf16[384,2048]{1,0:T(8,128)(2,1)S(1)}, bf16[384,2048]{1,0:T(8,128)(2,1)S(1)}, u32[]{:S(2)}, u32[]{:S(2)}) collective-permute-start(bf16[384,2048]{1,0:T(8,128)(2,1)S(1)} %get-tuple-element.82.refs_8_), channel_id=1, source_target_pairs={{0,2},{1,3},{2,0},{3,1},{4,6},{5,7},{6,4},{7,5},{8,10},{9,11},{10,... | collective-permute-start | bytes 4718600 | tf_op jit(solution)/shard_map/ppermute | solution.py:232
  10.0 14.4 %collective-permute-start.3 = (bf16[64,2048]{1,0:T(8,128)(2,1)S(1)}, bf16[64,2048]{1,0:T(8,128)(2,1)S(1)}, u32[]{:S(2)}, u32[]{:S(2)}) collective-permute-start(bf16[64,2048]{1,0:T(8,128)(2,1)S(1)} %get-tuple-element.68), channel_id=1, source_target_pairs={{0,16},{4,20},{8,24},{12,28},{16,0},{20,4},{24,8},{28,12},{1,17},{... | collective-permute-start | bytes 786440 | tf_op jit(solution)/shard_map/ppermute | solution.py:232
  12.6 12.2 %collective-permute-start = (bf16[64,2048]{1,0:T(8,128)(2,1)S(1)}, bf16[64,2048]{1,0:T(8,128)(2,1)S(1)}, u32[]{:S(2)}, u32[]{:S(2)}) collective-permute-start(bf16[64,2048]{1,0:T(8,128)(2,1)S(1)} %get-tuple-element.65), channel_id=1, source_target_pairs={{0,4},{4,0},{8,12},{12,8},{16,20},{20,16},{24,28},{28,24},{1,5},{5... | collective-permute-start | bytes 786440 | tf_op jit(solution)/shard_map/ppermute | solution.py:232
  14.1 15.6 %collective-permute-start.1 = (bf16[64,2048]{1,0:T(8,128)(2,1)S(1)}, bf16[64,2048]{1,0:T(8,128)(2,1)S(1)}, u32[]{:S(2)}, u32[]{:S(2)}) collective-permute-start(bf16[64,2048]{1,0:T(8,128)(2,1)S(1)} %get-tuple-element.66), channel_id=1, source_target_pairs={{0,8},{4,12},{8,0},{12,4},{16,24},{20,28},{24,16},{28,20},{1,9},{5... | collective-permute-start | bytes 786440 | tf_op jit(solution)/shard_map/ppermute | solution.py:232
  15.7 19.6 %collective-permute-start.2 = (bf16[64,2048]{1,0:T(8,128)(2,1)S(1)}, bf16[64,2048]{1,0:T(8,128)(2,1)S(1)}, u32[]{:S(2)}, u32[]{:S(2)}) collective-permute-start(bf16[64,2048]{1,0:T(8,128)(2,1)S(1)} %get-tuple-element.67), channel_id=1, source_target_pairs={{0,12},{4,8},{8,4},{12,0},{16,28},{20,24},{24,20},{28,16},{1,13},{... | collective-permute-start | bytes 786440 | tf_op jit(solution)/shard_map/ppermute | solution.py:232
  24.4 27.9 %collective-permute-start.4 = (bf16[64,2048]{1,0:T(8,128)(2,1)S(1)}, bf16[64,2048]{1,0:T(8,128)(2,1)S(1)}, u32[]{:S(2)}, u32[]{:S(2)}) collective-permute-start(bf16[64,2048]{1,0:T(8,128)(2,1)S(1)} %get-tuple-element.70), channel_id=1, source_target_pairs={{0,20},{4,16},{8,28},{12,24},{16,4},{20,0},{24,12},{28,8},{1,21},{... | collective-permute-start | bytes 786440 | tf_op jit(solution)/shard_map/ppermute | solution.py:232
  24.8 27.5 %collective-permute-start.5 = (bf16[64,2048]{1,0:T(8,128)(2,1)S(1)}, bf16[64,2048]{1,0:T(8,128)(2,1)S(1)}, u32[]{:S(2)}, u32[]{:S(2)}) collective-permute-start(bf16[64,2048]{1,0:T(8,128)(2,1)S(1)} %get-tuple-element.71), channel_id=1, source_target_pairs={{0,24},{4,28},{8,16},{12,20},{16,8},{20,12},{24,0},{28,4},{1,25},{... | collective-permute-start | bytes 786440 | tf_op jit(solution)/shard_map/ppermute | solution.py:232
  29.7 22.6 %collective-permute-start.6 = (bf16[64,2048]{1,0:T(8,128)(2,1)S(1)}, bf16[64,2048]{1,0:T(8,128)(2,1)S(1)}, u32[]{:S(2)}, u32[]{:S(2)}) collective-permute-start(bf16[64,2048]{1,0:T(8,128)(2,1)S(1)} %get-tuple-element.72), channel_id=1, source_target_pairs={{0,28},{4,24},{8,20},{12,16},{16,12},{20,8},{24,4},{28,0},{1,29},{... | collective-permute-start | bytes 786440 | tf_op jit(solution)/shard_map/ppermute | solution.py:232
  52.9 19.5 %collective-permute-start.10 = (bf16[192,2048]{1,0:T(8,128)(2,1)S(1)}, bf16[192,2048]{1,0:T(8,128)(2,1)S(1)}, u32[]{:S(2)}, u32[]{:S(2)}) collective-permute-start(bf16[192,2048]{1,0:T(8,128)(2,1)S(1)} %bitcast.8), channel_id=1, source_target_pairs={{0,2},{1,3},{2,0},{3,1},{4,6},{5,7},{6,4},{7,5},{8,10},{9,11},{10,... | collective-permute-start | bytes 2359304 | tf_op jit(solution)/shard_map/ppermute | solution.py:232
  72.4 6.1 %collective-permute-start.11 = (bf16[192,2048]{1,0:T(8,128)(2,1)S(1)}, bf16[192,2048]{1,0:T(8,128)(2,1)S(1)}, u32[]{:S(2)}, u32[]{:S(2)}) collective-permute-start(bf16[192,2048]{1,0:T(8,128)(2,1)S(1)} %bitcast.9), channel_id=1, source_target_pairs={{0,1},{1,0},{2,3},{3,2},{4,5},{5,4},{6,7},{7,6},{8,9},{9,8},{10,11... | collective-permute-start | bytes 2359304 | tf_op jit(solution)/shard_map/ppermute | solution.py:232
  78.0 19.6 %collective-permute-start.21 = (bf16[192,2048]{1,0:T(8,128)(2,1)S(1)}, bf16[192,2048]{1,0:T(8,128)(2,1)S(1)}, u32[]{:S(2)}, u32[]{:S(2)}) collective-permute-start(bf16[192,2048]{1,0:T(8,128)(2,1)S(1)} %get-tuple-element.101), channel_id=1, source_target_pairs={{0,2},{1,3},{2,0},{3,1},{4,6},{5,7},{6,4},{7,5},{8,10},{9,11},{10,... | collective-permute-start | bytes 2359304 | tf_op jit(solution)/shard_map/ppermute | solution.py:232
  84.8 25.2 %collective-permute-start.13 = (bf16[32,2048]{1,0:T(8,128)(2,1)S(1)}, bf16[32,2048]{1,0:T(8,128)(2,1)S(1)}, u32[]{:S(2)}, u32[]{:S(2)}) collective-permute-start(bf16[32,2048]{1,0:T(8,128)(2,1)S(1)} %get-tuple-element.91), channel_id=1, source_target_pairs={{0,4},{4,0},{8,12},{12,8},{16,20},{20,16},{24,28},{28,24},{1,5},{5... | collective-permute-start | bytes 393224 | tf_op jit(solution)/shard_map/ppermute | solution.py:232
  86.3 27.7 %collective-permute-start.14 = (bf16[32,2048]{1,0:T(8,128)(2,1)S(1)}, bf16[32,2048]{1,0:T(8,128)(2,1)S(1)}, u32[]{:S(2)}, u32[]{:S(2)}) collective-permute-start(bf16[32,2048]{1,0:T(8,128)(2,1)S(1)} %get-tuple-element.92), channel_id=1, source_target_pairs={{0,8},{4,12},{8,0},{12,4},{16,24},{20,28},{24,16},{28,20},{1,9},{5... | collective-permute-start | bytes 393224 | tf_op jit(solution)/shard_map/ppermute | solution.py:232
  97.9 17.0 %collective-permute-start.22 = (bf16[24,2048]{1,0:T(8,128)(2,1)S(1)}, bf16[24,2048]{1,0:T(8,128)(2,1)S(1)}, u32[]{:S(2)}, u32[]{:S(2)}) collective-permute-start(bf16[24,2048]{1,0:T(8,128)(2,1)S(1)} %get-tuple-element.103), channel_id=1, source_target_pairs={{0,4},{4,0},{8,12},{12,8},{16,20},{20,16},{24,28},{28,24},{1,5},{5... | collective-permute-start | bytes 294920 | tf_op jit(solution)/shard_map/ppermute | solution.py:232
  99.3 17.9 %collective-permute-start.23 = (bf16[24,2048]{1,0:T(8,128)(2,1)S(1)}, bf16[24,2048]{1,0:T(8,128)(2,1)S(1)}, u32[]{:S(2)}, u32[]{:S(2)}) collective-permute-start(bf16[24,2048]{1,0:T(8,128)(2,1)S(1)} %get-tuple-element.104), channel_id=1, source_target_pairs={{0,8},{4,12},{8,0},{12,4},{16,24},{20,28},{24,16},{28,20},{1,9},{5... | collective-permute-start | bytes 294920 | tf_op jit(solution)/shard_map/ppermute | solution.py:232
  109.2 9.7 %collective-permute-start.24 = (bf16[24,2048]{1,0:T(8,128)(2,1)S(1)}, bf16[24,2048]{1,0:T(8,128)(2,1)S(1)}, u32[]{:S(2)}, u32[]{:S(2)}) collective-permute-start(bf16[24,2048]{1,0:T(8,128)(2,1)S(1)} %get-tuple-element.105), channel_id=1, source_target_pairs={{0,12},{4,8},{8,4},{12,0},{16,28},{20,24},{24,20},{28,16},{1,13},{... | collective-permute-start | bytes 294920 | tf_op jit(solution)/shard_map/ppermute | solution.py:232
  110.0 9.3 %collective-permute-start.25 = (bf16[24,2048]{1,0:T(8,128)(2,1)S(1)}, bf16[24,2048]{1,0:T(8,128)(2,1)S(1)}, u32[]{:S(2)}, u32[]{:S(2)}) collective-permute-start(bf16[24,2048]{1,0:T(8,128)(2,1)S(1)} %get-tuple-element.106), channel_id=1, source_target_pairs={{0,16},{4,20},{8,24},{12,28},{16,0},{20,4},{24,8},{28,12},{1,17},{... | collective-permute-start | bytes 294920 | tf_op jit(solution)/shard_map/ppermute | solution.py:232
  114.0 16.2 %collective-permute-start.26 = (bf16[24,2048]{1,0:T(8,128)(2,1)S(1)}, bf16[24,2048]{1,0:T(8,128)(2,1)S(1)}, u32[]{:S(2)}, u32[]{:S(2)}) collective-permute-start(bf16[24,2048]{1,0:T(8,128)(2,1)S(1)} %get-tuple-element.107), channel_id=1, source_target_pairs={{0,20},{4,16},{8,28},{12,24},{16,4},{20,0},{24,12},{28,8},{1,21},{... | collective-permute-start | bytes 294920 | tf_op jit(solution)/shard_map/ppermute | solution.py:232
  114.9 15.3 %collective-permute-start.27 = (bf16[24,2048]{1,0:T(8,128)(2,1)S(1)}, bf16[24,2048]{1,0:T(8,128)(2,1)S(1)}, u32[]{:S(2)}, u32[]{:S(2)}) collective-permute-start(bf16[24,2048]{1,0:T(8,128)(2,1)S(1)} %get-tuple-element.108), channel_id=1, source_target_pairs={{0,24},{4,28},{8,16},{12,20},{16,8},{20,12},{24,0},{28,4},{1,25},{... | collective-permute-start | bytes 294920 | tf_op jit(solution)/shard_map/ppermute | solution.py:232
  117.2 21.8 %collective-permute-start.28 = (bf16[24,2048]{1,0:T(8,128)(2,1)S(1)}, bf16[24,2048]{1,0:T(8,128)(2,1)S(1)}, u32[]{:S(2)}, u32[]{:S(2)}) collective-permute-start(bf16[24,2048]{1,0:T(8,128)(2,1)S(1)} %get-tuple-element.109), channel_id=1, source_target_pairs={{0,28},{4,24},{8,20},{12,16},{16,12},{20,8},{24,4},{28,0},{1,29},{... | collective-permute-start | bytes 294920 | tf_op jit(solution)/shard_map/ppermute | solution.py:232
  118.8 24.2 %collective-permute-start.15 = (bf16[32,2048]{1,0:T(8,128)(2,1)S(1)}, bf16[32,2048]{1,0:T(8,128)(2,1)S(1)}, u32[]{:S(2)}, u32[]{:S(2)}) collective-permute-start(bf16[32,2048]{1,0:T(8,128)(2,1)S(1)} %get-tuple-element.93), channel_id=1, source_target_pairs={{0,12},{4,8},{8,4},{12,0},{16,28},{20,24},{24,20},{28,16},{1,13},{... | collective-permute-start | bytes 393224 | tf_op jit(solution)/shard_map/ppermute | solution.py:232
  119.3 26.9 %collective-permute-start.16 = (bf16[32,2048]{1,0:T(8,128)(2,1)S(1)}, bf16[32,2048]{1,0:T(8,128)(2,1)S(1)}, u32[]{:S(2)}, u32[]{:S(2)}) collective-permute-start(bf16[32,2048]{1,0:T(8,128)(2,1)S(1)} %get-tuple-element.94), channel_id=1, source_target_pairs={{0,16},{4,20},{8,24},{12,28},{16,0},{20,4},{24,8},{28,12},{1,17},{... | collective-permute-start | bytes 393224 | tf_op jit(solution)/shard_map/ppermute | solution.py:232
  130.2 19.3 %collective-permute-start.17 = (bf16[32,2048]{1,0:T(8,128)(2,1)S(1)}, bf16[32,2048]{1,0:T(8,128)(2,1)S(1)}, u32[]{:S(2)}, u32[]{:S(2)}) collective-permute-start(bf16[32,2048]{1,0:T(8,128)(2,1)S(1)} %get-tuple-element.95), channel_id=1, source_target_pairs={{0,20},{4,16},{8,28},{12,24},{16,4},{20,0},{24,12},{28,8},{1,21},{... | collective-permute-start | bytes 393224 | tf_op jit(solution)/shard_map/ppermute | solution.py:232
  130.2 19.3 %collective-permute-start.18 = (bf16[32,2048]{1,0:T(8,128)(2,1)S(1)}, bf16[32,2048]{1,0:T(8,128)(2,1)S(1)}, u32[]{:S(2)}, u32[]{:S(2)}) collective-permute-start(bf16[32,2048]{1,0:T(8,128)(2,1)S(1)} %get-tuple-element.96), channel_id=1, source_target_pairs={{0,24},{4,28},{8,16},{12,20},{16,8},{20,12},{24,0},{28,4},{1,25},{... | collective-permute-start | bytes 393224 | tf_op jit(solution)/shard_map/ppermute | solution.py:232
  139.0 13.7 %collective-permute-start.19 = (bf16[32,2048]{1,0:T(8,128)(2,1)S(1)}, bf16[32,2048]{1,0:T(8,128)(2,1)S(1)}, u32[]{:S(2)}, u32[]{:S(2)}) collective-permute-start(bf16[32,2048]{1,0:T(8,128)(2,1)S(1)} %get-tuple-element.97), channel_id=1, source_target_pairs={{0,28},{4,24},{8,20},{12,16},{16,12},{20,8},{24,4},{28,0},{1,29},{... | collective-permute-start | bytes 393224 | tf_op jit(solution)/shard_map/ppermute | solution.py:232
  143.0 14.2 %collective-permute-start.29 = (bf16[24,2048]{1,0:T(8,128)(2,1)S(1)}, bf16[24,2048]{1,0:T(8,128)(2,1)S(1)}, u32[]{:S(2)}, u32[]{:S(2)}) collective-permute-start(bf16[24,2048]{1,0:T(8,128)(2,1)S(1)} %get-tuple-element.114), channel_id=1, source_target_pairs={{0,4},{4,0},{8,12},{12,8},{16,20},{20,16},{24,28},{28,24},{1,5},{5... | collective-permute-start | bytes 294920 | tf_op jit(solution)/shard_map/ppermute | solution.py:232
  146.2 13.5 %collective-permute-start.30 = (bf16[24,2048]{1,0:T(8,128)(2,1)S(1)}, bf16[24,2048]{1,0:T(8,128)(2,1)S(1)}, u32[]{:S(2)}, u32[]{:S(2)}) collective-permute-start(bf16[24,2048]{1,0:T(8,128)(2,1)S(1)} %get-tuple-element.115), channel_id=1, source_target_pairs={{0,8},{4,12},{8,0},{12,4},{16,24},{20,28},{24,16},{28,20},{1,9},{5... | collective-permute-start | bytes 294920 | tf_op jit(solution)/shard_map/ppermute | solution.py:232
  149.5 13.6 %collective-permute-start.31 = (bf16[24,2048]{1,0:T(8,128)(2,1)S(1)}, bf16[24,2048]{1,0:T(8,128)(2,1)S(1)}, u32[]{:S(2)}, u32[]{:S(2)}) collective-permute-start(bf16[24,2048]{1,0:T(8,128)(2,1)S(1)} %get-tuple-element.116), channel_id=1, source_target_pairs={{0,12},{4,8},{8,4},{12,0},{16,28},{20,24},{24,20},{28,16},{1,13},{... | collective-permute-start | bytes 294920 | tf_op jit(solution)/shard_map/ppermute | solution.py:232
  149.5 13.6 %collective-permute-start.32 = (bf16[24,2048]{1,0:T(8,128)(2,1)S(1)}, bf16[24,2048]{1,0:T(8,128)(2,1)S(1)}, u32[]{:S(2)}, u32[]{:S(2)}) collective-permute-start(bf16[24,2048]{1,0:T(8,128)(2,1)S(1)} %get-tuple-element.117), channel_id=1, source_target_pairs={{0,16},{4,20},{8,24},{12,28},{16,0},{20,4},{24,8},{28,12},{1,17},{... | collective-permute-start | bytes 294920 | tf_op jit(solution)/shard_map/ppermute | solution.py:232
  152.7 15.3 %collective-permute-start.33 = (bf16[24,2048]{1,0:T(8,128)(2,1)S(1)}, bf16[24,2048]{1,0:T(8,128)(2,1)S(1)}, u32[]{:S(2)}, u32[]{:S(2)}) collective-permute-start(bf16[24,2048]{1,0:T(8,128)(2,1)S(1)} %get-tuple-element.118), channel_id=1, source_target_pairs={{0,20},{4,16},{8,28},{12,24},{16,4},{20,0},{24,12},{28,8},{1,21},{... | collective-permute-start | bytes 294920 | tf_op jit(solution)/shard_map/ppermute | solution.py:232
  157.2 10.7 %collective-permute-start.34 = (bf16[24,2048]{1,0:T(8,128)(2,1)S(1)}, bf16[24,2048]{1,0:T(8,128)(2,1)S(1)}, u32[]{:S(2)}, u32[]{:S(2)}) collective-permute-start(bf16[24,2048]{1,0:T(8,128)(2,1)S(1)} %get-tuple-element.119), channel_id=1, source_target_pairs={{0,24},{4,28},{8,16},{12,20},{16,8},{20,12},{24,0},{28,4},{1,25},{... | collective-permute-start | bytes 294920 | tf_op jit(solution)/shard_map/ppermute | solution.py:232
  159.7 8.2 %collective-permute-start.35 = (bf16[24,2048]{1,0:T(8,128)(2,1)S(1)}, bf16[24,2048]{1,0:T(8,128)(2,1)S(1)}, u32[]{:S(2)}, u32[]{:S(2)}) collective-permute-start(bf16[24,2048]{1,0:T(8,128)(2,1)S(1)} %get-tuple-element.120), channel_id=1, source_target_pairs={{0,28},{4,24},{8,20},{12,16},{16,12},{20,8},{24,4},{28,0},{1,29},{... | collective-permute-start | bytes 294920 | tf_op jit(solution)/shard_map/ppermute | solution.py:232
  (14 other events, 300.3 us)

commit v3 on v1

v3 whole, which is shorter than its diff:
```python
import functools

import jax
import jax.numpy as jnp
from jax import lax
from jax.experimental import pallas as pl
from jax.experimental.pallas import tpu as pltpu
from jax.sharding import PartitionSpec as P

BF16 = jnp.bfloat16
F32 = jnp.float32
NT = (((1,), (1,)), ((), ()))
TN = (((0,), (0,)), ((), ()))
NN = (((1,), (0,)), ((), ()))
COLUMNS = 512
EARLY = 5


def dot(a, b, dims):
    return lax.dot_general(a, b, dims, preferred_element_type=F32)


def call(
    kernel, outs, args, scratch=(), smem=(), far=(), far_out=(), name=None, mib=40, flops=0
):
    moved = sum(a.size * a.dtype.itemsize for a in args) + sum(
        o.size * o.dtype.itemsize for o in outs
    )
    return pl.pallas_call(
        kernel,
        out_shape=tuple(outs),
        in_specs=[
            pl.BlockSpec(
                memory_space=pltpu.SMEM if i in smem else pl.ANY if i in far else pltpu.VMEM
            )
            for i in range(len(args))
        ],
        out_specs=tuple(
            pl.BlockSpec(memory_space=pl.ANY if i in far_out else pltpu.VMEM)
            for i in range(len(outs))
        ),
        scratch_shapes=list(scratch),
        compiler_params=pltpu.CompilerParams(vmem_limit_bytes=mib * 2**20),
        cost_estimate=pl.CostEstimate(flops=flops, bytes_accessed=moved, transcendentals=0),
        name=name,
    )(*args)


def columns(width):
    step = min(COLUMNS, width)
    return [slice(c, c + step) for c in range(0, width, step)]


def pack_kernel(n, capacity, joint, r_ref, x_ref, g_ref, *refs):
    weights, place_ref, joined_ref, outs = refs[:3], refs[3], refs[4], refs[5:-3]
    x_held, g_held, sem = refs[-3:]
    part = weights[0].shape[0]
    pairs = [(x_ref, x_held), (g_ref, g_held)]
    pairs += [(w, joined_ref.at[i * part : (i + 1) * part]) for i, w in enumerate(weights)]
    copies = [pltpu.make_async_copy(src, dst, sem.at[i]) for i, (src, dst) in enumerate(pairs)]
    for copy in copies:
        copy.start()
    e = lax.axis_index("expert")
    owned, width = x_ref.shape
    rel = r_ref[...] ^ e
    block = lax.broadcasted_iota(jnp.int32, (n, owned), 0)
    match = (rel == block).astype(F32)
    upper = lax.broadcasted_iota(jnp.int32, (owned, owned), 0) <= lax.broadcasted_iota(
        jnp.int32, (owned, owned), 1
    )
    count = dot(match.astype(BF16), upper.astype(BF16), NN)
    pos = jnp.sum(match * (count - 1.0 + (block * capacity).astype(F32)), axis=0, keepdims=True)
    spot = lax.broadcasted_iota(jnp.int32, (n * capacity, owned), 0)
    place = (pos.astype(jnp.int32) == spot).astype(BF16)
    place_ref[...] = place
    for half, held in enumerate((x_held, g_held)):
        copies[half].wait()
        for cols in columns(width):
            packed = dot(place, held[:, cols], NN).astype(BF16)
            if joint:
                for d in range(n):
                    outs[d][half * capacity : (half + 1) * capacity, cols] = packed[
                        d * capacity : (d + 1) * capacity
                    ]
            else:
                outs[half][:, cols] = packed
    for copy in copies[2:]:
        copy.wait()


def halves(blocks, half):
    parts = []
    for ref in blocks:
        rows = ref.shape[0] // 2
        parts.append(ref[half * rows : (half + 1) * rows])
    return parts[0] if len(parts) == 1 else jnp.concatenate(parts, axis=0)


def forward(weight, x):
    part = weight.shape[0] // 3
    both = dot(weight[: 2 * part], x, NT)
    gate, up = both[:part], both[part:]
    sig = jax.nn.sigmoid(gate)
    silu = gate * sig
    return (silu * up).astype(BF16), up * sig * (1.0 + gate * (1.0 - sig)), silu


def weight_gradient(hidden, g, send_ref, keep_ref):
    part = hidden.shape[1]
    for r in range(hidden.shape[0]):
        rows = slice(r // 2 * part, (r // 2 + 1) * part)
        for cols in columns(g.shape[1]):
            value = dot(hidden[r], g[:, cols], NN).astype(BF16)
            (send_ref if r % 2 else keep_ref)[rows, cols] = value


def turn(weight, g, a, b):
    part = weight.shape[0] // 3
    dh = dot(weight[2 * part :], g, NT)
    both = jnp.concatenate(((dh * a).astype(BF16), (dh * b).astype(BF16)), axis=0)
    return both.T


def input_gradient(turned, weights, cols):
    wide = weights[0].shape[0] // 3 * 2
    total = None
    for r, weight in enumerate(weights):
        term = dot(turned[:, r * wide : (r + 1) * wide], weight[:wide, cols], NN)
        total = term if total is None else total + term
    return total


def near_kernel(nb, nw, *refs):
    blocks, weights = refs[:nb], refs[nb : nb + nw]
    send_ref, keep_ref, partial_ref, hidden, turned = refs[nb + nw :]
    x, g = halves(blocks, 0), halves(blocks, 1)
    wide = weights[0].shape[0] // 3 * 2
    for r in range(nw):
        hidden[r], a, b = forward(weights[r], x)
        turned[:, r * wide : (r + 1) * wide] = turn(weights[r], g, a, b)
    weight_gradient(hidden, g, send_ref, keep_ref)
    for cols in columns(g.shape[1]):
        partial_ref[:, cols] = input_gradient(turned, weights, cols)


def hidden_kernel(nb, nw, *refs):
    blocks, weights = refs[:nb], refs[nb : nb + nw]
    send_ref, keep_ref, a_ref, b_ref, hidden = refs[nb + nw :]
    x, g = halves(blocks, 0), halves(blocks, 1)
    for r in range(nw):
        hidden[r], a_ref[r], b_ref[r] = forward(weights[r], x)
    weight_gradient(hidden, g, send_ref, keep_ref)


def back_kernel(nb, nw, *refs):
    blocks, weights = refs[:nb], refs[nb : nb + nw]
    a_ref, b_ref, partial_ref = refs[nb + nw : nb + nw + 3]
    outs, turned = refs[nb + nw + 3 : -1], refs[-1]
    g = halves(blocks, 1)
    wide = weights[0].shape[0] // 3 * 2
    for r in range(nw):
        turned[:, r * wide : (r + 1) * wide] = turn(weights[r], g, a_ref[r], b_ref[r])
    for cols in columns(g.shape[1]):
        total = (partial_ref[:, cols] + input_gradient(turned, weights, cols)).astype(BF16)
        start = 0
        for out in outs:
            out[:, cols] = total[start : start + out.shape[0]]
            start += out.shape[0]


def add_kernel(keep_ref, got_ref, *outs):
    part = outs[0].shape[0]
    for i, out in enumerate(outs):
        rows = slice(i * part, (i + 1) * part)
        out[...] = (keep_ref[rows].astype(F32) + got_ref[rows].astype(F32)).astype(BF16)


def cut_kernel(count, blocks, *refs):
    terms, outs, sums = refs[:count], refs[count:-1], refs[-1]
    e = lax.axis_index("expert")
    total = terms[0][...].astype(F32)
    for ref in terms[1:]:
        total = total + ref[...].astype(F32)
    if len(outs) == 1:
        outs[0][...] = total.astype(BF16)
        return
    sums[...] = total
    rows = outs[0].shape[0]
    for d, out in zip(blocks, outs, strict=True):
        out[...] = sums[pl.ds(pl.multiple_of((e ^ d) * rows, 8), rows)].astype(BF16)


def fold(blocks, plan_ref, pieces, folded):
    e = lax.axis_index("expert")
    folded[...] = jnp.zeros_like(folded)
    for i, d in enumerate(blocks):
        p = plan_ref[e ^ d]
        piece = pieces[0][i] if len(pieces) == 1 else pieces[i][...]
        folded[p] = folded[p] + piece.astype(F32)


def adam_update(folded, master, moment, second):
    new_moment = 0.9 * moment + 0.1 * folded
    new_second = 0.95 * second + 0.05 * folded * folded
    first_hat = new_moment / (1.0 - 0.9**10)
    second_hat = new_second / (1.0 - 0.95**10)
    new_master = master - 0.01 * (first_hat / (jnp.sqrt(second_hat) + 1e-08) + 0.1 * master)
    return new_master, new_moment, new_second


def rows_kernel(blocks, count, plan_ref, *refs):
    pieces, (master_ref, moment_ref, second_ref) = refs[:count], refs[count : count + 3]
    outs, folded = refs[count + 3 : -1], refs[-1]
    e = lax.axis_index("expert")
    fold(blocks, plan_ref, pieces, folded)
    for p in range(folded.shape[0]):
        folded[p] = adam_update(folded[p], master_ref[p], moment_ref[p], second_ref[p])[0]
    for i, d in enumerate(blocks):
        row = folded[plan_ref[e ^ d]].astype(BF16)
        if len(outs) == 1:
            outs[0][i] = row
        else:
            outs[i][...] = row


def state_kernel(blocks, count, plan_ref, *refs):
    pieces, (master_ref, moment_ref, second_ref) = refs[:count], refs[count : count + 3]
    new_master, new_moment, new_second, folded = refs[count + 3 :]
    fold(blocks, plan_ref, pieces, folded)
    for p in range(folded.shape[0]):
        new_master[p], new_moment[p], new_second[p] = adam_update(
            folded[p], master_ref[p], moment_ref[p], second_ref[p]
        )


def unpack_kernel(blocks, place_ref, *refs):
    parts, out_ref = refs[:-1], refs[-1]
    place = place_ref[...].T
    if len(parts) > 1:
        parts = [parts[blocks.index(d)] for d in range(len(parts))]
    for cols in columns(out_ref.shape[1]):
        rows = [p[:, cols] for p in parts]
        rows = rows[0] if len(rows) == 1 else jnp.concatenate(rows, axis=0)
        out_ref[:, cols] = dot(place, rows, NN).astype(BF16)


def order_kernel(blocks, *refs):
    e = lax.axis_index("expert")
    for i, d in enumerate(blocks):
        refs[-1][e ^ d] = refs[i][...]


def swap(x, axis, mask):
    size = lax.axis_size(axis)
    return lax.ppermute(x, axis, [(i, i ^ mask) for i in range(size)])


def order(n):
    return [0, n // 2, *(d for d in range(1, n) if d != n // 2)]


def exchange(blocks):
    return [
        swap(block, "expert", d) if d else block
        for d, block in zip(order(len(blocks)), blocks, strict=True)
    ]


def exchange_whole(x):
    flip = jnp.arange(x.shape[0], dtype=jnp.int32) ^ lax.axis_index("expert")
    x = jnp.take(x, flip, axis=0)
    x = lax.all_to_all(x, "expert", split_axis=0, concat_axis=0, tiled=True)
    return jnp.take(x, flip, axis=0)


def body(
    tokens, out_grad, routing, plan, gate_weight, up_weight, down_weight, master, moment, second
):
    n, m = lax.axis_size("expert"), lax.axis_size("slot")
    owned, width = tokens.shape
    capacity = 2 * owned // n
    part = down_weight.shape[1]
    owner = part // n
    rows = n * capacity
    few = capacity % 16 == 0
    ways = order(n) if few else list(range(n))
    shape = jax.ShapeDtypeStruct

    weights = [jnp.swapaxes(w, 1, 2)[0] for w in (gate_weight, up_weight)] + [down_weight[0]]
    outs = [shape((rows, owned), BF16), shape((3 * part, width), BF16)]
    outs += [shape((2 * capacity, width), BF16)] * n if few else [shape((rows, width), BF16)] * 2
    place, joined, *packed = call(
        functools.partial(pack_kernel, n, capacity, few),
        outs,
        (routing.reshape(1, owned), tokens, out_grad, *weights),
        scratch=[
            pltpu.VMEM((owned, width), BF16),
            pltpu.VMEM((owned, width), BF16),
            pltpu.SemaphoreType.DMA((5,)),
        ],
        far=range(1, 6),
        name="pack_rows",
        mib=56,
        flops=4 * owned * rows * width,
    )
    held = {0: joined}
    for mask in [1 << i for i in range(1, m.bit_length() - 1)][::-1]:
        for r in sorted(held):
            held[r | mask] = swap(held[r], "slot", mask)
    near = [joined, swap(joined, "slot", 1)]
    if few:
        blocks = exchange([packed[d] for d in ways])
    else:
        x, g = (
            exchange_whole(p.reshape(n, capacity, width)).reshape(rows, width) for p in packed
        )
        blocks = [jnp.concatenate((x, g), axis=0)]
    nb = len(blocks)
    blocks, held, near = lax.optimization_barrier((blocks, held, near))
    far = []
    for r in range(2, m, 2):
        far += [held[r], swap(held[r], "slot", 1)]
    nf = len(far)

    send, keep, partial = call(
        functools.partial(near_kernel, nb, 2),
        [shape((part, width), BF16), shape((part, width), BF16), shape((rows, width), F32)],
        (*blocks, *near),
        scratch=[pltpu.VMEM((2, part, rows), BF16), pltpu.VMEM((rows, 4 * part), BF16)],
        name="near_units",
        flops=24 * rows * width * part,
    )
    first = [keep, swap(send, "slot", 1)]
    far, partial = lax.optimization_barrier((far, partial))
    send, keep, a, b = call(
        functools.partial(hidden_kernel, nb, nf),
        [shape((nf // 2 * part, width), BF16)] * 2 + [shape((nf, part, rows), F32)] * 2,
        (*blocks, *far),
        scratch=[pltpu.VMEM((nf, part, rows), BF16)],
        name="far_units",
        flops=6 * rows * width * part * nf,
    )
    dx = call(
        functools.partial(back_kernel, nb, nf),
        [shape((r.shape[0] // 2, width), BF16) for r in blocks],
        (*blocks, *far, a, b, partial),
        scratch=[pltpu.VMEM((rows, nf * 2 * part), BF16)],
        name="input_gradient",
        flops=6 * rows * width * part * nf,
    )
    rest = call(
        add_kernel,
        [shape((part, width), BF16)] * (nf // 2),
        (keep, swap(send, "slot", 1)),
        name="add_pair",
    )
    rest = [swap(r, "slot", 2 * i) for i, r in enumerate(rest, 1)]
    if few:
        returned = exchange(dx)
        ahead = min(EARLY, n)
        returned[:ahead], rest = lax.optimization_barrier((returned[:ahead], rest))
    else:
        returned = [exchange_whole(dx[0].reshape(n, capacity, width)).reshape(rows, width)]
    pieces = call(
        functools.partial(cut_kernel, len(first) + len(rest), ways),
        [shape((owner, width), BF16)] * n if few else [shape((part, width), BF16)],
        (*first, *rest),
        scratch=[pltpu.VMEM((part, width), F32)],
        name="cut_gradient",
    )
    if few:
        arrived = exchange(pieces)
    else:
        flip = jnp.arange(n, dtype=jnp.int32) ^ lax.axis_index("expert")
        arrived = [exchange_whole(jnp.take(pieces[0].reshape(n, owner, width), flip, axis=0))]
    state = (plan, *arrived, master, moment, second)
    outgoing = call(
        functools.partial(rows_kernel, ways, len(arrived)),
        [shape((owner, width), BF16)] * n if few else [shape((n, owner, width), BF16)],
        state,
        scratch=[pltpu.VMEM(master.shape, F32)],
        smem=(0,),
        name="new_rows",
    )
    new_master, new_moment, new_second = call(
        functools.partial(state_kernel, ways, len(arrived)),
        [shape(master.shape, F32)] * 3,
        state,
        scratch=[pltpu.VMEM(master.shape, F32)],
        smem=(0,),
        name="new_state",
    )
    (token_grad,) = call(
        functools.partial(unpack_kernel, ways),
        [shape((owned, width), BF16)],
        (place, *returned),
        name="unpack_rows",
        flops=2 * owned * rows * width,
    )
    if few:
        (fresh,) = call(
            functools.partial(order_kernel, ways),
            [shape((n, owner, width), BF16)],
            exchange(outgoing),
            name="order_rows",
        )
    else:
        fresh = exchange_whole(outgoing[0])
    return (token_grad, new_master, new_moment, new_second, fresh.reshape(1, part, width))


def solution(mesh):
    rows, state = P(("expert", "slot"), None), P(None, ("slot", "expert"), None)
    split, held = P("expert", None, "slot"), P("expert", "slot", None)
    return jax.shard_map(
        body,
        mesh=mesh,
        in_specs=(rows, rows, rows, P(), split, split, held, state, state, state),
        out_specs=(rows, state, state, state, held),
        check_vma=False,
    )
```

time: 213 us -> 150 us (0.70)
  waiting for transfers between devices: 104 us -> 62.5 us
  starting transfers between devices: 74.1 us -> 62.9 us
  local copies, waits for them, and re-layouts: 11 us -> 2.64 us
    ppermute x36 -> x34, waiting for transfers between devices: 104 us -> 62.5 us  [swap(): return lax.ppermute(x, axis, [(i, i ^ mask) for i in range(size)])]
    ppermute x36 -> x34, starting transfers between devices: 74.1 us -> 62.9 us  [swap(): return lax.ppermute(x, axis, [(i, i ^ mask) for i in range(size)])]
    unnamed x38 -> x14, local copies, waits for them, and re-layouts: 10.2 us -> 2.64 us
    pallas_call x9 -> x10, Pallas kernels: 21.4 us -> 20.4 us  [call(): pl.pallas_call(kernel, out_shape=tuple(outs), in_specs=[pl.BlockSpec(memo...]
  transfers between devices with their start and end apart: 36 -> 34, of which waited for: 10 -> 12; matrix products, arithmetic and copies ran while one was open for 0% -> 0% of each run, Pallas kernels for 5% -> 8%
where the time goes in v3:
time: 150 us; the launch traced here: 149 us
  starting transfers between devices  62.9 us (42%)
  waiting for transfers between devices  62.5 us (42%)
  Pallas kernels  20.4 us (14%)
  local copies, waits for them, and re-layouts  2.64 us (2%)
    ppermute x34, starting transfers between devices, swap(): return lax.ppermute(x, axis, [(i, i ^ mask) for i in range(size)])  62.9 us
    ppermute x34, waiting for transfers between devices, swap(): return lax.ppermute(x, axis, [(i, i ^ mask) for i in range(size)])  62.5 us
    pallas_call x10, Pallas kernels, call(): pl.pallas_call(kernel, out_shape=tuple(outs), in_specs=[pl.BlockSpec(memo...  20.4 us
  transfers between devices with their start and end apart: 34, of which 12 were waited for; matrix products, arithmetic and copies ran while one was open for 0% of the time, Pallas kernels for 8%

profile of v3, /device:TPU:0, one launch (start us, length us, event | category | flops | bytes accessed | tf_op | source)
XLA Modules:
  0.0 149.3 jit_solution(2149219186315722210)
XLA Ops:
  0.6 4.7 %pack_rows.1 = (bf16[256,128]{1,0:T(8,128)(2,1)}, bf16[576,2048]{1,0:T(8,128)(2,1)}, bf16[64,2048]{1,0:T(8,128)(2,1)}, bf16[64,2048]{1,0:T(8,128)(2,1)}, bf16[64...) custom-call(s32[1,128]{1,0:T(1,128)} %bitcast.13, ...), custom_call_target="tpu_custom_call" | custom-call | flops 268435456 | bytes 7930368 | tf_op jit(solution)/shard_map/pack_rows/pallas_call | solution.py:29
  5.4 3.0 %collective-permute-start.7 = (bf16[576,2048]{1,0:T(8,128)(2,1)}, bf16[576,2048]{1,0:T(8,128)(2,1)S(1)}, u32[]{:S(2)}, u32[]{:S(2)}) collective-permute-start(bf16[576,2048]{1,0:T(8,128)(2,1)} %get-tuple-element.88.refs_8_), channel_id=1, source_target_pairs={{0,2},{1,3},{2,0},{3,1},{4,6},{5,7},{6,4},{7,5},{8,10},{9,11},{10,... | collective-permute-start | bytes 7077896 | tf_op jit(solution)/shard_map/ppermute | solution.py:255
  8.4 2.6 %collective-permute-start = (bf16[64,2048]{1,0:T(8,128)(2,1)}, bf16[64,2048]{1,0:T(8,128)(2,1)S(1)}, u32[]{:S(2)}, u32[]{:S(2)}) collective-permute-start(bf16[64,2048]{1,0:T(8,128)(2,1)} %get-tuple-element.71), channel_id=1, source_target_pairs={{0,16},{4,20},{8,24},{12,28},{16,0},{20,4},{24,8},{28,12},{1,17},{... | collective-permute-start | bytes 786440 | tf_op jit(solution)/shard_map/ppermute | solution.py:255
  14.1 9.9 %collective-permute-done.refs_1_ = bf16[64,2048]{1,0:T(8,128)(2,1)S(1)} collective-permute-done((bf16[64,2048]{1,0:T(8,128)(2,1)}, bf16[64,2048]{1,0:T(8,128)(2,1)S(1)}, u32[]{:S(2)}, u32[]{:S(2)}) %collective-permute-start) | collective-permute-done | bytes 262176 | tf_op jit(solution)/shard_map/ppermute | solution.py:255
  23.9 1.6 %collective-permute-start.3 = (bf16[64,2048]{1,0:T(8,128)(2,1)}, bf16[64,2048]{1,0:T(8,128)(2,1)S(1)}, u32[]{:S(2)}, u32[]{:S(2)}) collective-permute-start(bf16[64,2048]{1,0:T(8,128)(2,1)} %get-tuple-element.74), channel_id=1, source_target_pairs={{0,12},{4,8},{8,4},{12,0},{16,28},{20,24},{24,20},{28,16},{1,13},{... | collective-permute-start | bytes 786440 | tf_op jit(solution)/shard_map/ppermute | solution.py:255
  25.6 3.3 %collective-permute-start.4 = (bf16[64,2048]{1,0:T(8,128)(2,1)}, bf16[64,2048]{1,0:T(8,128)(2,1)S(1)}, u32[]{:S(2)}, u32[]{:S(2)}) collective-permute-start(bf16[64,2048]{1,0:T(8,128)(2,1)} %get-tuple-element.75), channel_id=1, source_target_pairs={{0,20},{4,16},{8,28},{12,24},{16,4},{20,0},{24,12},{28,8},{1,21},{... | collective-permute-start | bytes 786440 | tf_op jit(solution)/shard_map/ppermute | solution.py:255
  29.2 8.5 %collective-permute-done.3.refs_4_ = bf16[64,2048]{1,0:T(8,128)(2,1)S(1)} collective-permute-done((bf16[64,2048]{1,0:T(8,128)(2,1)}, bf16[64,2048]{1,0:T(8,128)(2,1)S(1)}, u32[]{:S(2)}, u32[]{:S(2)}) %collective-permute-start.3) | collective-permute-done | bytes 262176 | tf_op jit(solution)/shard_map/ppermute | solution.py:255
  37.7 3.8 %collective-permute-start.6 = (bf16[64,2048]{1,0:T(8,128)(2,1)}, bf16[64,2048]{1,0:T(8,128)(2,1)S(1)}, u32[]{:S(2)}, u32[]{:S(2)}) collective-permute-start(bf16[64,2048]{1,0:T(8,128)(2,1)} %get-tuple-element.77), channel_id=1, source_target_pairs={{0,28},{4,24},{8,20},{12,16},{16,12},{20,8},{24,4},{28,0},{1,29},{... | collective-permute-start | bytes 786440 | tf_op jit(solution)/shard_map/ppermute | solution.py:255
  41.5 12.1 %collective-permute-done.4.refs_5_ = bf16[64,2048]{1,0:T(8,128)(2,1)S(1)} collective-permute-done((bf16[64,2048]{1,0:T(8,128)(2,1)}, bf16[64,2048]{1,0:T(8,128)(2,1)S(1)}, u32[]{:S(2)}, u32[]{:S(2)}) %collective-permute-start.4) | collective-permute-done | bytes 262176 | tf_op jit(solution)/shard_map/ppermute | solution.py:255
  53.6 6.2 %collective-permute-done.7.refs_8_ = bf16[576,2048]{1,0:T(8,128)(2,1)S(1)} collective-permute-done((bf16[576,2048]{1,0:T(8,128)(2,1)}, bf16[576,2048]{1,0:T(8,128)(2,1)S(1)}, u32[]{:S(2)}, u32[]{:S(2)}) %collective-permute-start.7) | collective-permute-done | bytes 2359328 | tf_op jit(solution)/shard_map/ppermute | solution.py:255
  60.8 1.7 %copy-done.6 = bf16[576,2048]{1,0:T(8,128)(2,1)S(1)} copy-done((bf16[576,2048]{1,0:T(8,128)(2,1)S(1)}, bf16[576,2048]{1,0:T(8,128)(2,1)}, u32[]{:S(2)}) %copy-start.6) | copy-done | bytes 2359320
  62.5 3.1 %near_units.1 = (bf16[192,2048]{1,0:T(8,128)(2,1)S(1)}, bf16[192,2048]{1,0:T(8,128)(2,1)S(1)}, f32[256,2048]{1,0:T(8,128)S(1)}) custom-call(bf16[64,2048]{1,0:T(8,128)(2,1)S(1)} %copy-done.3, bf16[64,2048]{1,0:T(8,128)(2,1)S(1)} %collective-permute-done.refs_1_, bf16[64,2048]{1,0:T(8,128)(2,1)S(1)} %collective-permute-done.1.refs_2_, ...), custom_call_target="tpu_custom_call" | custom-call | flops 2415919104 | bytes 10485760 | tf_op jit(solution)/shard_map/near_units/pallas_call | solution.py:29
  65.6 1.6 %far_units.1 = (bf16[192,2048]{1,0:T(8,128)(2,1)S(1)}, bf16[192,2048]{1,0:T(8,128)(2,1)S(1)}, f32[2,192,256]{2,1,0:T(8,128)S(1)}, f32[2,192,256]{2,1,0:T(8,128)S(1)}) custom-call(bf16[64,2048]{1,0:T(8,128)(2,1)S(1)} %copy-done.3, bf16[64,2048]{1,0:T(8,128)(2,1)S(1)} %collective-permute-done.refs_1_, bf16[64,2048]{1,0:T(8,128)(2,1)S(1)} %collective-permute-done.1.refs_2_, ...), custom_call_target="tpu_custom_call" | custom-call | flops 1207959552 | bytes 9175040 | tf_op jit(solution)/shard_map/far_units/pallas_call | solution.py:29
  67.8 1.9 %collective-permute-done.14.got_ref = bf16[192,2048]{1,0:T(8,128)(2,1)S(1)} collective-permute-done((bf16[192,2048]{1,0:T(8,128)(2,1)S(1)}, bf16[192,2048]{1,0:T(8,128)(2,1)S(1)}, u32[]{:S(2)}, u32[]{:S(2)}) %collective-permute-start.14) | collective-permute-done | bytes 786464 | tf_op jit(solution)/shard_map/ppermute | solution.py:255
  69.9 1.8 %collective-permute-start.15 = (bf16[192,2048]{1,0:T(8,128)(2,1)S(1)}, bf16[192,2048]{1,0:T(8,128)(2,1)S(1)}, u32[]{:S(2)}, u32[]{:S(2)}) collective-permute-start(bf16[192,2048]{1,0:T(8,128)(2,1)S(1)} %add_pair.1), channel_id=1, source_target_pairs={{0,2},{1,3},{2,0},{3,1},{4,6},{5,7},{6,4},{7,5},{8,10},{9,11},{10,... | collective-permute-start | bytes 2359304 | tf_op jit(solution)/shard_map/ppermute | solution.py:255
  71.8 2.1 %input_gradient.1 = (bf16[32,2048]{1,0:T(8,128)(2,1)S(1)}, bf16[32,2048]{1,0:T(8,128)(2,1)S(1)}, bf16[32,2048]{1,0:T(8,128)(2,1)S(1)}, bf16[32,2048]{1,0:T(8,128...) custom-call(bf16[64,2048]{1,0:T(8,128)(2,1)S(1)} %copy-done.3, ...), custom_call_target="tpu_custom_call" | custom-call | flops 1207959552 | bytes 10747904 | tf_op jit(solution)/shard_map/input_gradient/pallas_call | solution.py:29
  73.9 3.9 %collective-permute-start.10 = (bf16[32,2048]{1,0:T(8,128)(2,1)S(1)}, bf16[32,2048]{1,0:T(8,128)(2,1)S(1)}, u32[]{:S(2)}, u32[]{:S(2)}) collective-permute-start(bf16[32,2048]{1,0:T(8,128)(2,1)S(1)} %get-tuple-element.97), channel_id=1, source_target_pairs={{0,16},{4,20},{8,24},{12,28},{16,0},{20,4},{24,8},{28,12},{1,17},{... | collective-permute-start | bytes 393224 | tf_op jit(solution)/shard_map/ppermute | solution.py:255
  79.7 5.2 %collective-permute-done.10.refs_1_ = bf16[32,2048]{1,0:T(8,128)(2,1)S(1)} collective-permute-done((bf16[32,2048]{1,0:T(8,128)(2,1)S(1)}, bf16[32,2048]{1,0:T(8,128)(2,1)S(1)}, u32[]{:S(2)}, u32[]{:S(2)}) %collective-permute-start.10) | collective-permute-done | bytes 131104 | tf_op jit(solution)/shard_map/ppermute | solution.py:255
  85.8 5.1 %collective-permute-done.13.refs_4_ = bf16[32,2048]{1,0:T(8,128)(2,1)S(1)} collective-permute-done((bf16[32,2048]{1,0:T(8,128)(2,1)S(1)}, bf16[32,2048]{1,0:T(8,128)(2,1)S(1)}, u32[]{:S(2)}, u32[]{:S(2)}) %collective-permute-start.13) | collective-permute-done | bytes 131104 | tf_op jit(solution)/shard_map/ppermute | solution.py:255
  91.5 4.0 %collective-permute-start.20 = (bf16[24,2048]{1,0:T(8,128)(2,1)S(1)}, bf16[24,2048]{1,0:T(8,128)(2,1)S(1)}, u32[]{:S(2)}, u32[]{:S(2)}) collective-permute-start(bf16[24,2048]{1,0:T(8,128)(2,1)S(1)} %get-tuple-element.115), channel_id=1, source_target_pairs={{0,16},{4,20},{8,24},{12,28},{16,0},{20,4},{24,8},{28,12},{1,17},{... | collective-permute-start | bytes 294920 | tf_op jit(solution)/shard_map/ppermute | solution.py:255
  96.9 2.0 %collective-permute-start.23 = (bf16[24,2048]{1,0:T(8,128)(2,1)S(1)}, bf16[24,2048]{1,0:T(8,128)(2,1)S(1)}, u32[]{:S(2)}, u32[]{:S(2)}) collective-permute-start(bf16[24,2048]{1,0:T(8,128)(2,1)S(1)} %get-tuple-element.118), channel_id=1, source_target_pairs={{0,12},{4,8},{8,4},{12,0},{16,28},{20,24},{24,20},{28,16},{1,13},{... | collective-permute-start | bytes 294920 | tf_op jit(solution)/shard_map/ppermute | solution.py:255
  100.0 2.3 %collective-permute-start.25 = (bf16[24,2048]{1,0:T(8,128)(2,1)S(1)}, bf16[24,2048]{1,0:T(8,128)(2,1)S(1)}, u32[]{:S(2)}, u32[]{:S(2)}) collective-permute-start(bf16[24,2048]{1,0:T(8,128)(2,1)S(1)} %get-tuple-element.120), channel_id=1, source_target_pairs={{0,24},{4,28},{8,16},{12,20},{16,8},{20,12},{24,0},{28,4},{1,25},{... | collective-permute-start | bytes 294920 | tf_op jit(solution)/shard_map/ppermute | solution.py:255
  102.2 2.2 %collective-permute-start.26 = (bf16[24,2048]{1,0:T(8,128)(2,1)S(1)}, bf16[24,2048]{1,0:T(8,128)(2,1)S(1)}, u32[]{:S(2)}, u32[]{:S(2)}) collective-permute-start(bf16[24,2048]{1,0:T(8,128)(2,1)S(1)} %get-tuple-element.121), channel_id=1, source_target_pairs={{0,28},{4,24},{8,20},{12,16},{16,12},{20,8},{24,4},{28,0},{1,29},{... | collective-permute-start | bytes 294920 | tf_op jit(solution)/shard_map/ppermute | solution.py:255
  107.2 11.9 %collective-permute-done.24.refs_5_ = bf16[24,2048]{1,0:T(8,128)(2,1)S(1)} collective-permute-done((bf16[24,2048]{1,0:T(8,128)(2,1)S(1)}, bf16[24,2048]{1,0:T(8,128)(2,1)S(1)}, u32[]{:S(2)}, u32[]{:S(2)}) %collective-permute-start.24) | collective-permute-done | bytes 98336 | tf_op jit(solution)/shard_map/ppermute | solution.py:255
  119.1 2.5 %collective-permute-start.18 = (bf16[32,2048]{1,0:T(8,128)(2,1)S(1)}, bf16[32,2048]{1,0:T(8,128)(2,1)S(1)}, u32[]{:S(2)}, u32[]{:S(2)}) collective-permute-start(bf16[32,2048]{1,0:T(8,128)(2,1)S(1)} %get-tuple-element.110), channel_id=1, source_target_pairs={{0,28},{4,24},{8,20},{12,16},{16,12},{20,8},{24,4},{28,0},{1,29},{... | collective-permute-start | bytes 393224 | tf_op jit(solution)/shard_map/ppermute | solution.py:255
  121.7 2.4 %new_rows.1 = (bf16[24,2048]{1,0:T(8,128)(2,1)S(1)}, bf16[24,2048]{1,0:T(8,128)(2,1)S(1)}, bf16[24,2048]{1,0:T(8,128)(2,1)S(1)}, bf16[24,2048]{1,0:T(8,128)(2,1)...) custom-call(s32[8]{0:T(128)S(1)} %copy-done.5, ...), custom_call_target="tpu_custom_call" | custom-call | bytes 5111840 | tf_op jit(solution)/shard_map/new_rows/pallas_call | solution.py:29
  124.1 2.9 %collective-permute-start.27 = (bf16[24,2048]{1,0:T(8,128)(2,1)S(1)}, bf16[24,2048]{1,0:T(8,128)(2,1)S(1)}, u32[]{:S(2)}, u32[]{:S(2)}) collective-permute-start(bf16[24,2048]{1,0:T(8,128)(2,1)S(1)} %get-tuple-element.126), channel_id=1, source_target_pairs={{0,16},{4,20},{8,24},{12,28},{16,0},{20,4},{24,8},{28,12},{1,17},{... | collective-permute-start | bytes 294920 | tf_op jit(solution)/shard_map/ppermute | solution.py:255
  128.6 4.4 %collective-permute-start.30 = (bf16[24,2048]{1,0:T(8,128)(2,1)S(1)}, bf16[24,2048]{1,0:T(8,128)(2,1)S(1)}, u32[]{:S(2)}, u32[]{:S(2)}) collective-permute-start(bf16[24,2048]{1,0:T(8,128)(2,1)S(1)} %get-tuple-element.129), channel_id=1, source_target_pairs={{0,12},{4,8},{8,4},{12,0},{16,28},{20,24},{24,20},{28,16},{1,13},{... | collective-permute-start | bytes 294920 | tf_op jit(solution)/shard_map/ppermute | solution.py:255
  133.0 4.9 %collective-permute-start.31 = (bf16[24,2048]{1,0:T(8,128)(2,1)S(1)}, bf16[24,2048]{1,0:T(8,128)(2,1)S(1)}, u32[]{:S(2)}, u32[]{:S(2)}) collective-permute-start(bf16[24,2048]{1,0:T(8,128)(2,1)S(1)} %get-tuple-element.130), channel_id=1, source_target_pairs={{0,20},{4,16},{8,28},{12,24},{16,4},{20,0},{24,12},{28,8},{1,21},{... | collective-permute-start | bytes 294920 | tf_op jit(solution)/shard_map/ppermute | solution.py:255
  138.2 2.9 %collective-permute-start.32 = (bf16[24,2048]{1,0:T(8,128)(2,1)S(1)}, bf16[24,2048]{1,0:T(8,128)(2,1)S(1)}, u32[]{:S(2)}, u32[]{:S(2)}) collective-permute-start(bf16[24,2048]{1,0:T(8,128)(2,1)S(1)} %get-tuple-element.131), channel_id=1, source_target_pairs={{0,24},{4,28},{8,16},{12,20},{16,8},{20,12},{24,0},{28,4},{1,25},{... | collective-permute-start | bytes 294920 | tf_op jit(solution)/shard_map/ppermute | solution.py:255
  141.1 2.3 %collective-permute-start.33 = (bf16[24,2048]{1,0:T(8,128)(2,1)S(1)}, bf16[24,2048]{1,0:T(8,128)(2,1)S(1)}, u32[]{:S(2)}, u32[]{:S(2)}) collective-permute-start(bf16[24,2048]{1,0:T(8,128)(2,1)S(1)} %get-tuple-element.132), channel_id=1, source_target_pairs={{0,28},{4,24},{8,20},{12,16},{16,12},{20,8},{24,4},{28,0},{1,29},{... | collective-permute-start | bytes 294920 | tf_op jit(solution)/shard_map/ppermute | solution.py:255
  144.5 3.6 %new_state.1 = (f32[6,24,2048]{2,1,0:T(8,128)}, f32[6,24,2048]{2,1,0:T(8,128)}, f32[6,24,2048]{2,1,0:T(8,128)}) custom-call(s32[8]{0:T(128)S(1)} %copy-done.5, bf16[24,2048]{1,0:T(8,128)(2,1)S(1)} %get-tuple-element.114.refs_0_, bf16[24,2048]{1,0:T(8,128)(2,1)S(1)} %collective-permute-done.20.refs_1_, bf16[24,2048]{1,0:T(8,128)(2,1)S(1)} %collective-permute-done.21.refs_2_, ...), custom_call_target="tpu_custom_call" | custom-call | bytes 7864352 | tf_op jit(solution)/shard_map/new_state/pallas_call | solution.py:29
  (60 shorter events, 18.1 us)
Async XLA Ops:
  5.4 54.5 %collective-permute-start.7 = (bf16[576,2048]{1,0:T(8,128)(2,1)}, bf16[576,2048]{1,0:T(8,128)(2,1)S(1)}, u32[]{:S(2)}, u32[]{:S(2)}) collective-permute-start(bf16[576,2048]{1,0:T(8,128)(2,1)} %get-tuple-element.88.refs_8_), channel_id=1, source_target_pairs={{0,2},{1,3},{2,0},{3,1},{4,6},{5,7},{6,4},{7,5},{8,10},{9,11},{10,... | collective-permute-start | bytes 7077896 | tf_op jit(solution)/shard_map/ppermute | solution.py:255
  8.4 51.5 %collective-permute-start.8 = (bf16[576,2048]{1,0:T(8,128)(2,1)}, bf16[576,2048]{1,0:T(8,128)(2,1)S(1)}, u32[]{:S(2)}, u32[]{:S(2)}) collective-permute-start(bf16[576,2048]{1,0:T(8,128)(2,1)} %get-tuple-element.88.refs_8_), channel_id=1, source_target_pairs={{0,1},{1,0},{2,3},{3,2},{4,5},{5,4},{6,7},{7,6},{8,9},{9,8},{10,11... | collective-permute-start | bytes 7077896 | tf_op jit(solution)/shard_map/ppermute | solution.py:255
  8.4 15.6 %collective-permute-start = (bf16[64,2048]{1,0:T(8,128)(2,1)}, bf16[64,2048]{1,0:T(8,128)(2,1)S(1)}, u32[]{:S(2)}, u32[]{:S(2)}) collective-permute-start(bf16[64,2048]{1,0:T(8,128)(2,1)} %get-tuple-element.71), channel_id=1, source_target_pairs={{0,16},{4,20},{8,24},{12,28},{16,0},{20,4},{24,8},{28,12},{1,17},{... | collective-permute-start | bytes 786440 | tf_op jit(solution)/shard_map/ppermute | solution.py:255
  11.0 14.6 %collective-permute-start.1 = (bf16[64,2048]{1,0:T(8,128)(2,1)}, bf16[64,2048]{1,0:T(8,128)(2,1)S(1)}, u32[]{:S(2)}, u32[]{:S(2)}) collective-permute-start(bf16[64,2048]{1,0:T(8,128)(2,1)} %get-tuple-element.72), channel_id=1, source_target_pairs={{0,4},{4,0},{8,12},{12,8},{16,20},{20,16},{24,28},{28,24},{1,5},{5... | collective-permute-start | bytes 786440 | tf_op jit(solution)/shard_map/ppermute | solution.py:255
  12.5 16.4 %collective-permute-start.2 = (bf16[64,2048]{1,0:T(8,128)(2,1)}, bf16[64,2048]{1,0:T(8,128)(2,1)S(1)}, u32[]{:S(2)}, u32[]{:S(2)}) collective-permute-start(bf16[64,2048]{1,0:T(8,128)(2,1)} %get-tuple-element.73), channel_id=1, source_target_pairs={{0,8},{4,12},{8,0},{12,4},{16,24},{20,28},{24,16},{28,20},{1,9},{5... | collective-permute-start | bytes 786440 | tf_op jit(solution)/shard_map/ppermute | solution.py:255
  23.9 13.8 %collective-permute-start.3 = (bf16[64,2048]{1,0:T(8,128)(2,1)}, bf16[64,2048]{1,0:T(8,128)(2,1)S(1)}, u32[]{:S(2)}, u32[]{:S(2)}) collective-permute-start(bf16[64,2048]{1,0:T(8,128)(2,1)} %get-tuple-element.74), channel_id=1, source_target_pairs={{0,12},{4,8},{8,4},{12,0},{16,28},{20,24},{24,20},{28,16},{1,13},{... | collective-permute-start | bytes 786440 | tf_op jit(solution)/shard_map/ppermute | solution.py:255
  25.6 28.1 %collective-permute-start.4 = (bf16[64,2048]{1,0:T(8,128)(2,1)}, bf16[64,2048]{1,0:T(8,128)(2,1)S(1)}, u32[]{:S(2)}, u32[]{:S(2)}) collective-permute-start(bf16[64,2048]{1,0:T(8,128)(2,1)} %get-tuple-element.75), channel_id=1, source_target_pairs={{0,20},{4,16},{8,28},{12,24},{16,4},{20,0},{24,12},{28,8},{1,21},{... | collective-permute-start | bytes 786440 | tf_op jit(solution)/shard_map/ppermute | solution.py:255
  28.9 24.7 %collective-permute-start.5 = (bf16[64,2048]{1,0:T(8,128)(2,1)}, bf16[64,2048]{1,0:T(8,128)(2,1)S(1)}, u32[]{:S(2)}, u32[]{:S(2)}) collective-permute-start(bf16[64,2048]{1,0:T(8,128)(2,1)} %get-tuple-element.76), channel_id=1, source_target_pairs={{0,24},{4,28},{8,16},{12,20},{16,8},{20,12},{24,0},{28,4},{1,25},{... | collective-permute-start | bytes 786440 | tf_op jit(solution)/shard_map/ppermute | solution.py:255
  37.7 15.9 %collective-permute-start.6 = (bf16[64,2048]{1,0:T(8,128)(2,1)}, bf16[64,2048]{1,0:T(8,128)(2,1)S(1)}, u32[]{:S(2)}, u32[]{:S(2)}) collective-permute-start(bf16[64,2048]{1,0:T(8,128)(2,1)} %get-tuple-element.77), channel_id=1, source_target_pairs={{0,28},{4,24},{8,20},{12,16},{16,12},{20,8},{24,4},{28,0},{1,29},{... | collective-permute-start | bytes 786440 | tf_op jit(solution)/shard_map/ppermute | solution.py:255
  69.9 21.0 %collective-permute-start.15 = (bf16[192,2048]{1,0:T(8,128)(2,1)S(1)}, bf16[192,2048]{1,0:T(8,128)(2,1)S(1)}, u32[]{:S(2)}, u32[]{:S(2)}) collective-permute-start(bf16[192,2048]{1,0:T(8,128)(2,1)S(1)} %add_pair.1), channel_id=1, source_target_pairs={{0,2},{1,3},{2,0},{3,1},{4,6},{5,7},{6,4},{7,5},{8,10},{9,11},{10,... | collective-permute-start | bytes 2359304 | tf_op jit(solution)/shard_map/ppermute | solution.py:255
  71.7 19.2 %collective-permute-start.19 = (bf16[192,2048]{1,0:T(8,128)(2,1)S(1)}, bf16[192,2048]{1,0:T(8,128)(2,1)S(1)}, u32[]{:S(2)}, u32[]{:S(2)}) collective-permute-start(bf16[192,2048]{1,0:T(8,128)(2,1)S(1)} %get-tuple-element.112), channel_id=1, source_target_pairs={{0,1},{1,0},{2,3},{3,2},{4,5},{5,4},{6,7},{7,6},{8,9},{9,8},{10,11... | collective-permute-start | bytes 2359304 | tf_op jit(solution)/shard_map/ppermute | solution.py:255
  73.9 10.9 %collective-permute-start.10 = (bf16[32,2048]{1,0:T(8,128)(2,1)S(1)}, bf16[32,2048]{1,0:T(8,128)(2,1)S(1)}, u32[]{:S(2)}, u32[]{:S(2)}) collective-permute-start(bf16[32,2048]{1,0:T(8,128)(2,1)S(1)} %get-tuple-element.97), channel_id=1, source_target_pairs={{0,16},{4,20},{8,24},{12,28},{16,0},{20,4},{24,8},{28,12},{1,17},{... | collective-permute-start | bytes 393224 | tf_op jit(solution)/shard_map/ppermute | solution.py:255
  77.8 7.4 %collective-permute-start.11 = (bf16[32,2048]{1,0:T(8,128)(2,1)S(1)}, bf16[32,2048]{1,0:T(8,128)(2,1)S(1)}, u32[]{:S(2)}, u32[]{:S(2)}) collective-permute-start(bf16[32,2048]{1,0:T(8,128)(2,1)S(1)} %get-tuple-element.98), channel_id=1, source_target_pairs={{0,4},{4,0},{8,12},{12,8},{16,20},{20,16},{24,28},{28,24},{1,5},{5... | collective-permute-start | bytes 393224 | tf_op jit(solution)/shard_map/ppermute | solution.py:255
  79.3 6.5 %collective-permute-start.12 = (bf16[32,2048]{1,0:T(8,128)(2,1)S(1)}, bf16[32,2048]{1,0:T(8,128)(2,1)S(1)}, u32[]{:S(2)}, u32[]{:S(2)}) collective-permute-start(bf16[32,2048]{1,0:T(8,128)(2,1)S(1)} %get-tuple-element.99), channel_id=1, source_target_pairs={{0,8},{4,12},{8,0},{12,4},{16,24},{20,28},{24,16},{28,20},{1,9},{5... | collective-permute-start | bytes 393224 | tf_op jit(solution)/shard_map/ppermute | solution.py:255
  84.8 6.0 %collective-permute-start.13 = (bf16[32,2048]{1,0:T(8,128)(2,1)S(1)}, bf16[32,2048]{1,0:T(8,128)(2,1)S(1)}, u32[]{:S(2)}, u32[]{:S(2)}) collective-permute-start(bf16[32,2048]{1,0:T(8,128)(2,1)S(1)} %get-tuple-element.100), channel_id=1, source_target_pairs={{0,12},{4,8},{8,4},{12,0},{16,28},{20,24},{24,20},{28,16},{1,13},{... | collective-permute-start | bytes 393224 | tf_op jit(solution)/shard_map/ppermute | solution.py:255
  91.5 8.5 %collective-permute-start.20 = (bf16[24,2048]{1,0:T(8,128)(2,1)S(1)}, bf16[24,2048]{1,0:T(8,128)(2,1)S(1)}, u32[]{:S(2)}, u32[]{:S(2)}) collective-permute-start(bf16[24,2048]{1,0:T(8,128)(2,1)S(1)} %get-tuple-element.115), channel_id=1, source_target_pairs={{0,16},{4,20},{8,24},{12,28},{16,0},{20,4},{24,8},{28,12},{1,17},{... | collective-permute-start | bytes 294920 | tf_op jit(solution)/shard_map/ppermute | solution.py:255
  95.5 6.8 %collective-permute-start.21 = (bf16[24,2048]{1,0:T(8,128)(2,1)S(1)}, bf16[24,2048]{1,0:T(8,128)(2,1)S(1)}, u32[]{:S(2)}, u32[]{:S(2)}) collective-permute-start(bf16[24,2048]{1,0:T(8,128)(2,1)S(1)} %get-tuple-element.116), channel_id=1, source_target_pairs={{0,4},{4,0},{8,12},{12,8},{16,20},{20,16},{24,28},{28,24},{1,5},{5... | collective-permute-start | bytes 294920 | tf_op jit(solution)/shard_map/ppermute | solution.py:255
  96.9 7.5 %collective-permute-start.22 = (bf16[24,2048]{1,0:T(8,128)(2,1)S(1)}, bf16[24,2048]{1,0:T(8,128)(2,1)S(1)}, u32[]{:S(2)}, u32[]{:S(2)}) collective-permute-start(bf16[24,2048]{1,0:T(8,128)(2,1)S(1)} %get-tuple-element.117), channel_id=1, source_target_pairs={{0,8},{4,12},{8,0},{12,4},{16,24},{20,28},{24,16},{28,20},{1,9},{5... | collective-permute-start | bytes 294920 | tf_op jit(solution)/shard_map/ppermute | solution.py:255
  96.9 8.8 %collective-permute-start.23 = (bf16[24,2048]{1,0:T(8,128)(2,1)S(1)}, bf16[24,2048]{1,0:T(8,128)(2,1)S(1)}, u32[]{:S(2)}, u32[]{:S(2)}) collective-permute-start(bf16[24,2048]{1,0:T(8,128)(2,1)S(1)} %get-tuple-element.118), channel_id=1, source_target_pairs={{0,12},{4,8},{8,4},{12,0},{16,28},{20,24},{24,20},{28,16},{1,13},{... | collective-permute-start | bytes 294920 | tf_op jit(solution)/shard_map/ppermute | solution.py:255
  99.0 20.2 %collective-permute-start.24 = (bf16[24,2048]{1,0:T(8,128)(2,1)S(1)}, bf16[24,2048]{1,0:T(8,128)(2,1)S(1)}, u32[]{:S(2)}, u32[]{:S(2)}) collective-permute-start(bf16[24,2048]{1,0:T(8,128)(2,1)S(1)} %get-tuple-element.119), channel_id=1, source_target_pairs={{0,20},{4,16},{8,28},{12,24},{16,4},{20,0},{24,12},{28,8},{1,21},{... | collective-permute-start | bytes 294920 | tf_op jit(solution)/shard_map/ppermute | solution.py:255
  100.0 21.7 %collective-permute-start.25 = (bf16[24,2048]{1,0:T(8,128)(2,1)S(1)}, bf16[24,2048]{1,0:T(8,128)(2,1)S(1)}, u32[]{:S(2)}, u32[]{:S(2)}) collective-permute-start(bf16[24,2048]{1,0:T(8,128)(2,1)S(1)} %get-tuple-element.120), channel_id=1, source_target_pairs={{0,24},{4,28},{8,16},{12,20},{16,8},{20,12},{24,0},{28,4},{1,25},{... | collective-permute-start | bytes 294920 | tf_op jit(solution)/shard_map/ppermute | solution.py:255
  102.2 19.4 %collective-permute-start.26 = (bf16[24,2048]{1,0:T(8,128)(2,1)S(1)}, bf16[24,2048]{1,0:T(8,128)(2,1)S(1)}, u32[]{:S(2)}, u32[]{:S(2)}) collective-permute-start(bf16[24,2048]{1,0:T(8,128)(2,1)S(1)} %get-tuple-element.121), channel_id=1, source_target_pairs={{0,28},{4,24},{8,20},{12,16},{16,12},{20,8},{24,4},{28,0},{1,29},{... | collective-permute-start | bytes 294920 | tf_op jit(solution)/shard_map/ppermute | solution.py:255
  104.5 24.2 %collective-permute-start.16 = (bf16[32,2048]{1,0:T(8,128)(2,1)S(1)}, bf16[32,2048]{1,0:T(8,128)(2,1)S(1)}, u32[]{:S(2)}, u32[]{:S(2)}) collective-permute-start(bf16[32,2048]{1,0:T(8,128)(2,1)S(1)} %get-tuple-element.108), channel_id=1, source_target_pairs={{0,20},{4,16},{8,28},{12,24},{16,4},{20,0},{24,12},{28,8},{1,21},{... | collective-permute-start | bytes 393224 | tf_op jit(solution)/shard_map/ppermute | solution.py:255
  105.7 22.9 %collective-permute-start.17 = (bf16[32,2048]{1,0:T(8,128)(2,1)S(1)}, bf16[32,2048]{1,0:T(8,128)(2,1)S(1)}, u32[]{:S(2)}, u32[]{:S(2)}) collective-permute-start(bf16[32,2048]{1,0:T(8,128)(2,1)S(1)} %get-tuple-element.109), channel_id=1, source_target_pairs={{0,24},{4,28},{8,16},{12,20},{16,8},{20,12},{24,0},{28,4},{1,25},{... | collective-permute-start | bytes 393224 | tf_op jit(solution)/shard_map/ppermute | solution.py:255
  119.1 13.9 %collective-permute-start.18 = (bf16[32,2048]{1,0:T(8,128)(2,1)S(1)}, bf16[32,2048]{1,0:T(8,128)(2,1)S(1)}, u32[]{:S(2)}, u32[]{:S(2)}) collective-permute-start(bf16[32,2048]{1,0:T(8,128)(2,1)S(1)} %get-tuple-element.110), channel_id=1, source_target_pairs={{0,28},{4,24},{8,20},{12,16},{16,12},{20,8},{24,4},{28,0},{1,29},{... | collective-permute-start | bytes 393224 | tf_op jit(solution)/shard_map/ppermute | solution.py:255
  124.1 14.1 %collective-permute-start.27 = (bf16[24,2048]{1,0:T(8,128)(2,1)S(1)}, bf16[24,2048]{1,0:T(8,128)(2,1)S(1)}, u32[]{:S(2)}, u32[]{:S(2)}) collective-permute-start(bf16[24,2048]{1,0:T(8,128)(2,1)S(1)} %get-tuple-element.126), channel_id=1, source_target_pairs={{0,16},{4,20},{8,24},{12,28},{16,0},{20,4},{24,8},{28,12},{1,17},{... | collective-permute-start | bytes 294920 | tf_op jit(solution)/shard_map/ppermute | solution.py:255
  127.0 14.1 %collective-permute-start.28 = (bf16[24,2048]{1,0:T(8,128)(2,1)S(1)}, bf16[24,2048]{1,0:T(8,128)(2,1)S(1)}, u32[]{:S(2)}, u32[]{:S(2)}) collective-permute-start(bf16[24,2048]{1,0:T(8,128)(2,1)S(1)} %get-tuple-element.127), channel_id=1, source_target_pairs={{0,4},{4,0},{8,12},{12,8},{16,20},{20,16},{24,28},{28,24},{1,5},{5... | collective-permute-start | bytes 294920 | tf_op jit(solution)/shard_map/ppermute | solution.py:255
  128.6 19.5 %collective-permute-start.29 = (bf16[24,2048]{1,0:T(8,128)(2,1)S(1)}, bf16[24,2048]{1,0:T(8,128)(2,1)S(1)}, u32[]{:S(2)}, u32[]{:S(2)}) collective-permute-start(bf16[24,2048]{1,0:T(8,128)(2,1)S(1)} %get-tuple-element.128), channel_id=1, source_target_pairs={{0,8},{4,12},{8,0},{12,4},{16,24},{20,28},{24,16},{28,20},{1,9},{5... | collective-permute-start | bytes 294920 | tf_op jit(solution)/shard_map/ppermute | solution.py:255
  128.6 19.5 %collective-permute-start.30 = (bf16[24,2048]{1,0:T(8,128)(2,1)S(1)}, bf16[24,2048]{1,0:T(8,128)(2,1)S(1)}, u32[]{:S(2)}, u32[]{:S(2)}) collective-permute-start(bf16[24,2048]{1,0:T(8,128)(2,1)S(1)} %get-tuple-element.129), channel_id=1, source_target_pairs={{0,12},{4,8},{8,4},{12,0},{16,28},{20,24},{24,20},{28,16},{1,13},{... | collective-permute-start | bytes 294920 | tf_op jit(solution)/shard_map/ppermute | solution.py:255
  133.0 15.0 %collective-permute-start.31 = (bf16[24,2048]{1,0:T(8,128)(2,1)S(1)}, bf16[24,2048]{1,0:T(8,128)(2,1)S(1)}, u32[]{:S(2)}, u32[]{:S(2)}) collective-permute-start(bf16[24,2048]{1,0:T(8,128)(2,1)S(1)} %get-tuple-element.130), channel_id=1, source_target_pairs={{0,20},{4,16},{8,28},{12,24},{16,4},{20,0},{24,12},{28,8},{1,21},{... | collective-permute-start | bytes 294920 | tf_op jit(solution)/shard_map/ppermute | solution.py:255
  138.2 9.9 %collective-permute-start.32 = (bf16[24,2048]{1,0:T(8,128)(2,1)S(1)}, bf16[24,2048]{1,0:T(8,128)(2,1)S(1)}, u32[]{:S(2)}, u32[]{:S(2)}) collective-permute-start(bf16[24,2048]{1,0:T(8,128)(2,1)S(1)} %get-tuple-element.131), channel_id=1, source_target_pairs={{0,24},{4,28},{8,16},{12,20},{16,8},{20,12},{24,0},{28,4},{1,25},{... | collective-permute-start | bytes 294920 | tf_op jit(solution)/shard_map/ppermute | solution.py:255
  141.1 7.3 %collective-permute-start.33 = (bf16[24,2048]{1,0:T(8,128)(2,1)S(1)}, bf16[24,2048]{1,0:T(8,128)(2,1)S(1)}, u32[]{:S(2)}, u32[]{:S(2)}) collective-permute-start(bf16[24,2048]{1,0:T(8,128)(2,1)S(1)} %get-tuple-element.132), channel_id=1, source_target_pairs={{0,28},{4,24},{8,20},{12,16},{16,12},{20,8},{24,4},{28,0},{1,29},{... | collective-permute-start | bytes 294920 | tf_op jit(solution)/shard_map/ppermute | solution.py:255
  (9 other events, 174.5 us)

commit v4 on v3

--- a/solution.py
+++ b/solution.py
@@ -13,16 +13,14 @@
 TN = (((0,), (0,)), ((), ()))
 NN = (((1,), (0,)), ((), ()))
 COLUMNS = 512
-EARLY = 5
+EARLY = 4
 
 
 def dot(a, b, dims):
     return lax.dot_general(a, b, dims, preferred_element_type=F32)
 
 
-def call(
-    kernel, outs, args, scratch=(), smem=(), far=(), far_out=(), name=None, mib=40, flops=0
-):
+def call(kernel, outs, args, scratch=(), smem=(), far=(), name=None, mib=40, flops=0):
     moved = sum(a.size * a.dtype.itemsize for a in args) + sum(
         o.size * o.dtype.itemsize for o in outs
     )
@@ -35,10 +33,7 @@
             )
             for i in range(len(args))
         ],
-        out_specs=tuple(
-            pl.BlockSpec(memory_space=pl.ANY if i in far_out else pltpu.VMEM)
-            for i in range(len(outs))
-        ),
+        out_specs=tuple(pl.BlockSpec(memory_space=pltpu.VMEM) for _ in outs),
         scratch_shapes=list(scratch),
         compiler_params=pltpu.CompilerParams(vmem_limit_bytes=mib * 2**20),
         cost_estimate=pl.CostEstimate(flops=flops, bytes_accessed=moved, transcendentals=0),
@@ -51,15 +46,7 @@
     return [slice(c, c + step) for c in range(0, width, step)]
 
 
-def pack_kernel(n, capacity, joint, r_ref, x_ref, g_ref, *refs):
-    weights, place_ref, joined_ref, outs = refs[:3], refs[3], refs[4], refs[5:-3]
-    x_held, g_held, sem = refs[-3:]
-    part = weights[0].shape[0]
-    pairs = [(x_ref, x_held), (g_ref, g_held)]
-    pairs += [(w, joined_ref.at[i * part : (i + 1) * part]) for i, w in enumerate(weights)]
-    copies = [pltpu.make_async_copy(src, dst, sem.at[i]) for i, (src, dst) in enumerate(pairs)]
-    for copy in copies:
-        copy.start()
+def pack_kernel(n, capacity, joint, r_ref, x_ref, g_ref, place_ref, *outs):
     e = lax.axis_index("expert")
     owned, width = x_ref.shape
     rel = r_ref[...] ^ e
@@ -73,10 +60,9 @@
     spot = lax.broadcasted_iota(jnp.int32, (n * capacity, owned), 0)
     place = (pos.astype(jnp.int32) == spot).astype(BF16)
     place_ref[...] = place
-    for half, held in enumerate((x_held, g_held)):
-        copies[half].wait()
+    for half, ref in enumerate((x_ref, g_ref)):
         for cols in columns(width):
-            packed = dot(place, held[:, cols], NN).astype(BF16)
+            packed = dot(place, ref[:, cols], NN).astype(BF16)
             if joint:
                 for d in range(n):
                     outs[d][half * capacity : (half + 1) * capacity, cols] = packed[
@@ -84,8 +70,6 @@
                     ]
             else:
                 outs[half][:, cols] = packed
-    for copy in copies[2:]:
-        copy.wait()
 
 
 def halves(blocks, half):
@@ -94,6 +78,18 @@
         rows = ref.shape[0] // 2
         parts.append(ref[half * rows : (half + 1) * rows])
     return parts[0] if len(parts) == 1 else jnp.concatenate(parts, axis=0)
+
+
+def join_kernel(*refs):
+    parts, out_ref, sem = refs[:-2], refs[-2], refs[-1]
+    start, copies = 0, []
+    for i, ref in enumerate(parts):
+        rows = ref.shape[0]
+        copies.append(pltpu.make_async_copy(ref, out_ref.at[start : start + rows], sem.at[i]))
+        copies[i].start()
+        start += rows
+    for copy in copies:
+        copy.wait()
 
 
 def forward(weight, x):
@@ -259,11 +255,13 @@
     return [0, n // 2, *(d for d in range(1, n) if d != n // 2)]
 
 
-def exchange(blocks):
-    return [
-        swap(block, "expert", d) if d else block
-        for d, block in zip(order(len(blocks)), blocks, strict=True)
-    ]
+def crossing(n):
+    long, short = list(range(n // 2, n)), list(range(1, n // 2))
+    return [0, *long[: EARLY - 1], *short[:1], *long[EARLY - 1 :], *short[1:]]
+
+
+def exchange(blocks, ways):
+    return [swap(blocks[d], "expert", d) if d else blocks[d] for d in ways]
 
 
 def exchange_whole(x):
@@ -287,42 +285,46 @@
     shape = jax.ShapeDtypeStruct
 
     weights = [jnp.swapaxes(w, 1, 2)[0] for w in (gate_weight, up_weight)] + [down_weight[0]]
-    outs = [shape((rows, owned), BF16), shape((3 * part, width), BF16)]
+    (joined,) = call(
+        join_kernel,
+        [shape((3 * part, width), BF16)],
+        weights,
+        scratch=[pltpu.SemaphoreType.DMA((3,))],
+        far=range(3),
+        name="join_weights",
+        mib=16,
+    )
+    outs = [shape((rows, owned), BF16)]
     outs += [shape((2 * capacity, width), BF16)] * n if few else [shape((rows, width), BF16)] * 2
-    place, joined, *packed = call(
+    place, *packed = call(
         functools.partial(pack_kernel, n, capacity, few),
         outs,
-        (routing.reshape(1, owned), tokens, out_grad, *weights),
-        scratch=[
-            pltpu.VMEM((owned, width), BF16),
-            pltpu.VMEM((owned, width), BF16),
-            pltpu.SemaphoreType.DMA((5,)),
-        ],
-        far=range(1, 6),
+        (routing.reshape(1, owned), tokens, out_grad),
         name="pack_rows",
-        mib=56,
         flops=4 * owned * rows * width,
     )
-    held = {0: joined}
-    for mask in [1 << i for i in range(1, m.bit_length() - 1)][::-1]:
-        for r in sorted(held):
-            held[r | mask] = swap(held[r], "slot", mask)
-    near = [joined, swap(joined, "slot", 1)]
     if few:
-        blocks = exchange([packed[d] for d in ways])
+        blocks = exchange(packed, ways)
     else:
         x, g = (
             exchange_whole(p.reshape(n, capacity, width)).reshape(rows, width) for p in packed
         )
         blocks = [jnp.concatenate((x, g), axis=0)]
     nb = len(blocks)
-    blocks, held, near = lax.optimization_barrier((blocks, held, near))
-    far = []
-    for r in range(2, m, 2):
-        far += [held[r], swap(held[r], "slot", 1)]
+
+    held = {0: joined}
+    for mask in [1 << i for i in range(1, m.bit_length() - 1)][::-1]:
+        for r in sorted(held):
+            held[r | mask] = swap(held[r], "slot", mask)
+    middle = nb // 2
+    neighbour, blocks[middle] = lax.optimization_barrier((joined, blocks[middle]))
+    near = [joined, swap(neighbour, "slot", 1)]
+    came, held = lax.optimization_barrier((blocks[1:], [held[r] for r in range(2, m, 2)]))
+    blocks[1:] = came
+    far = [w for v in held for w in (v, swap(v, "slot", 1))]
     nf = len(far)
 
-    send, keep, partial = call(
+    send, kept, partial = call(
         functools.partial(near_kernel, nb, 2),
         [shape((part, width), BF16), shape((part, width), BF16), shape((rows, width), F32)],
         (*blocks, *near),
@@ -330,7 +332,7 @@
         name="near_units",
         flops=24 * rows * width * part,
     )
-    first = [keep, swap(send, "slot", 1)]
+    first = [kept, swap(send, "slot", 1)]
     far, partial = lax.optimization_barrier((far, partial))
     send, keep, a, b = call(
         functools.partial(hidden_kernel, nb, nf),
@@ -340,6 +342,7 @@
         name="far_units",
         flops=6 * rows * width * part * nf,
     )
+    got = swap(send, "slot", 1)
     dx = call(
         functools.partial(back_kernel, nb, nf),
         [shape((r.shape[0] // 2, width), BF16) for r in blocks],
@@ -348,17 +351,18 @@
         name="input_gradient",
         flops=6 * rows * width * part * nf,
     )
+    got, dx = lax.optimization_barrier((got, dx))
     rest = call(
         add_kernel,
         [shape((part, width), BF16)] * (nf // 2),
-        (keep, swap(send, "slot", 1)),
+        (keep, got),
         name="add_pair",
     )
     rest = [swap(r, "slot", 2 * i) for i, r in enumerate(rest, 1)]
+    back = crossing(n) if few else ways
     if few:
-        returned = exchange(dx)
-        ahead = min(EARLY, n)
-        returned[:ahead], rest = lax.optimization_barrier((returned[:ahead], rest))
+        returned = exchange(dict(zip(ways, dx, strict=True)), back)
+        returned[1:EARLY], rest = lax.optimization_barrier((returned[1:EARLY], rest))
     else:
         returned = [exchange_whole(dx[0].reshape(n, capacity, width)).reshape(rows, width)]
     pieces = call(
@@ -369,7 +373,7 @@
         name="cut_gradient",
     )
     if few:
-        arrived = exchange(pieces)
+        arrived = exchange(dict(zip(ways, pieces, strict=True)), ways)
     else:
         flip = jnp.arange(n, dtype=jnp.int32) ^ lax.axis_index("expert")
         arrived = [exchange_whole(jnp.take(pieces[0].reshape(n, owner, width), flip, axis=0))]
@@ -391,7 +395,7 @@
         name="new_state",
     )
     (token_grad,) = call(
-        functools.partial(unpack_kernel, ways),
+        functools.partial(unpack_kernel, back),
         [shape((owned, width), BF16)],
         (place, *returned),
         name="unpack_rows",
@@ -401,7 +405,7 @@
         (fresh,) = call(
             functools.partial(order_kernel, ways),
             [shape((n, owner, width), BF16)],
-            exchange(outgoing),
+            exchange(dict(zip(ways, outgoing, strict=True)), ways),
             name="order_rows",
         )
     else:

time: 150 us -> 138 us (0.920)
  starting transfers between devices: 62.9 us -> 54.5 us
  Pallas kernels: 20.4 us -> 16.7 us
    ppermute x34, starting transfers between devices: 62.9 us -> 54.5 us  [swap(): return lax.ppermute(x, axis, [(i, i ^ mask) for i in range(size)])]
    pallas_call x10 -> x11, Pallas kernels: 20.4 us -> 16.7 us  [call(): pl.pallas_call(kernel, out_shape=tuple(outs), in_specs=[pl.BlockSpec(memo...]
    unnamed x14 -> x20, local copies, waits for them, and re-layouts: 2.64 us -> 3.43 us
  transfers between devices with their start and end apart: 34 -> 34, of which waited for: 12 -> 10; matrix products, arithmetic and copies ran while one was open for 0% -> 0% of each run, Pallas kernels for 8% -> 10%
where the time goes in v4:
time: 138 us; the launch traced here: 137 us
  waiting for transfers between devices  61.9 us (45%)
  starting transfers between devices  54.5 us (39%)
  Pallas kernels  16.7 us (12%)
  local copies, waits for them, and re-layouts  3.43 us (2%)
    ppermute x34, waiting for transfers between devices, swap(): return lax.ppermute(x, axis, [(i, i ^ mask) for i in range(size)])  61.9 us
    ppermute x34, starting transfers between devices, swap(): return lax.ppermute(x, axis, [(i, i ^ mask) for i in range(size)])  54.5 us
    pallas_call x11, Pallas kernels, call(): pl.pallas_call(kernel, out_shape=tuple(outs), in_specs=[pl.BlockSpec(memo...  16.7 us
    unnamed x20, local copies, waits for them, and re-layouts  3.43 us
  transfers between devices with their start and end apart: 34, of which 10 were waited for; matrix products, arithmetic and copies ran while one was open for 0% of the time, Pallas kernels for 10%

profile of v4, /device:TPU:0, one launch (start us, length us, event | category | flops | bytes accessed | tf_op | source)
XLA Modules:
  0.0 137.3 jit_solution(16504128439146935318)
XLA Ops:
  4.2 3.0 %collective-permute-start.7 = (bf16[576,2048]{1,0:T(8,128)(2,1)S(1)}, bf16[576,2048]{1,0:T(8,128)(2,1)S(1)}, u32[]{:S(2)}, u32[]{:S(2)}) collective-permute-start(bf16[576,2048]{1,0:T(8,128)(2,1)S(1)} %join_weights.1.refs_8_), channel_id=1, source_target_pairs={{0,2},{1,3},{2,0},{3,1},{4,6},{5,7},{6,4},{7,5},{8,10},{9,11},{10,... | collective-permute-start | bytes 7077896 | tf_op jit(solution)/shard_map/ppermute | solution.py:251
  8.1 2.7 %collective-permute-start = (bf16[64,2048]{1,0:T(8,128)(2,1)S(1)}, bf16[64,2048]{1,0:T(8,128)(2,1)S(1)}, u32[]{:S(2)}, u32[]{:S(2)}) collective-permute-start(bf16[64,2048]{1,0:T(8,128)(2,1)S(1)} %get-tuple-element.76), channel_id=1, source_target_pairs={{0,16},{4,20},{8,24},{12,28},{16,0},{20,4},{24,8},{28,12},{1,17},{... | collective-permute-start | bytes 786440 | tf_op jit(solution)/shard_map/ppermute | solution.py:251
  10.7 1.5 %collective-permute-start.1 = (bf16[64,2048]{1,0:T(8,128)(2,1)S(1)}, bf16[64,2048]{1,0:T(8,128)(2,1)S(1)}, u32[]{:S(2)}, u32[]{:S(2)}) collective-permute-start(bf16[64,2048]{1,0:T(8,128)(2,1)S(1)} %get-tuple-element.77), channel_id=1, source_target_pairs={{0,4},{4,0},{8,12},{12,8},{16,20},{20,16},{24,28},{28,24},{1,5},{5... | collective-permute-start | bytes 786440 | tf_op jit(solution)/shard_map/ppermute | solution.py:251
  12.3 1.5 %collective-permute-start.3 = (bf16[64,2048]{1,0:T(8,128)(2,1)S(1)}, bf16[64,2048]{1,0:T(8,128)(2,1)S(1)}, u32[]{:S(2)}, u32[]{:S(2)}) collective-permute-start(bf16[64,2048]{1,0:T(8,128)(2,1)S(1)} %get-tuple-element.79), channel_id=1, source_target_pairs={{0,12},{4,8},{8,4},{12,0},{16,28},{20,24},{24,20},{28,16},{1,13},{... | collective-permute-start | bytes 786440 | tf_op jit(solution)/shard_map/ppermute | solution.py:251
  14.2 8.3 %collective-permute-done.refs_1_ = bf16[64,2048]{1,0:T(8,128)(2,1)S(1)} collective-permute-done((bf16[64,2048]{1,0:T(8,128)(2,1)S(1)}, bf16[64,2048]{1,0:T(8,128)(2,1)S(1)}, u32[]{:S(2)}, u32[]{:S(2)}) %collective-permute-start) | collective-permute-done | bytes 262176 | tf_op jit(solution)/shard_map/ppermute | solution.py:251
  23.0 3.5 %collective-permute-start.5 = (bf16[64,2048]{1,0:T(8,128)(2,1)S(1)}, bf16[64,2048]{1,0:T(8,128)(2,1)S(1)}, u32[]{:S(2)}, u32[]{:S(2)}) collective-permute-start(bf16[64,2048]{1,0:T(8,128)(2,1)S(1)} %get-tuple-element.82), channel_id=1, source_target_pairs={{0,24},{4,28},{8,16},{12,20},{16,8},{20,12},{24,0},{28,4},{1,25},{... | collective-permute-start | bytes 786440 | tf_op jit(solution)/shard_map/ppermute | solution.py:251
  26.5 4.1 %collective-permute-done.3.refs_4_ = bf16[64,2048]{1,0:T(8,128)(2,1)S(1)} collective-permute-done((bf16[64,2048]{1,0:T(8,128)(2,1)S(1)}, bf16[64,2048]{1,0:T(8,128)(2,1)S(1)}, u32[]{:S(2)}, u32[]{:S(2)}) %collective-permute-start.3) | collective-permute-done | bytes 262176 | tf_op jit(solution)/shard_map/ppermute | solution.py:251
  30.5 2.4 %collective-permute-done.2.refs_3_ = bf16[64,2048]{1,0:T(8,128)(2,1)S(1)} collective-permute-done((bf16[64,2048]{1,0:T(8,128)(2,1)S(1)}, bf16[64,2048]{1,0:T(8,128)(2,1)S(1)}, u32[]{:S(2)}, u32[]{:S(2)}) %collective-permute-start.2) | collective-permute-done | bytes 262176 | tf_op jit(solution)/shard_map/ppermute | solution.py:251
  32.9 17.5 %collective-permute-done.4.refs_5_ = bf16[64,2048]{1,0:T(8,128)(2,1)S(1)} collective-permute-done((bf16[64,2048]{1,0:T(8,128)(2,1)S(1)}, bf16[64,2048]{1,0:T(8,128)(2,1)S(1)}, u32[]{:S(2)}, u32[]{:S(2)}) %collective-permute-start.4) | collective-permute-done | bytes 262176 | tf_op jit(solution)/shard_map/ppermute | solution.py:251
  50.4 8.1 %collective-permute-done.7.refs_8_ = bf16[576,2048]{1,0:T(8,128)(2,1)S(1)} collective-permute-done((bf16[576,2048]{1,0:T(8,128)(2,1)S(1)}, bf16[576,2048]{1,0:T(8,128)(2,1)S(1)}, u32[]{:S(2)}, u32[]{:S(2)}) %collective-permute-start.7) | collective-permute-done | bytes 2359328 | tf_op jit(solution)/shard_map/ppermute | solution.py:251
  58.5 3.1 %near_units.1 = (bf16[192,2048]{1,0:T(8,128)(2,1)S(1)}, bf16[192,2048]{1,0:T(8,128)(2,1)S(1)}, f32[256,2048]{1,0:T(8,128)S(1)}) custom-call(bf16[64,2048]{1,0:T(8,128)(2,1)S(1)} %get-tuple-element.75.refs_0_, bf16[64,2048]{1,0:T(8,128)(2,1)S(1)} %collective-permute-done.refs_1_, bf16[64,2048]{1,0:T(8,128)(2,1)S(1)} %collective-permute-done.1.refs_2_, ...), custom_call_target="tpu_custom_call" | custom-call | flops 2415919104 | bytes 10485760 | tf_op jit(solution)/shard_map/near_units/pallas_call | solution.py:27
  63.0 1.6 %far_units.1 = (bf16[192,2048]{1,0:T(8,128)(2,1)S(1)}, bf16[192,2048]{1,0:T(8,128)(2,1)S(1)}, f32[2,192,256]{2,1,0:T(8,128)S(1)}, f32[2,192,256]{2,1,0:T(8,128)S(1)}) custom-call(bf16[64,2048]{1,0:T(8,128)(2,1)S(1)} %get-tuple-element.75.refs_0_, bf16[64,2048]{1,0:T(8,128)(2,1)S(1)} %collective-permute-done.refs_1_, ...), custom_call_target="tpu_custom_call" | custom-call | flops 1207959552 | bytes 9175040 | tf_op jit(solution)/shard_map/far_units/pallas_call | solution.py:27
  64.8 2.1 %input_gradient.1 = (bf16[32,2048]{1,0:T(8,128)(2,1)S(1)}, bf16[32,2048]{1,0:T(8,128)(2,1)S(1)}, bf16[32,2048]{1,0:T(8,128)(2,1)S(1)}, bf16[32,2048]{1,0:T(8,128...) custom-call(bf16[64,2048]{1,0:T(8,128)(2,1)S(1)} %get-tuple-element., ...), custom_call_target="tpu_custom_call" | custom-call | flops 1207959552 | bytes 10747904 | tf_op jit(solution)/shard_map/input_gradient/pallas_call | solution.py:27
  67.2 1.8 %collective-permute-start.14 = (bf16[192,2048]{1,0:T(8,128)(2,1)S(1)}, bf16[192,2048]{1,0:T(8,128)(2,1)S(1)}, u32[]{:S(2)}, u32[]{:S(2)}) collective-permute-start(bf16[192,2048]{1,0:T(8,128)(2,1)S(1)} %add_pair.1), channel_id=1, source_target_pairs={{0,2},{1,3},{2,0},{3,1},{4,6},{5,7},{6,4},{7,5},{8,10},{9,11},{10,... | collective-permute-start | bytes 2359304 | tf_op jit(solution)/shard_map/ppermute | solution.py:251
  69.1 4.2 %collective-permute-start.11 = (bf16[32,2048]{1,0:T(8,128)(2,1)S(1)}, bf16[32,2048]{1,0:T(8,128)(2,1)S(1)}, u32[]{:S(2)}, u32[]{:S(2)}) collective-permute-start(bf16[32,2048]{1,0:T(8,128)(2,1)S(1)} %get-tuple-element.109), channel_id=1, source_target_pairs={{0,16},{4,20},{8,24},{12,28},{16,0},{20,4},{24,8},{28,12},{1,17},{... | collective-permute-start | bytes 393224 | tf_op jit(solution)/shard_map/ppermute | solution.py:251
  74.2 2.4 %collective-permute-start.13 = (bf16[32,2048]{1,0:T(8,128)(2,1)S(1)}, bf16[32,2048]{1,0:T(8,128)(2,1)S(1)}, u32[]{:S(2)}, u32[]{:S(2)}) collective-permute-start(bf16[32,2048]{1,0:T(8,128)(2,1)S(1)} %get-tuple-element.111), channel_id=1, source_target_pairs={{0,24},{4,28},{8,16},{12,20},{16,8},{20,12},{24,0},{28,4},{1,25},{... | collective-permute-start | bytes 393224 | tf_op jit(solution)/shard_map/ppermute | solution.py:251
  76.6 9.5 %collective-permute-done.11.refs_1_ = bf16[32,2048]{1,0:T(8,128)(2,1)S(1)} collective-permute-done((bf16[32,2048]{1,0:T(8,128)(2,1)S(1)}, bf16[32,2048]{1,0:T(8,128)(2,1)S(1)}, u32[]{:S(2)}, u32[]{:S(2)}) %collective-permute-start.11) | collective-permute-done | bytes 131104 | tf_op jit(solution)/shard_map/ppermute | solution.py:251
  86.1 3.0 %collective-permute-done.12.refs_2_ = bf16[32,2048]{1,0:T(8,128)(2,1)S(1)} collective-permute-done((bf16[32,2048]{1,0:T(8,128)(2,1)S(1)}, bf16[32,2048]{1,0:T(8,128)(2,1)S(1)}, u32[]{:S(2)}, u32[]{:S(2)}) %collective-permute-start.12) | collective-permute-done | bytes 131104 | tf_op jit(solution)/shard_map/ppermute | solution.py:251
  89.7 3.6 %collective-permute-start.20 = (bf16[24,2048]{1,0:T(8,128)(2,1)S(1)}, bf16[24,2048]{1,0:T(8,128)(2,1)S(1)}, u32[]{:S(2)}, u32[]{:S(2)}) collective-permute-start(bf16[24,2048]{1,0:T(8,128)(2,1)S(1)} %get-tuple-element.125), channel_id=1, source_target_pairs={{0,16},{4,20},{8,24},{12,28},{16,0},{20,4},{24,8},{28,12},{1,17},{... | collective-permute-start | bytes 294920 | tf_op jit(solution)/shard_map/ppermute | solution.py:251
  93.2 1.5 %collective-permute-start.21 = (bf16[24,2048]{1,0:T(8,128)(2,1)S(1)}, bf16[24,2048]{1,0:T(8,128)(2,1)S(1)}, u32[]{:S(2)}, u32[]{:S(2)}) collective-permute-start(bf16[24,2048]{1,0:T(8,128)(2,1)S(1)} %get-tuple-element.126), channel_id=1, source_target_pairs={{0,4},{4,0},{8,12},{12,8},{16,20},{20,16},{24,28},{28,24},{1,5},{5... | collective-permute-start | bytes 294920 | tf_op jit(solution)/shard_map/ppermute | solution.py:251
  94.8 2.0 %collective-permute-start.23 = (bf16[24,2048]{1,0:T(8,128)(2,1)S(1)}, bf16[24,2048]{1,0:T(8,128)(2,1)S(1)}, u32[]{:S(2)}, u32[]{:S(2)}) collective-permute-start(bf16[24,2048]{1,0:T(8,128)(2,1)S(1)} %get-tuple-element.128), channel_id=1, source_target_pairs={{0,12},{4,8},{8,4},{12,0},{16,28},{20,24},{24,20},{28,16},{1,13},{... | collective-permute-start | bytes 294920 | tf_op jit(solution)/shard_map/ppermute | solution.py:251
  97.8 2.3 %collective-permute-start.25 = (bf16[24,2048]{1,0:T(8,128)(2,1)S(1)}, bf16[24,2048]{1,0:T(8,128)(2,1)S(1)}, u32[]{:S(2)}, u32[]{:S(2)}) collective-permute-start(bf16[24,2048]{1,0:T(8,128)(2,1)S(1)} %get-tuple-element.130), channel_id=1, source_target_pairs={{0,24},{4,28},{8,16},{12,20},{16,8},{20,12},{24,0},{28,4},{1,25},{... | collective-permute-start | bytes 294920 | tf_op jit(solution)/shard_map/ppermute | solution.py:251
  100.9 2.1 %collective-permute-start.26 = (bf16[24,2048]{1,0:T(8,128)(2,1)S(1)}, bf16[24,2048]{1,0:T(8,128)(2,1)S(1)}, u32[]{:S(2)}, u32[]{:S(2)}) collective-permute-start(bf16[24,2048]{1,0:T(8,128)(2,1)S(1)} %get-tuple-element.131), channel_id=1, source_target_pairs={{0,28},{4,24},{8,20},{12,16},{16,12},{20,8},{24,4},{28,0},{1,29},{... | collective-permute-start | bytes 294920 | tf_op jit(solution)/shard_map/ppermute | solution.py:251
  103.1 2.6 %collective-permute-start.16 = (bf16[32,2048]{1,0:T(8,128)(2,1)S(1)}, bf16[32,2048]{1,0:T(8,128)(2,1)S(1)}, u32[]{:S(2)}, u32[]{:S(2)}) collective-permute-start(bf16[32,2048]{1,0:T(8,128)(2,1)S(1)} %get-tuple-element.118), channel_id=1, source_target_pairs={{0,28},{4,24},{8,20},{12,16},{16,12},{20,8},{24,4},{28,0},{1,29},{... | collective-permute-start | bytes 393224 | tf_op jit(solution)/shard_map/ppermute | solution.py:251
  105.7 7.3 %collective-permute-done.24.refs_5_ = bf16[24,2048]{1,0:T(8,128)(2,1)S(1)} collective-permute-done((bf16[24,2048]{1,0:T(8,128)(2,1)S(1)}, bf16[24,2048]{1,0:T(8,128)(2,1)S(1)}, u32[]{:S(2)}, u32[]{:S(2)}) %collective-permute-start.24) | collective-permute-done | bytes 98336 | tf_op jit(solution)/shard_map/ppermute | solution.py:251
  113.0 2.7 %collective-permute-start.18 = (bf16[32,2048]{1,0:T(8,128)(2,1)S(1)}, bf16[32,2048]{1,0:T(8,128)(2,1)S(1)}, u32[]{:S(2)}, u32[]{:S(2)}) collective-permute-start(bf16[32,2048]{1,0:T(8,128)(2,1)S(1)} %get-tuple-element.120), channel_id=1, source_target_pairs={{0,12},{4,8},{8,4},{12,0},{16,28},{20,24},{24,20},{28,16},{1,13},{... | collective-permute-start | bytes 393224 | tf_op jit(solution)/shard_map/ppermute | solution.py:251
  115.7 2.4 %new_rows.1 = (bf16[24,2048]{1,0:T(8,128)(2,1)S(1)}, bf16[24,2048]{1,0:T(8,128)(2,1)S(1)}, bf16[24,2048]{1,0:T(8,128)(2,1)S(1)}, bf16[24,2048]{1,0:T(8,128)(2,1)...) custom-call(s32[8]{0:T(128)S(1)} %copy-done.8, ...), custom_call_target="tpu_custom_call" | custom-call | bytes 5111840 | tf_op jit(solution)/shard_map/new_rows/pallas_call | solution.py:27
  118.2 2.7 %collective-permute-start.27 = (bf16[24,2048]{1,0:T(8,128)(2,1)S(1)}, bf16[24,2048]{1,0:T(8,128)(2,1)S(1)}, u32[]{:S(2)}, u32[]{:S(2)}) collective-permute-start(bf16[24,2048]{1,0:T(8,128)(2,1)S(1)} %get-tuple-element.136), channel_id=1, source_target_pairs={{0,16},{4,20},{8,24},{12,28},{16,0},{20,4},{24,8},{28,12},{1,17},{... | collective-permute-start | bytes 294920 | tf_op jit(solution)/shard_map/ppermute | solution.py:251
  121.6 2.7 %collective-permute-start.30 = (bf16[24,2048]{1,0:T(8,128)(2,1)S(1)}, bf16[24,2048]{1,0:T(8,128)(2,1)S(1)}, u32[]{:S(2)}, u32[]{:S(2)}) collective-permute-start(bf16[24,2048]{1,0:T(8,128)(2,1)S(1)} %get-tuple-element.139), channel_id=1, source_target_pairs={{0,12},{4,8},{8,4},{12,0},{16,28},{20,24},{24,20},{28,16},{1,13},{... | collective-permute-start | bytes 294920 | tf_op jit(solution)/shard_map/ppermute | solution.py:251
  125.3 1.6 %collective-permute-start.32 = (bf16[24,2048]{1,0:T(8,128)(2,1)S(1)}, bf16[24,2048]{1,0:T(8,128)(2,1)S(1)}, u32[]{:S(2)}, u32[]{:S(2)}) collective-permute-start(bf16[24,2048]{1,0:T(8,128)(2,1)S(1)} %get-tuple-element.141), channel_id=1, source_target_pairs={{0,24},{4,28},{8,16},{12,20},{16,8},{20,12},{24,0},{28,4},{1,25},{... | collective-permute-start | bytes 294920 | tf_op jit(solution)/shard_map/ppermute | solution.py:251
  126.9 4.7 %collective-permute-start.33 = (bf16[24,2048]{1,0:T(8,128)(2,1)S(1)}, bf16[24,2048]{1,0:T(8,128)(2,1)S(1)}, u32[]{:S(2)}, u32[]{:S(2)}) collective-permute-start(bf16[24,2048]{1,0:T(8,128)(2,1)S(1)} %get-tuple-element.142), channel_id=1, source_target_pairs={{0,28},{4,24},{8,20},{12,16},{16,12},{20,8},{24,4},{28,0},{1,29},{... | collective-permute-start | bytes 294920 | tf_op jit(solution)/shard_map/ppermute | solution.py:251
  132.7 3.6 %new_state.1 = (f32[6,24,2048]{2,1,0:T(8,128)}, f32[6,24,2048]{2,1,0:T(8,128)}, f32[6,24,2048]{2,1,0:T(8,128)}) custom-call(s32[8]{0:T(128)S(1)} %copy-done.8, bf16[24,2048]{1,0:T(8,128)(2,1)S(1)} %get-tuple-element.124.refs_0_, bf16[24,2048]{1,0:T(8,128)(2,1)S(1)} %collective-permute-done.20.refs_1_, bf16[24,2048]{1,0:T(8,128)(2,1)S(1)} %collective-permute-done.21.refs_2_, ...), custom_call_target="tpu_custom_call" | custom-call | bytes 7864352 | tf_op jit(solution)/shard_map/new_state/pallas_call | solution.py:27
  (67 shorter events, 14.5 us)
Async XLA Ops:
  4.2 54.3 %collective-permute-start.7 = (bf16[576,2048]{1,0:T(8,128)(2,1)S(1)}, bf16[576,2048]{1,0:T(8,128)(2,1)S(1)}, u32[]{:S(2)}, u32[]{:S(2)}) collective-permute-start(bf16[576,2048]{1,0:T(8,128)(2,1)S(1)} %join_weights.1.refs_8_), channel_id=1, source_target_pairs={{0,2},{1,3},{2,0},{3,1},{4,6},{5,7},{6,4},{7,5},{8,10},{9,11},{10,... | collective-permute-start | bytes 7077896 | tf_op jit(solution)/shard_map/ppermute | solution.py:251
  8.1 14.4 %collective-permute-start = (bf16[64,2048]{1,0:T(8,128)(2,1)S(1)}, bf16[64,2048]{1,0:T(8,128)(2,1)S(1)}, u32[]{:S(2)}, u32[]{:S(2)}) collective-permute-start(bf16[64,2048]{1,0:T(8,128)(2,1)S(1)} %get-tuple-element.76), channel_id=1, source_target_pairs={{0,16},{4,20},{8,24},{12,28},{16,0},{20,4},{24,8},{28,12},{1,17},{... | collective-permute-start | bytes 786440 | tf_op jit(solution)/shard_map/ppermute | solution.py:251
  10.7 12.2 %collective-permute-start.1 = (bf16[64,2048]{1,0:T(8,128)(2,1)S(1)}, bf16[64,2048]{1,0:T(8,128)(2,1)S(1)}, u32[]{:S(2)}, u32[]{:S(2)}) collective-permute-start(bf16[64,2048]{1,0:T(8,128)(2,1)S(1)} %get-tuple-element.77), channel_id=1, source_target_pairs={{0,4},{4,0},{8,12},{12,8},{16,20},{20,16},{24,28},{28,24},{1,5},{5... | collective-permute-start | bytes 786440 | tf_op jit(solution)/shard_map/ppermute | solution.py:251
  12.3 18.3 %collective-permute-start.3 = (bf16[64,2048]{1,0:T(8,128)(2,1)S(1)}, bf16[64,2048]{1,0:T(8,128)(2,1)S(1)}, u32[]{:S(2)}, u32[]{:S(2)}) collective-permute-start(bf16[64,2048]{1,0:T(8,128)(2,1)S(1)} %get-tuple-element.79), channel_id=1, source_target_pairs={{0,12},{4,8},{8,4},{12,0},{16,28},{20,24},{24,20},{28,16},{1,13},{... | collective-permute-start | bytes 786440 | tf_op jit(solution)/shard_map/ppermute | solution.py:251
  13.8 19.1 %collective-permute-start.2 = (bf16[64,2048]{1,0:T(8,128)(2,1)S(1)}, bf16[64,2048]{1,0:T(8,128)(2,1)S(1)}, u32[]{:S(2)}, u32[]{:S(2)}) collective-permute-start(bf16[64,2048]{1,0:T(8,128)(2,1)S(1)} %get-tuple-element.78), channel_id=1, source_target_pairs={{0,8},{4,12},{8,0},{12,4},{16,24},{20,28},{24,16},{28,20},{1,9},{5... | collective-permute-start | bytes 786440 | tf_op jit(solution)/shard_map/ppermute | solution.py:251
  22.5 27.9 %collective-permute-start.4 = (bf16[64,2048]{1,0:T(8,128)(2,1)S(1)}, bf16[64,2048]{1,0:T(8,128)(2,1)S(1)}, u32[]{:S(2)}, u32[]{:S(2)}) collective-permute-start(bf16[64,2048]{1,0:T(8,128)(2,1)S(1)} %get-tuple-element.81), channel_id=1, source_target_pairs={{0,20},{4,16},{8,28},{12,24},{16,4},{20,0},{24,12},{28,8},{1,21},{... | collective-permute-start | bytes 786440 | tf_op jit(solution)/shard_map/ppermute | solution.py:251
  23.0 27.4 %collective-permute-start.5 = (bf16[64,2048]{1,0:T(8,128)(2,1)S(1)}, bf16[64,2048]{1,0:T(8,128)(2,1)S(1)}, u32[]{:S(2)}, u32[]{:S(2)}) collective-permute-start(bf16[64,2048]{1,0:T(8,128)(2,1)S(1)} %get-tuple-element.82), channel_id=1, source_target_pairs={{0,24},{4,28},{8,16},{12,20},{16,8},{20,12},{24,0},{28,4},{1,25},{... | collective-permute-start | bytes 786440 | tf_op jit(solution)/shard_map/ppermute | solution.py:251
  30.5 19.9 %collective-permute-start.6 = (bf16[64,2048]{1,0:T(8,128)(2,1)S(1)}, bf16[64,2048]{1,0:T(8,128)(2,1)S(1)}, u32[]{:S(2)}, u32[]{:S(2)}) collective-permute-start(bf16[64,2048]{1,0:T(8,128)(2,1)S(1)} %get-tuple-element.83), channel_id=1, source_target_pairs={{0,28},{4,24},{8,20},{12,16},{16,12},{20,8},{24,4},{28,0},{1,29},{... | collective-permute-start | bytes 786440 | tf_op jit(solution)/shard_map/ppermute | solution.py:251
  32.9 25.6 %collective-permute-start.9 = (bf16[576,2048]{1,0:T(8,128)(2,1)S(1)}, bf16[576,2048]{1,0:T(8,128)(2,1)S(1)}, u32[]{:S(2)}, u32[]{:S(2)}) collective-permute-start(bf16[576,2048]{1,0:T(8,128)(2,1)S(1)} %join_weights.1.refs_8_), channel_id=1, source_target_pairs={{0,1},{1,0},{2,3},{3,2},{4,5},{5,4},{6,7},{7,6},{8,9},{9,8},{10,11... | collective-permute-start | bytes 7077896 | tf_op jit(solution)/shard_map/ppermute | solution.py:251
  67.2 21.9 %collective-permute-start.14 = (bf16[192,2048]{1,0:T(8,128)(2,1)S(1)}, bf16[192,2048]{1,0:T(8,128)(2,1)S(1)}, u32[]{:S(2)}, u32[]{:S(2)}) collective-permute-start(bf16[192,2048]{1,0:T(8,128)(2,1)S(1)} %add_pair.1), channel_id=1, source_target_pairs={{0,2},{1,3},{2,0},{3,1},{4,6},{5,7},{6,4},{7,5},{8,10},{9,11},{10,... | collective-permute-start | bytes 2359304 | tf_op jit(solution)/shard_map/ppermute | solution.py:251
  69.0 20.1 %collective-permute-start.19 = (bf16[192,2048]{1,0:T(8,128)(2,1)S(1)}, bf16[192,2048]{1,0:T(8,128)(2,1)S(1)}, u32[]{:S(2)}, u32[]{:S(2)}) collective-permute-start(bf16[192,2048]{1,0:T(8,128)(2,1)S(1)} %get-tuple-element.122), channel_id=1, source_target_pairs={{0,1},{1,0},{2,3},{3,2},{4,5},{5,4},{6,7},{7,6},{8,9},{9,8},{10,11... | collective-permute-start | bytes 2359304 | tf_op jit(solution)/shard_map/ppermute | solution.py:251
  69.1 17.0 %collective-permute-start.11 = (bf16[32,2048]{1,0:T(8,128)(2,1)S(1)}, bf16[32,2048]{1,0:T(8,128)(2,1)S(1)}, u32[]{:S(2)}, u32[]{:S(2)}) collective-permute-start(bf16[32,2048]{1,0:T(8,128)(2,1)S(1)} %get-tuple-element.109), channel_id=1, source_target_pairs={{0,16},{4,20},{8,24},{12,28},{16,0},{20,4},{24,8},{28,12},{1,17},{... | collective-permute-start | bytes 393224 | tf_op jit(solution)/shard_map/ppermute | solution.py:251
  73.3 15.7 %collective-permute-start.12 = (bf16[32,2048]{1,0:T(8,128)(2,1)S(1)}, bf16[32,2048]{1,0:T(8,128)(2,1)S(1)}, u32[]{:S(2)}, u32[]{:S(2)}) collective-permute-start(bf16[32,2048]{1,0:T(8,128)(2,1)S(1)} %get-tuple-element.110), channel_id=1, source_target_pairs={{0,20},{4,16},{8,28},{12,24},{16,4},{20,0},{24,12},{28,8},{1,21},{... | collective-permute-start | bytes 393224 | tf_op jit(solution)/shard_map/ppermute | solution.py:251
  74.2 14.8 %collective-permute-start.13 = (bf16[32,2048]{1,0:T(8,128)(2,1)S(1)}, bf16[32,2048]{1,0:T(8,128)(2,1)S(1)}, u32[]{:S(2)}, u32[]{:S(2)}) collective-permute-start(bf16[32,2048]{1,0:T(8,128)(2,1)S(1)} %get-tuple-element.111), channel_id=1, source_target_pairs={{0,24},{4,28},{8,16},{12,20},{16,8},{20,12},{24,0},{28,4},{1,25},{... | collective-permute-start | bytes 393224 | tf_op jit(solution)/shard_map/ppermute | solution.py:251
  89.7 8.1 %collective-permute-start.20 = (bf16[24,2048]{1,0:T(8,128)(2,1)S(1)}, bf16[24,2048]{1,0:T(8,128)(2,1)S(1)}, u32[]{:S(2)}, u32[]{:S(2)}) collective-permute-start(bf16[24,2048]{1,0:T(8,128)(2,1)S(1)} %get-tuple-element.125), channel_id=1, source_target_pairs={{0,16},{4,20},{8,24},{12,28},{16,0},{20,4},{24,8},{28,12},{1,17},{... | collective-permute-start | bytes 294920 | tf_op jit(solution)/shard_map/ppermute | solution.py:251
  93.2 6.8 %collective-permute-start.21 = (bf16[24,2048]{1,0:T(8,128)(2,1)S(1)}, bf16[24,2048]{1,0:T(8,128)(2,1)S(1)}, u32[]{:S(2)}, u32[]{:S(2)}) collective-permute-start(bf16[24,2048]{1,0:T(8,128)(2,1)S(1)} %get-tuple-element.126), channel_id=1, source_target_pairs={{0,4},{4,0},{8,12},{12,8},{16,20},{20,16},{24,28},{28,24},{1,5},{5... | collective-permute-start | bytes 294920 | tf_op jit(solution)/shard_map/ppermute | solution.py:251
  94.8 6.2 %collective-permute-start.22 = (bf16[24,2048]{1,0:T(8,128)(2,1)S(1)}, bf16[24,2048]{1,0:T(8,128)(2,1)S(1)}, u32[]{:S(2)}, u32[]{:S(2)}) collective-permute-start(bf16[24,2048]{1,0:T(8,128)(2,1)S(1)} %get-tuple-element.127), channel_id=1, source_target_pairs={{0,8},{4,12},{8,0},{12,4},{16,24},{20,28},{24,16},{28,20},{1,9},{5... | collective-permute-start | bytes 294920 | tf_op jit(solution)/shard_map/ppermute | solution.py:251
  94.8 8.3 %collective-permute-start.23 = (bf16[24,2048]{1,0:T(8,128)(2,1)S(1)}, bf16[24,2048]{1,0:T(8,128)(2,1)S(1)}, u32[]{:S(2)}, u32[]{:S(2)}) collective-permute-start(bf16[24,2048]{1,0:T(8,128)(2,1)S(1)} %get-tuple-element.128), channel_id=1, source_target_pairs={{0,12},{4,8},{8,4},{12,0},{16,28},{20,24},{24,20},{28,16},{1,13},{... | collective-permute-start | bytes 294920 | tf_op jit(solution)/shard_map/ppermute | solution.py:251
  96.7 16.3 %collective-permute-start.24 = (bf16[24,2048]{1,0:T(8,128)(2,1)S(1)}, bf16[24,2048]{1,0:T(8,128)(2,1)S(1)}, u32[]{:S(2)}, u32[]{:S(2)}) collective-permute-start(bf16[24,2048]{1,0:T(8,128)(2,1)S(1)} %get-tuple-element.129), channel_id=1, source_target_pairs={{0,20},{4,16},{8,28},{12,24},{16,4},{20,0},{24,12},{28,8},{1,21},{... | collective-permute-start | bytes 294920 | tf_op jit(solution)/shard_map/ppermute | solution.py:251
  97.8 15.2 %collective-permute-start.25 = (bf16[24,2048]{1,0:T(8,128)(2,1)S(1)}, bf16[24,2048]{1,0:T(8,128)(2,1)S(1)}, u32[]{:S(2)}, u32[]{:S(2)}) collective-permute-start(bf16[24,2048]{1,0:T(8,128)(2,1)S(1)} %get-tuple-element.130), channel_id=1, source_target_pairs={{0,24},{4,28},{8,16},{12,20},{16,8},{20,12},{24,0},{28,4},{1,25},{... | collective-permute-start | bytes 294920 | tf_op jit(solution)/shard_map/ppermute | solution.py:251
  100.1 20.8 %collective-permute-start.15 = (bf16[32,2048]{1,0:T(8,128)(2,1)S(1)}, bf16[32,2048]{1,0:T(8,128)(2,1)S(1)}, u32[]{:S(2)}, u32[]{:S(2)}) collective-permute-start(bf16[32,2048]{1,0:T(8,128)(2,1)S(1)} %get-tuple-element.117), channel_id=1, source_target_pairs={{0,4},{4,0},{8,12},{12,8},{16,20},{20,16},{24,28},{28,24},{1,5},{5... | collective-permute-start | bytes 393224 | tf_op jit(solution)/shard_map/ppermute | solution.py:251
  100.9 14.8 %collective-permute-start.26 = (bf16[24,2048]{1,0:T(8,128)(2,1)S(1)}, bf16[24,2048]{1,0:T(8,128)(2,1)S(1)}, u32[]{:S(2)}, u32[]{:S(2)}) collective-permute-start(bf16[24,2048]{1,0:T(8,128)(2,1)S(1)} %get-tuple-element.131), channel_id=1, source_target_pairs={{0,28},{4,24},{8,20},{12,16},{16,12},{20,8},{24,4},{28,0},{1,29},{... | collective-permute-start | bytes 294920 | tf_op jit(solution)/shard_map/ppermute | solution.py:251
  103.1 18.4 %collective-permute-start.16 = (bf16[32,2048]{1,0:T(8,128)(2,1)S(1)}, bf16[32,2048]{1,0:T(8,128)(2,1)S(1)}, u32[]{:S(2)}, u32[]{:S(2)}) collective-permute-start(bf16[32,2048]{1,0:T(8,128)(2,1)S(1)} %get-tuple-element.118), channel_id=1, source_target_pairs={{0,28},{4,24},{8,20},{12,16},{16,12},{20,8},{24,4},{28,0},{1,29},{... | collective-permute-start | bytes 393224 | tf_op jit(solution)/shard_map/ppermute | solution.py:251
  113.0 8.6 %collective-permute-start.17 = (bf16[32,2048]{1,0:T(8,128)(2,1)S(1)}, bf16[32,2048]{1,0:T(8,128)(2,1)S(1)}, u32[]{:S(2)}, u32[]{:S(2)}) collective-permute-start(bf16[32,2048]{1,0:T(8,128)(2,1)S(1)} %get-tuple-element.119), channel_id=1, source_target_pairs={{0,8},{4,12},{8,0},{12,4},{16,24},{20,28},{24,16},{28,20},{1,9},{5... | collective-permute-start | bytes 393224 | tf_op jit(solution)/shard_map/ppermute | solution.py:251
  113.0 11.3 %collective-permute-start.18 = (bf16[32,2048]{1,0:T(8,128)(2,1)S(1)}, bf16[32,2048]{1,0:T(8,128)(2,1)S(1)}, u32[]{:S(2)}, u32[]{:S(2)}) collective-permute-start(bf16[32,2048]{1,0:T(8,128)(2,1)S(1)} %get-tuple-element.120), channel_id=1, source_target_pairs={{0,12},{4,8},{8,4},{12,0},{16,28},{20,24},{24,20},{28,16},{1,13},{... | collective-permute-start | bytes 393224 | tf_op jit(solution)/shard_map/ppermute | solution.py:251
  118.2 7.1 %collective-permute-start.27 = (bf16[24,2048]{1,0:T(8,128)(2,1)S(1)}, bf16[24,2048]{1,0:T(8,128)(2,1)S(1)}, u32[]{:S(2)}, u32[]{:S(2)}) collective-permute-start(bf16[24,2048]{1,0:T(8,128)(2,1)S(1)} %get-tuple-element.136), channel_id=1, source_target_pairs={{0,16},{4,20},{8,24},{12,28},{16,0},{20,4},{24,8},{28,12},{1,17},{... | collective-permute-start | bytes 294920 | tf_op jit(solution)/shard_map/ppermute | solution.py:251
  120.8 6.1 %collective-permute-start.28 = (bf16[24,2048]{1,0:T(8,128)(2,1)S(1)}, bf16[24,2048]{1,0:T(8,128)(2,1)S(1)}, u32[]{:S(2)}, u32[]{:S(2)}) collective-permute-start(bf16[24,2048]{1,0:T(8,128)(2,1)S(1)} %get-tuple-element.137), channel_id=1, source_target_pairs={{0,4},{4,0},{8,12},{12,8},{16,20},{20,16},{24,28},{28,24},{1,5},{5... | collective-permute-start | bytes 294920 | tf_op jit(solution)/shard_map/ppermute | solution.py:251
  121.5 14.9 %collective-permute-start.29 = (bf16[24,2048]{1,0:T(8,128)(2,1)S(1)}, bf16[24,2048]{1,0:T(8,128)(2,1)S(1)}, u32[]{:S(2)}, u32[]{:S(2)}) collective-permute-start(bf16[24,2048]{1,0:T(8,128)(2,1)S(1)} %get-tuple-element.138), channel_id=1, source_target_pairs={{0,8},{4,12},{8,0},{12,4},{16,24},{20,28},{24,16},{28,20},{1,9},{5... | collective-permute-start | bytes 294920 | tf_op jit(solution)/shard_map/ppermute | solution.py:251
  121.6 14.7 %collective-permute-start.30 = (bf16[24,2048]{1,0:T(8,128)(2,1)S(1)}, bf16[24,2048]{1,0:T(8,128)(2,1)S(1)}, u32[]{:S(2)}, u32[]{:S(2)}) collective-permute-start(bf16[24,2048]{1,0:T(8,128)(2,1)S(1)} %get-tuple-element.139), channel_id=1, source_target_pairs={{0,12},{4,8},{8,4},{12,0},{16,28},{20,24},{24,20},{28,16},{1,13},{... | collective-permute-start | bytes 294920 | tf_op jit(solution)/shard_map/ppermute | solution.py:251
  124.3 12.0 %collective-permute-start.31 = (bf16[24,2048]{1,0:T(8,128)(2,1)S(1)}, bf16[24,2048]{1,0:T(8,128)(2,1)S(1)}, u32[]{:S(2)}, u32[]{:S(2)}) collective-permute-start(bf16[24,2048]{1,0:T(8,128)(2,1)S(1)} %get-tuple-element.140), channel_id=1, source_target_pairs={{0,20},{4,16},{8,28},{12,24},{16,4},{20,0},{24,12},{28,8},{1,21},{... | collective-permute-start | bytes 294920 | tf_op jit(solution)/shard_map/ppermute | solution.py:251
  125.3 11.1 %collective-permute-start.32 = (bf16[24,2048]{1,0:T(8,128)(2,1)S(1)}, bf16[24,2048]{1,0:T(8,128)(2,1)S(1)}, u32[]{:S(2)}, u32[]{:S(2)}) collective-permute-start(bf16[24,2048]{1,0:T(8,128)(2,1)S(1)} %get-tuple-element.141), channel_id=1, source_target_pairs={{0,24},{4,28},{8,16},{12,20},{16,8},{20,12},{24,0},{28,4},{1,25},{... | collective-permute-start | bytes 294920 | tf_op jit(solution)/shard_map/ppermute | solution.py:251
  126.9 9.5 %collective-permute-start.33 = (bf16[24,2048]{1,0:T(8,128)(2,1)S(1)}, bf16[24,2048]{1,0:T(8,128)(2,1)S(1)}, u32[]{:S(2)}, u32[]{:S(2)}) collective-permute-start(bf16[24,2048]{1,0:T(8,128)(2,1)S(1)} %get-tuple-element.142), channel_id=1, source_target_pairs={{0,28},{4,24},{8,20},{12,16},{16,12},{20,8},{24,4},{28,0},{1,29},{... | collective-permute-start | bytes 294920 | tf_op jit(solution)/shard_map/ppermute | solution.py:251
  (12 other events, 148.6 us)

commit v5 on v4

--- a/solution.py
+++ b/solution.py
@@ -13,7 +13,9 @@
 TN = (((0,), (0,)), ((), ()))
 NN = (((1,), (0,)), ((), ()))
 COLUMNS = 512
-EARLY = 4
+PIECES = 6
+OUT = 3
+NEWFLOPS = 2 * 10**9
 
 
 def dot(a, b, dims):
@@ -80,18 +82,6 @@
     return parts[0] if len(parts) == 1 else jnp.concatenate(parts, axis=0)
 
 
-def join_kernel(*refs):
-    parts, out_ref, sem = refs[:-2], refs[-2], refs[-1]
-    start, copies = 0, []
-    for i, ref in enumerate(parts):
-        rows = ref.shape[0]
-        copies.append(pltpu.make_async_copy(ref, out_ref.at[start : start + rows], sem.at[i]))
-        copies[i].start()
-        start += rows
-    for copy in copies:
-        copy.wait()
-
-
 def forward(weight, x):
     part = weight.shape[0] // 3
     both = dot(weight[: 2 * part], x, NT)
@@ -198,20 +188,20 @@
 def adam_update(folded, master, moment, second):
     new_moment = 0.9 * moment + 0.1 * folded
     new_second = 0.95 * second + 0.05 * folded * folded
-    first_hat = new_moment / (1.0 - 0.9**10)
-    second_hat = new_second / (1.0 - 0.95**10)
+    first_hat = new_moment * (1.0 / (1.0 - 0.9**10))
+    second_hat = new_second * (1.0 / (1.0 - 0.95**10))
     new_master = master - 0.01 * (first_hat / (jnp.sqrt(second_hat) + 1e-08) + 0.1 * master)
     return new_master, new_moment, new_second
 
 
-def rows_kernel(blocks, count, plan_ref, *refs):
+def rows_kernel(blocks, new, count, plan_ref, *refs):
     pieces, (master_ref, moment_ref, second_ref) = refs[:count], refs[count : count + 3]
     outs, folded = refs[count + 3 : -1], refs[-1]
     e = lax.axis_index("expert")
     fold(blocks, plan_ref, pieces, folded)
     for p in range(folded.shape[0]):
         folded[p] = adam_update(folded[p], master_ref[p], moment_ref[p], second_ref[p])[0]
-    for i, d in enumerate(blocks):
+    for i, d in enumerate(new):
         row = folded[plan_ref[e ^ d]].astype(BF16)
         if len(outs) == 1:
             outs[0][i] = row
@@ -256,8 +246,11 @@
 
 
 def crossing(n):
-    long, short = list(range(n // 2, n)), list(range(1, n // 2))
-    return [0, *long[: EARLY - 1], *short[:1], *long[EARLY - 1 :], *short[1:]]
+    return [0, *range(n // 2, n - 1), *range(1, n // 2), n - 1]
+
+
+def by_turns(n):
+    return [0, *(d for r in range(n // 2) for d in (n // 2 + r, r + 1))][:n]
 
 
 def exchange(blocks, ways):
@@ -269,6 +262,10 @@
     x = jnp.take(x, flip, axis=0)
     x = lax.all_to_all(x, "expert", split_axis=0, concat_axis=0, tiled=True)
     return jnp.take(x, flip, axis=0)
+
+
+def after(*values):
+    return lax.optimization_barrier(values)
 
 
 def body(
@@ -282,18 +279,11 @@
     rows = n * capacity
     few = capacity % 16 == 0
     ways = order(n) if few else list(range(n))
+    mixed = by_turns(n) if few else ways
     shape = jax.ShapeDtypeStruct
 
     weights = [jnp.swapaxes(w, 1, 2)[0] for w in (gate_weight, up_weight)] + [down_weight[0]]
-    (joined,) = call(
-        join_kernel,
-        [shape((3 * part, width), BF16)],
-        weights,
-        scratch=[pltpu.SemaphoreType.DMA((3,))],
-        far=range(3),
-        name="join_weights",
-        mib=16,
-    )
+    joined = jnp.concatenate(weights, axis=0)
     outs = [shape((rows, owned), BF16)]
     outs += [shape((2 * capacity, width), BF16)] * n if few else [shape((rows, width), BF16)] * 2
     place, *packed = call(
@@ -304,7 +294,7 @@
         flops=4 * owned * rows * width,
     )
     if few:
-        blocks = exchange(packed, ways)
+        blocks = exchange(packed, mixed)
     else:
         x, g = (
             exchange_whole(p.reshape(n, capacity, width)).reshape(rows, width) for p in packed
@@ -351,7 +341,7 @@
         name="input_gradient",
         flops=6 * rows * width * part * nf,
     )
-    got, dx = lax.optimization_barrier((got, dx))
+    got, dx = after(got, list(dx))
     rest = call(
         add_kernel,
         [shape((part, width), BF16)] * (nf // 2),
@@ -359,12 +349,13 @@
         name="add_pair",
     )
     rest = [swap(r, "slot", 2 * i) for i, r in enumerate(rest, 1)]
-    back = crossing(n) if few else ways
+    owner = part // n
     if few:
-        returned = exchange(dict(zip(ways, dx, strict=True)), back)
-        returned[1:EARLY], rest = lax.optimization_barrier((returned[1:EARLY], rest))
-    else:
-        returned = [exchange_whole(dx[0].reshape(n, capacity, width)).reshape(rows, width)]
+        back = crossing(n)
+        dx = dict(zip(mixed, dx, strict=True))
+        returned = exchange(dx, back[:-1])
+        ahead = n // 2
+        returned[1:ahead], rest = after(returned[1:ahead], rest)
     pieces = call(
         functools.partial(cut_kernel, len(first) + len(rest), ways),
         [shape((owner, width), BF16)] * n if few else [shape((part, width), BF16)],
@@ -374,18 +365,27 @@
     )
     if few:
         arrived = exchange(dict(zip(ways, pieces, strict=True)), ways)
+        if PIECES:
+            dx[n - 1], arrived[PIECES] = after(dx[n - 1], arrived[PIECES])
+        returned += exchange(dx, back[-1:])
     else:
+        back = ways
+        returned = [exchange_whole(dx[0].reshape(n, capacity, width)).reshape(rows, width)]
         flip = jnp.arange(n, dtype=jnp.int32) ^ lax.axis_index("expert")
         arrived = [exchange_whole(jnp.take(pieces[0].reshape(n, owner, width), flip, axis=0))]
     state = (plan, *arrived, master, moment, second)
     outgoing = call(
-        functools.partial(rows_kernel, ways, len(arrived)),
+        functools.partial(rows_kernel, ways, mixed, len(arrived)),
         [shape((owner, width), BF16)] * n if few else [shape((n, owner, width), BF16)],
         state,
         scratch=[pltpu.VMEM(master.shape, F32)],
         smem=(0,),
         name="new_rows",
-    )
+        flops=NEWFLOPS,
+    )
+    if few and OUT:
+        outgoing = list(outgoing)
+        returned[-1], outgoing[OUT:] = after(returned[-1], outgoing[OUT:])
     new_master, new_moment, new_second = call(
         functools.partial(state_kernel, ways, len(arrived)),
         [shape(master.shape, F32)] * 3,
@@ -403,9 +403,9 @@
     )
     if few:
         (fresh,) = call(
-            functools.partial(order_kernel, ways),
+            functools.partial(order_kernel, mixed),
             [shape((n, owner, width), BF16)],
-            exchange(dict(zip(ways, outgoing, strict=True)), ways),
+            exchange(dict(zip(mixed, outgoing, strict=True)), mixed),
             name="order_rows",
         )
     else:

time: 138 us -> 134 us (0.971)
  waiting for transfers between devices: 61.9 us -> 56.9 us
  local copies, waits for them, and re-layouts: 3.43 us -> 0.03 us
  starting transfers between devices: 54.5 us -> 57.5 us
  other arithmetic: 0 us -> 1.97 us
    ppermute x34, waiting for transfers between devices: 61.9 us -> 56.9 us  [swap(): return lax.ppermute(x, axis, [(i, i ^ mask) for i in range(size)])]
    unnamed x20 -> x14, local copies, waits for them, and re-layouts: 3.43 us -> 0.03 us
    ppermute x34, starting transfers between devices: 54.5 us -> 57.5 us  [swap(): return lax.ppermute(x, axis, [(i, i ^ mask) for i in range(size)])]
    concatenate x0 -> x1, other arithmetic: none -> 1.97 us  [body(): joined = jnp.concatenate(weights, axis=0)]
    pallas_call x11 -> x10, Pallas kernels: 16.7 us -> 16.6 us  [call(): pl.pallas_call(kernel, out_shape=tuple(outs), in_specs=[pl.BlockSpec(memo...]
where the time goes in v5:
time: 134 us
  starting transfers between devices  57.5 us (43%)
  waiting for transfers between devices  56.9 us (42%)
  Pallas kernels  16.6 us (12%)
  other arithmetic  1.97 us (1%)
    ppermute x34, starting transfers between devices, swap(): return lax.ppermute(x, axis, [(i, i ^ mask) for i in range(size)])  57.5 us
    ppermute x34, waiting for transfers between devices, swap(): return lax.ppermute(x, axis, [(i, i ^ mask) for i in range(size)])  56.9 us
    pallas_call x10, Pallas kernels, call(): pl.pallas_call(kernel, out_shape=tuple(outs), in_specs=[pl.BlockSpec(memo...  16.6 us
  transfers between devices with their start and end apart: 34, of which 10 were waited for; matrix products, arithmetic and copies ran while one was open for 0% of the time, Pallas kernels for 10%

profile of v5, /device:TPU:0, one launch (start us, length us, event | category | flops | bytes accessed | tf_op | source)
XLA Modules:
  0.0 133.7 jit_solution(6454806047147799615)
XLA Ops:
  0.7 2.0 %pad_maximum_fusion.refs_8_ = bf16[576,2048]{1,0:T(8,128)(2,1)S(1)} fusion(bf16[192,2048]{1,0:T(8,128)(2,1)} %bitcast.10, bf16[192,2048]{1,0:T(8,128)(2,1)} %bitcast.11, bf16[192,2048]{1,0:T(8,128)(2,1)} %bitcast.12), kind=kLoop, calls=%fused_computation | loop fusion | flops 7077888 | bytes 4718592 | tf_op jit(solution)/shard_map/concatenate | solution.py:286
  2.6 3.0 %collective-permute-start.7 = (bf16[576,2048]{1,0:T(8,128)(2,1)S(1)}, bf16[576,2048]{1,0:T(8,128)(2,1)S(1)}, u32[]{:S(2)}, u32[]{:S(2)}) collective-permute-start(bf16[576,2048]{1,0:T(8,128)(2,1)S(1)} %pad_maximum_fusion.refs_8_), channel_id=1, source_target_pairs={{0,2},{1,3},{2,0},{3,1},{4,6},{5,7},{6,4},{7,5},{8,10},{9,11},{10,... | collective-permute-start | bytes 7077896 | tf_op jit(solution)/shard_map/ppermute | solution.py:241
  6.5 2.7 %collective-permute-start = (bf16[64,2048]{1,0:T(8,128)(2,1)S(1)}, bf16[64,2048]{1,0:T(8,128)(2,1)S(1)}, u32[]{:S(2)}, u32[]{:S(2)}) collective-permute-start(bf16[64,2048]{1,0:T(8,128)(2,1)S(1)} %get-tuple-element.84), channel_id=1, source_target_pairs={{0,16},{4,20},{8,24},{12,28},{16,0},{20,4},{24,8},{28,12},{1,17},{... | collective-permute-start | bytes 786440 | tf_op jit(solution)/shard_map/ppermute | solution.py:241
  9.1 1.5 %collective-permute-start.1 = (bf16[64,2048]{1,0:T(8,128)(2,1)S(1)}, bf16[64,2048]{1,0:T(8,128)(2,1)S(1)}, u32[]{:S(2)}, u32[]{:S(2)}) collective-permute-start(bf16[64,2048]{1,0:T(8,128)(2,1)S(1)} %get-tuple-element.85), channel_id=1, source_target_pairs={{0,4},{4,0},{8,12},{12,8},{16,20},{20,16},{24,28},{28,24},{1,5},{5... | collective-permute-start | bytes 786440 | tf_op jit(solution)/shard_map/ppermute | solution.py:241
  10.7 1.6 %collective-permute-start.3 = (bf16[64,2048]{1,0:T(8,128)(2,1)S(1)}, bf16[64,2048]{1,0:T(8,128)(2,1)S(1)}, u32[]{:S(2)}, u32[]{:S(2)}) collective-permute-start(bf16[64,2048]{1,0:T(8,128)(2,1)S(1)} %get-tuple-element.87), channel_id=1, source_target_pairs={{0,8},{4,12},{8,0},{12,4},{16,24},{20,28},{24,16},{28,20},{1,9},{5... | collective-permute-start | bytes 786440 | tf_op jit(solution)/shard_map/ppermute | solution.py:241
  12.5 18.1 %collective-permute-done.refs_1_ = bf16[64,2048]{1,0:T(8,128)(2,1)S(1)} collective-permute-done((bf16[64,2048]{1,0:T(8,128)(2,1)S(1)}, bf16[64,2048]{1,0:T(8,128)(2,1)S(1)}, u32[]{:S(2)}, u32[]{:S(2)}) %collective-permute-start) | collective-permute-done | bytes 262176 | tf_op jit(solution)/shard_map/ppermute | solution.py:241
  30.6 4.8 %collective-permute-start.6 = (bf16[64,2048]{1,0:T(8,128)(2,1)S(1)}, bf16[64,2048]{1,0:T(8,128)(2,1)S(1)}, u32[]{:S(2)}, u32[]{:S(2)}) collective-permute-start(bf16[64,2048]{1,0:T(8,128)(2,1)S(1)} %get-tuple-element.91), channel_id=1, source_target_pairs={{0,28},{4,24},{8,20},{12,16},{16,12},{20,8},{24,4},{28,0},{1,29},{... | collective-permute-start | bytes 786440 | tf_op jit(solution)/shard_map/ppermute | solution.py:241
  35.4 10.1 %collective-permute-done.2.refs_3_ = bf16[64,2048]{1,0:T(8,128)(2,1)S(1)} collective-permute-done((bf16[64,2048]{1,0:T(8,128)(2,1)S(1)}, bf16[64,2048]{1,0:T(8,128)(2,1)S(1)}, u32[]{:S(2)}, u32[]{:S(2)}) %collective-permute-start.2) | collective-permute-done | bytes 262176 | tf_op jit(solution)/shard_map/ppermute | solution.py:241
  45.5 4.1 %collective-permute-done.5.refs_6_ = bf16[64,2048]{1,0:T(8,128)(2,1)S(1)} collective-permute-done((bf16[64,2048]{1,0:T(8,128)(2,1)S(1)}, bf16[64,2048]{1,0:T(8,128)(2,1)S(1)}, u32[]{:S(2)}, u32[]{:S(2)}) %collective-permute-start.5) | collective-permute-done | bytes 262176 | tf_op jit(solution)/shard_map/ppermute | solution.py:241
  49.6 7.2 %collective-permute-done.7.refs_8_ = bf16[576,2048]{1,0:T(8,128)(2,1)S(1)} collective-permute-done((bf16[576,2048]{1,0:T(8,128)(2,1)S(1)}, bf16[576,2048]{1,0:T(8,128)(2,1)S(1)}, u32[]{:S(2)}, u32[]{:S(2)}) %collective-permute-start.7) | collective-permute-done | bytes 2359328 | tf_op jit(solution)/shard_map/ppermute | solution.py:241
  56.9 3.1 %near_units.1 = (bf16[192,2048]{1,0:T(8,128)(2,1)S(1)}, bf16[192,2048]{1,0:T(8,128)(2,1)S(1)}, f32[256,2048]{1,0:T(8,128)S(1)}) custom-call(bf16[64,2048]{1,0:T(8,128)(2,1)S(1)} %get-tuple-element.83.refs_0_, bf16[64,2048]{1,0:T(8,128)(2,1)S(1)} %collective-permute-done.refs_1_, bf16[64,2048]{1,0:T(8,128)(2,1)S(1)} %collective-permute-done.1.refs_2_, ...), custom_call_target="tpu_custom_call" | custom-call | flops 2415919104 | bytes 10485760 | tf_op jit(solution)/shard_map/near_units/pallas_call | solution.py:29
  61.4 1.6 %far_units.1 = (bf16[192,2048]{1,0:T(8,128)(2,1)S(1)}, bf16[192,2048]{1,0:T(8,128)(2,1)S(1)}, f32[2,192,256]{2,1,0:T(8,128)S(1)}, f32[2,192,256]{2,1,0:T(8,128)S(1)}) custom-call(bf16[64,2048]{1,0:T(8,128)(2,1)S(1)} %get-tuple-element.83.refs_0_, bf16[64,2048]{1,0:T(8,128)(2,1)S(1)} %collective-permute-done.refs_1_, ...), custom_call_target="tpu_custom_call" | custom-call | flops 1207959552 | bytes 9175040 | tf_op jit(solution)/shard_map/far_units/pallas_call | solution.py:29
  63.2 2.1 %input_gradient.1 = (bf16[32,2048]{1,0:T(8,128)(2,1)S(1)}, bf16[32,2048]{1,0:T(8,128)(2,1)S(1)}, bf16[32,2048]{1,0:T(8,128)(2,1)S(1)}, bf16[32,2048]{1,0:T(8,128...) custom-call(bf16[64,2048]{1,0:T(8,128)(2,1)S(1)} %get-tuple-element., ...), custom_call_target="tpu_custom_call" | custom-call | flops 1207959552 | bytes 10747904 | tf_op jit(solution)/shard_map/input_gradient/pallas_call | solution.py:29
  65.6 1.8 %collective-permute-start.14 = (bf16[192,2048]{1,0:T(8,128)(2,1)S(1)}, bf16[192,2048]{1,0:T(8,128)(2,1)S(1)}, u32[]{:S(2)}, u32[]{:S(2)}) collective-permute-start(bf16[192,2048]{1,0:T(8,128)(2,1)S(1)} %add_pair.1), channel_id=1, source_target_pairs={{0,2},{1,3},{2,0},{3,1},{4,6},{5,7},{6,4},{7,5},{8,10},{9,11},{10,... | collective-permute-start | bytes 2359304 | tf_op jit(solution)/shard_map/ppermute | solution.py:241
  67.5 2.6 %collective-permute-start.11 = (bf16[32,2048]{1,0:T(8,128)(2,1)S(1)}, bf16[32,2048]{1,0:T(8,128)(2,1)S(1)}, u32[]{:S(2)}, u32[]{:S(2)}) collective-permute-start(bf16[32,2048]{1,0:T(8,128)(2,1)S(1)} %get-tuple-element.117), channel_id=1, source_target_pairs={{0,16},{4,20},{8,24},{12,28},{16,0},{20,4},{24,8},{28,12},{1,17},{... | collective-permute-start | bytes 393224 | tf_op jit(solution)/shard_map/ppermute | solution.py:241
  71.4 3.6 %collective-permute-start.13 = (bf16[32,2048]{1,0:T(8,128)(2,1)S(1)}, bf16[32,2048]{1,0:T(8,128)(2,1)S(1)}, u32[]{:S(2)}, u32[]{:S(2)}) collective-permute-start(bf16[32,2048]{1,0:T(8,128)(2,1)S(1)} %get-tuple-element.119), channel_id=1, source_target_pairs={{0,24},{4,28},{8,16},{12,20},{16,8},{20,12},{24,0},{28,4},{1,25},{... | collective-permute-start | bytes 393224 | tf_op jit(solution)/shard_map/ppermute | solution.py:241
  75.0 8.1 %collective-permute-done.11.refs_1_ = bf16[32,2048]{1,0:T(8,128)(2,1)S(1)} collective-permute-done((bf16[32,2048]{1,0:T(8,128)(2,1)S(1)}, bf16[32,2048]{1,0:T(8,128)(2,1)S(1)}, u32[]{:S(2)}, u32[]{:S(2)}) %collective-permute-start.11) | collective-permute-done | bytes 131104 | tf_op jit(solution)/shard_map/ppermute | solution.py:241
  83.2 3.8 %collective-permute-done.12.refs_2_ = bf16[32,2048]{1,0:T(8,128)(2,1)S(1)} collective-permute-done((bf16[32,2048]{1,0:T(8,128)(2,1)S(1)}, bf16[32,2048]{1,0:T(8,128)(2,1)S(1)}, u32[]{:S(2)}, u32[]{:S(2)}) %collective-permute-start.12) | collective-permute-done | bytes 131104 | tf_op jit(solution)/shard_map/ppermute | solution.py:241
  87.5 3.1 %collective-permute-start.19 = (bf16[24,2048]{1,0:T(8,128)(2,1)S(1)}, bf16[24,2048]{1,0:T(8,128)(2,1)S(1)}, u32[]{:S(2)}, u32[]{:S(2)}) collective-permute-start(bf16[24,2048]{1,0:T(8,128)(2,1)S(1)} %get-tuple-element.132), channel_id=1, source_target_pairs={{0,24},{4,28},{8,16},{12,20},{16,8},{20,12},{24,0},{28,4},{1,25},{... | collective-permute-start | bytes 294920 | tf_op jit(solution)/shard_map/ppermute | solution.py:241
  91.6 1.5 %collective-permute-start.22 = (bf16[24,2048]{1,0:T(8,128)(2,1)S(1)}, bf16[24,2048]{1,0:T(8,128)(2,1)S(1)}, u32[]{:S(2)}, u32[]{:S(2)}) collective-permute-start(bf16[24,2048]{1,0:T(8,128)(2,1)S(1)} %get-tuple-element.136), channel_id=1, source_target_pairs={{0,4},{4,0},{8,12},{12,8},{16,20},{20,16},{24,28},{28,24},{1,5},{5... | collective-permute-start | bytes 294920 | tf_op jit(solution)/shard_map/ppermute | solution.py:241
  93.6 1.5 %collective-permute-start.24 = (bf16[24,2048]{1,0:T(8,128)(2,1)S(1)}, bf16[24,2048]{1,0:T(8,128)(2,1)S(1)}, u32[]{:S(2)}, u32[]{:S(2)}) collective-permute-start(bf16[24,2048]{1,0:T(8,128)(2,1)S(1)} %get-tuple-element.138), channel_id=1, source_target_pairs={{0,12},{4,8},{8,4},{12,0},{16,28},{20,24},{24,20},{28,16},{1,13},{... | collective-permute-start | bytes 294920 | tf_op jit(solution)/shard_map/ppermute | solution.py:241
  95.1 5.7 %collective-permute-start.25 = (bf16[24,2048]{1,0:T(8,128)(2,1)S(1)}, bf16[24,2048]{1,0:T(8,128)(2,1)S(1)}, u32[]{:S(2)}, u32[]{:S(2)}) collective-permute-start(bf16[24,2048]{1,0:T(8,128)(2,1)S(1)} %get-tuple-element.139), channel_id=1, source_target_pairs={{0,20},{4,16},{8,28},{12,24},{16,4},{20,0},{24,12},{28,8},{1,21},{... | collective-permute-start | bytes 294920 | tf_op jit(solution)/shard_map/ppermute | solution.py:241
  100.8 3.1 %collective-permute-start.26 = (bf16[24,2048]{1,0:T(8,128)(2,1)S(1)}, bf16[24,2048]{1,0:T(8,128)(2,1)S(1)}, u32[]{:S(2)}, u32[]{:S(2)}) collective-permute-start(bf16[24,2048]{1,0:T(8,128)(2,1)S(1)} %get-tuple-element.141), channel_id=1, source_target_pairs={{0,28},{4,24},{8,20},{12,16},{16,12},{20,8},{24,4},{28,0},{1,29},{... | collective-permute-start | bytes 294920 | tf_op jit(solution)/shard_map/ppermute | solution.py:241
  105.1 2.2 %collective-permute-start.17 = (bf16[32,2048]{1,0:T(8,128)(2,1)S(1)}, bf16[32,2048]{1,0:T(8,128)(2,1)S(1)}, u32[]{:S(2)}, u32[]{:S(2)}) collective-permute-start(bf16[32,2048]{1,0:T(8,128)(2,1)S(1)} %get-tuple-element.127), channel_id=1, source_target_pairs={{0,12},{4,8},{8,4},{12,0},{16,28},{20,24},{24,20},{28,16},{1,13},{... | collective-permute-start | bytes 393224 | tf_op jit(solution)/shard_map/ppermute | solution.py:241
  107.8 2.1 %collective-permute-start.20 = (bf16[32,2048]{1,0:T(8,128)(2,1)S(1)}, bf16[32,2048]{1,0:T(8,128)(2,1)S(1)}, u32[]{:S(2)}, u32[]{:S(2)}) collective-permute-start(bf16[32,2048]{1,0:T(8,128)(2,1)S(1)} %get-tuple-element.133), channel_id=1, source_target_pairs={{0,28},{4,24},{8,20},{12,16},{16,12},{20,8},{24,4},{28,0},{1,29},{... | collective-permute-start | bytes 393224 | tf_op jit(solution)/shard_map/ppermute | solution.py:241
  109.9 2.4 %new_rows.1 = (bf16[24,2048]{1,0:T(8,128)(2,1)S(1)}, bf16[24,2048]{1,0:T(8,128)(2,1)S(1)}, bf16[24,2048]{1,0:T(8,128)(2,1)S(1)}, bf16[24,2048]{1,0:T(8,128)(2,1)...) custom-call(s32[8]{0:T(128)S(1)} %copy-done.6, ...), custom_call_target="tpu_custom_call" | custom-call | flops 2000000000 | bytes 5111840 | tf_op jit(solution)/shard_map/new_rows/pallas_call | solution.py:29
  112.3 1.7 %collective-permute-start.27 = (bf16[24,2048]{1,0:T(8,128)(2,1)S(1)}, bf16[24,2048]{1,0:T(8,128)(2,1)S(1)}, u32[]{:S(2)}, u32[]{:S(2)}) collective-permute-start(bf16[24,2048]{1,0:T(8,128)(2,1)S(1)} %get-tuple-element.152), channel_id=1, source_target_pairs={{0,16},{4,20},{8,24},{12,28},{16,0},{20,4},{24,8},{28,12},{1,17},{... | collective-permute-start | bytes 294920 | tf_op jit(solution)/shard_map/ppermute | solution.py:241
  114.1 2.3 %collective-permute-done.20.refs_7_ = bf16[32,2048]{1,0:T(8,128)(2,1)S(1)} collective-permute-done((bf16[32,2048]{1,0:T(8,128)(2,1)S(1)}, bf16[32,2048]{1,0:T(8,128)(2,1)S(1)}, u32[]{:S(2)}, u32[]{:S(2)}) %collective-permute-start.20) | collective-permute-done | bytes 131104 | tf_op jit(solution)/shard_map/ppermute | solution.py:241
  116.4 2.2 %collective-permute-start.28 = (bf16[24,2048]{1,0:T(8,128)(2,1)S(1)}, bf16[24,2048]{1,0:T(8,128)(2,1)S(1)}, u32[]{:S(2)}, u32[]{:S(2)}) collective-permute-start(bf16[24,2048]{1,0:T(8,128)(2,1)S(1)} %get-tuple-element.153), channel_id=1, source_target_pairs={{0,4},{4,0},{8,12},{12,8},{16,20},{20,16},{24,28},{28,24},{1,5},{5... | collective-permute-start | bytes 294920 | tf_op jit(solution)/shard_map/ppermute | solution.py:241
  118.6 4.0 %collective-permute-start.30 = (bf16[24,2048]{1,0:T(8,128)(2,1)S(1)}, bf16[24,2048]{1,0:T(8,128)(2,1)S(1)}, u32[]{:S(2)}, u32[]{:S(2)}) collective-permute-start(bf16[24,2048]{1,0:T(8,128)(2,1)S(1)} %get-tuple-element.155), channel_id=1, source_target_pairs={{0,8},{4,12},{8,0},{12,4},{16,24},{20,28},{24,16},{28,20},{1,9},{5... | collective-permute-start | bytes 294920 | tf_op jit(solution)/shard_map/ppermute | solution.py:241
  123.3 3.5 %collective-permute-start.33 = (bf16[24,2048]{1,0:T(8,128)(2,1)S(1)}, bf16[24,2048]{1,0:T(8,128)(2,1)S(1)}, u32[]{:S(2)}, u32[]{:S(2)}) collective-permute-start(bf16[24,2048]{1,0:T(8,128)(2,1)S(1)} %get-tuple-element.158), channel_id=1, source_target_pairs={{0,28},{4,24},{8,20},{12,16},{16,12},{20,8},{24,4},{28,0},{1,29},{... | collective-permute-start | bytes 294920 | tf_op jit(solution)/shard_map/ppermute | solution.py:241
  126.8 3.6 %new_state.1 = (f32[6,24,2048]{2,1,0:T(8,128)}, f32[6,24,2048]{2,1,0:T(8,128)}, f32[6,24,2048]{2,1,0:T(8,128)}) custom-call(s32[8]{0:T(128)S(1)} %copy-done.6, bf16[24,2048]{1,0:T(8,128)(2,1)S(1)} %get-tuple-element.134.refs_0_, bf16[24,2048]{1,0:T(8,128)(2,1)S(1)} %collective-permute-done.21.refs_1_, bf16[24,2048]{1,0:T(8,128)(2,1)S(1)} %collective-permute-done.22.refs_2_, ...), custom_call_target="tpu_custom_call" | custom-call | bytes 7864352 | tf_op jit(solution)/shard_map/new_state/pallas_call | solution.py:29
  (61 shorter events, 12.1 us)
Async XLA Ops:
  2.6 54.3 %collective-permute-start.7 = (bf16[576,2048]{1,0:T(8,128)(2,1)S(1)}, bf16[576,2048]{1,0:T(8,128)(2,1)S(1)}, u32[]{:S(2)}, u32[]{:S(2)}) collective-permute-start(bf16[576,2048]{1,0:T(8,128)(2,1)S(1)} %pad_maximum_fusion.refs_8_), channel_id=1, source_target_pairs={{0,2},{1,3},{2,0},{3,1},{4,6},{5,7},{6,4},{7,5},{8,10},{9,11},{10,... | collective-permute-start | bytes 7077896 | tf_op jit(solution)/shard_map/ppermute | solution.py:241
  6.5 24.1 %collective-permute-start = (bf16[64,2048]{1,0:T(8,128)(2,1)S(1)}, bf16[64,2048]{1,0:T(8,128)(2,1)S(1)}, u32[]{:S(2)}, u32[]{:S(2)}) collective-permute-start(bf16[64,2048]{1,0:T(8,128)(2,1)S(1)} %get-tuple-element.84), channel_id=1, source_target_pairs={{0,16},{4,20},{8,24},{12,28},{16,0},{20,4},{24,8},{28,12},{1,17},{... | collective-permute-start | bytes 786440 | tf_op jit(solution)/shard_map/ppermute | solution.py:241
  9.1 21.4 %collective-permute-start.1 = (bf16[64,2048]{1,0:T(8,128)(2,1)S(1)}, bf16[64,2048]{1,0:T(8,128)(2,1)S(1)}, u32[]{:S(2)}, u32[]{:S(2)}) collective-permute-start(bf16[64,2048]{1,0:T(8,128)(2,1)S(1)} %get-tuple-element.85), channel_id=1, source_target_pairs={{0,4},{4,0},{8,12},{12,8},{16,20},{20,16},{24,28},{28,24},{1,5},{5... | collective-permute-start | bytes 786440 | tf_op jit(solution)/shard_map/ppermute | solution.py:241
  10.7 19.9 %collective-permute-start.3 = (bf16[64,2048]{1,0:T(8,128)(2,1)S(1)}, bf16[64,2048]{1,0:T(8,128)(2,1)S(1)}, u32[]{:S(2)}, u32[]{:S(2)}) collective-permute-start(bf16[64,2048]{1,0:T(8,128)(2,1)S(1)} %get-tuple-element.87), channel_id=1, source_target_pairs={{0,8},{4,12},{8,0},{12,4},{16,24},{20,28},{24,16},{28,20},{1,9},{5... | collective-permute-start | bytes 786440 | tf_op jit(solution)/shard_map/ppermute | solution.py:241
  12.2 33.3 %collective-permute-start.2 = (bf16[64,2048]{1,0:T(8,128)(2,1)S(1)}, bf16[64,2048]{1,0:T(8,128)(2,1)S(1)}, u32[]{:S(2)}, u32[]{:S(2)}) collective-permute-start(bf16[64,2048]{1,0:T(8,128)(2,1)S(1)} %get-tuple-element.86), channel_id=1, source_target_pairs={{0,20},{4,16},{8,28},{12,24},{16,4},{20,0},{24,12},{28,8},{1,21},{... | collective-permute-start | bytes 786440 | tf_op jit(solution)/shard_map/ppermute | solution.py:241
  30.6 15.0 %collective-permute-start.4 = (bf16[64,2048]{1,0:T(8,128)(2,1)S(1)}, bf16[64,2048]{1,0:T(8,128)(2,1)S(1)}, u32[]{:S(2)}, u32[]{:S(2)}) collective-permute-start(bf16[64,2048]{1,0:T(8,128)(2,1)S(1)} %get-tuple-element.89), channel_id=1, source_target_pairs={{0,24},{4,28},{8,16},{12,20},{16,8},{20,12},{24,0},{28,4},{1,25},{... | collective-permute-start | bytes 786440 | tf_op jit(solution)/shard_map/ppermute | solution.py:241
  30.6 19.1 %collective-permute-start.5 = (bf16[64,2048]{1,0:T(8,128)(2,1)S(1)}, bf16[64,2048]{1,0:T(8,128)(2,1)S(1)}, u32[]{:S(2)}, u32[]{:S(2)}) collective-permute-start(bf16[64,2048]{1,0:T(8,128)(2,1)S(1)} %get-tuple-element.90), channel_id=1, source_target_pairs={{0,12},{4,8},{8,4},{12,0},{16,28},{20,24},{24,20},{28,16},{1,13},{... | collective-permute-start | bytes 786440 | tf_op jit(solution)/shard_map/ppermute | solution.py:241
  30.6 19.0 %collective-permute-start.6 = (bf16[64,2048]{1,0:T(8,128)(2,1)S(1)}, bf16[64,2048]{1,0:T(8,128)(2,1)S(1)}, u32[]{:S(2)}, u32[]{:S(2)}) collective-permute-start(bf16[64,2048]{1,0:T(8,128)(2,1)S(1)} %get-tuple-element.91), channel_id=1, source_target_pairs={{0,28},{4,24},{8,20},{12,16},{16,12},{20,8},{24,4},{28,0},{1,29},{... | collective-permute-start | bytes 786440 | tf_op jit(solution)/shard_map/ppermute | solution.py:241
  45.5 11.4 %collective-permute-start.9 = (bf16[576,2048]{1,0:T(8,128)(2,1)S(1)}, bf16[576,2048]{1,0:T(8,128)(2,1)S(1)}, u32[]{:S(2)}, u32[]{:S(2)}) collective-permute-start(bf16[576,2048]{1,0:T(8,128)(2,1)S(1)} %pad_maximum_fusion.refs_8_), channel_id=1, source_target_pairs={{0,1},{1,0},{2,3},{3,2},{4,5},{5,4},{6,7},{7,6},{8,9},{9,8},{10,11... | collective-permute-start | bytes 7077896 | tf_op jit(solution)/shard_map/ppermute | solution.py:241
  65.6 21.3 %collective-permute-start.14 = (bf16[192,2048]{1,0:T(8,128)(2,1)S(1)}, bf16[192,2048]{1,0:T(8,128)(2,1)S(1)}, u32[]{:S(2)}, u32[]{:S(2)}) collective-permute-start(bf16[192,2048]{1,0:T(8,128)(2,1)S(1)} %add_pair.1), channel_id=1, source_target_pairs={{0,2},{1,3},{2,0},{3,1},{4,6},{5,7},{6,4},{7,5},{8,10},{9,11},{10,... | collective-permute-start | bytes 2359304 | tf_op jit(solution)/shard_map/ppermute | solution.py:241
  67.5 19.5 %collective-permute-start.18 = (bf16[192,2048]{1,0:T(8,128)(2,1)S(1)}, bf16[192,2048]{1,0:T(8,128)(2,1)S(1)}, u32[]{:S(2)}, u32[]{:S(2)}) collective-permute-start(bf16[192,2048]{1,0:T(8,128)(2,1)S(1)} %get-tuple-element.130), channel_id=1, source_target_pairs={{0,1},{1,0},{2,3},{3,2},{4,5},{5,4},{6,7},{7,6},{8,9},{9,8},{10,11... | collective-permute-start | bytes 2359304 | tf_op jit(solution)/shard_map/ppermute | solution.py:241
  67.5 15.6 %collective-permute-start.11 = (bf16[32,2048]{1,0:T(8,128)(2,1)S(1)}, bf16[32,2048]{1,0:T(8,128)(2,1)S(1)}, u32[]{:S(2)}, u32[]{:S(2)}) collective-permute-start(bf16[32,2048]{1,0:T(8,128)(2,1)S(1)} %get-tuple-element.117), channel_id=1, source_target_pairs={{0,16},{4,20},{8,24},{12,28},{16,0},{20,4},{24,8},{28,12},{1,17},{... | collective-permute-start | bytes 393224 | tf_op jit(solution)/shard_map/ppermute | solution.py:241
  70.1 16.8 %collective-permute-start.12 = (bf16[32,2048]{1,0:T(8,128)(2,1)S(1)}, bf16[32,2048]{1,0:T(8,128)(2,1)S(1)}, u32[]{:S(2)}, u32[]{:S(2)}) collective-permute-start(bf16[32,2048]{1,0:T(8,128)(2,1)S(1)} %get-tuple-element.118), channel_id=1, source_target_pairs={{0,20},{4,16},{8,28},{12,24},{16,4},{20,0},{24,12},{28,8},{1,21},{... | collective-permute-start | bytes 393224 | tf_op jit(solution)/shard_map/ppermute | solution.py:241
  71.4 15.5 %collective-permute-start.13 = (bf16[32,2048]{1,0:T(8,128)(2,1)S(1)}, bf16[32,2048]{1,0:T(8,128)(2,1)S(1)}, u32[]{:S(2)}, u32[]{:S(2)}) collective-permute-start(bf16[32,2048]{1,0:T(8,128)(2,1)S(1)} %get-tuple-element.119), channel_id=1, source_target_pairs={{0,24},{4,28},{8,16},{12,20},{16,8},{20,12},{24,0},{28,4},{1,25},{... | collective-permute-start | bytes 393224 | tf_op jit(solution)/shard_map/ppermute | solution.py:241
  87.5 7.6 %collective-permute-start.19 = (bf16[24,2048]{1,0:T(8,128)(2,1)S(1)}, bf16[24,2048]{1,0:T(8,128)(2,1)S(1)}, u32[]{:S(2)}, u32[]{:S(2)}) collective-permute-start(bf16[24,2048]{1,0:T(8,128)(2,1)S(1)} %get-tuple-element.132), channel_id=1, source_target_pairs={{0,24},{4,28},{8,16},{12,20},{16,8},{20,12},{24,0},{28,4},{1,25},{... | collective-permute-start | bytes 294920 | tf_op jit(solution)/shard_map/ppermute | solution.py:241
  90.6 10.1 %collective-permute-start.21 = (bf16[24,2048]{1,0:T(8,128)(2,1)S(1)}, bf16[24,2048]{1,0:T(8,128)(2,1)S(1)}, u32[]{:S(2)}, u32[]{:S(2)}) collective-permute-start(bf16[24,2048]{1,0:T(8,128)(2,1)S(1)} %get-tuple-element.135), channel_id=1, source_target_pairs={{0,16},{4,20},{8,24},{12,28},{16,0},{20,4},{24,8},{28,12},{1,17},{... | collective-permute-start | bytes 294920 | tf_op jit(solution)/shard_map/ppermute | solution.py:241
  91.6 12.3 %collective-permute-start.22 = (bf16[24,2048]{1,0:T(8,128)(2,1)S(1)}, bf16[24,2048]{1,0:T(8,128)(2,1)S(1)}, u32[]{:S(2)}, u32[]{:S(2)}) collective-permute-start(bf16[24,2048]{1,0:T(8,128)(2,1)S(1)} %get-tuple-element.136), channel_id=1, source_target_pairs={{0,4},{4,0},{8,12},{12,8},{16,20},{20,16},{24,28},{28,24},{1,5},{5... | collective-permute-start | bytes 294920 | tf_op jit(solution)/shard_map/ppermute | solution.py:241
  93.1 12.0 %collective-permute-start.23 = (bf16[24,2048]{1,0:T(8,128)(2,1)S(1)}, bf16[24,2048]{1,0:T(8,128)(2,1)S(1)}, u32[]{:S(2)}, u32[]{:S(2)}) collective-permute-start(bf16[24,2048]{1,0:T(8,128)(2,1)S(1)} %get-tuple-element.137), channel_id=1, source_target_pairs={{0,8},{4,12},{8,0},{12,4},{16,24},{20,28},{24,16},{28,20},{1,9},{5... | collective-permute-start | bytes 294920 | tf_op jit(solution)/shard_map/ppermute | solution.py:241
  93.6 11.5 %collective-permute-start.24 = (bf16[24,2048]{1,0:T(8,128)(2,1)S(1)}, bf16[24,2048]{1,0:T(8,128)(2,1)S(1)}, u32[]{:S(2)}, u32[]{:S(2)}) collective-permute-start(bf16[24,2048]{1,0:T(8,128)(2,1)S(1)} %get-tuple-element.138), channel_id=1, source_target_pairs={{0,12},{4,8},{8,4},{12,0},{16,28},{20,24},{24,20},{28,16},{1,13},{... | collective-permute-start | bytes 294920 | tf_op jit(solution)/shard_map/ppermute | solution.py:241
  95.1 12.7 %collective-permute-start.25 = (bf16[24,2048]{1,0:T(8,128)(2,1)S(1)}, bf16[24,2048]{1,0:T(8,128)(2,1)S(1)}, u32[]{:S(2)}, u32[]{:S(2)}) collective-permute-start(bf16[24,2048]{1,0:T(8,128)(2,1)S(1)} %get-tuple-element.139), channel_id=1, source_target_pairs={{0,20},{4,16},{8,28},{12,24},{16,4},{20,0},{24,12},{28,8},{1,21},{... | collective-permute-start | bytes 294920 | tf_op jit(solution)/shard_map/ppermute | solution.py:241
  100.8 9.1 %collective-permute-start.26 = (bf16[24,2048]{1,0:T(8,128)(2,1)S(1)}, bf16[24,2048]{1,0:T(8,128)(2,1)S(1)}, u32[]{:S(2)}, u32[]{:S(2)}) collective-permute-start(bf16[24,2048]{1,0:T(8,128)(2,1)S(1)} %get-tuple-element.141), channel_id=1, source_target_pairs={{0,28},{4,24},{8,20},{12,16},{16,12},{20,8},{24,4},{28,0},{1,29},{... | collective-permute-start | bytes 294920 | tf_op jit(solution)/shard_map/ppermute | solution.py:241
  103.9 14.7 %collective-permute-start.15 = (bf16[32,2048]{1,0:T(8,128)(2,1)S(1)}, bf16[32,2048]{1,0:T(8,128)(2,1)S(1)}, u32[]{:S(2)}, u32[]{:S(2)}) collective-permute-start(bf16[32,2048]{1,0:T(8,128)(2,1)S(1)} %get-tuple-element.125), channel_id=1, source_target_pairs={{0,4},{4,0},{8,12},{12,8},{16,20},{20,16},{24,28},{28,24},{1,5},{5... | collective-permute-start | bytes 393224 | tf_op jit(solution)/shard_map/ppermute | solution.py:241
  105.1 13.5 %collective-permute-start.16 = (bf16[32,2048]{1,0:T(8,128)(2,1)S(1)}, bf16[32,2048]{1,0:T(8,128)(2,1)S(1)}, u32[]{:S(2)}, u32[]{:S(2)}) collective-permute-start(bf16[32,2048]{1,0:T(8,128)(2,1)S(1)} %get-tuple-element.126), channel_id=1, source_target_pairs={{0,8},{4,12},{8,0},{12,4},{16,24},{20,28},{24,16},{28,20},{1,9},{5... | collective-permute-start | bytes 393224 | tf_op jit(solution)/shard_map/ppermute | solution.py:241
  105.1 17.5 %collective-permute-start.17 = (bf16[32,2048]{1,0:T(8,128)(2,1)S(1)}, bf16[32,2048]{1,0:T(8,128)(2,1)S(1)}, u32[]{:S(2)}, u32[]{:S(2)}) collective-permute-start(bf16[32,2048]{1,0:T(8,128)(2,1)S(1)} %get-tuple-element.127), channel_id=1, source_target_pairs={{0,12},{4,8},{8,4},{12,0},{16,28},{20,24},{24,20},{28,16},{1,13},{... | collective-permute-start | bytes 393224 | tf_op jit(solution)/shard_map/ppermute | solution.py:241
  107.8 8.6 %collective-permute-start.20 = (bf16[32,2048]{1,0:T(8,128)(2,1)S(1)}, bf16[32,2048]{1,0:T(8,128)(2,1)S(1)}, u32[]{:S(2)}, u32[]{:S(2)}) collective-permute-start(bf16[32,2048]{1,0:T(8,128)(2,1)S(1)} %get-tuple-element.133), channel_id=1, source_target_pairs={{0,28},{4,24},{8,20},{12,16},{16,12},{20,8},{24,4},{28,0},{1,29},{... | collective-permute-start | bytes 393224 | tf_op jit(solution)/shard_map/ppermute | solution.py:241
  112.3 10.3 %collective-permute-start.27 = (bf16[24,2048]{1,0:T(8,128)(2,1)S(1)}, bf16[24,2048]{1,0:T(8,128)(2,1)S(1)}, u32[]{:S(2)}, u32[]{:S(2)}) collective-permute-start(bf16[24,2048]{1,0:T(8,128)(2,1)S(1)} %get-tuple-element.152), channel_id=1, source_target_pairs={{0,16},{4,20},{8,24},{12,28},{16,0},{20,4},{24,8},{28,12},{1,17},{... | collective-permute-start | bytes 294920 | tf_op jit(solution)/shard_map/ppermute | solution.py:241
  116.4 6.9 %collective-permute-start.28 = (bf16[24,2048]{1,0:T(8,128)(2,1)S(1)}, bf16[24,2048]{1,0:T(8,128)(2,1)S(1)}, u32[]{:S(2)}, u32[]{:S(2)}) collective-permute-start(bf16[24,2048]{1,0:T(8,128)(2,1)S(1)} %get-tuple-element.153), channel_id=1, source_target_pairs={{0,4},{4,0},{8,12},{12,8},{16,20},{20,16},{24,28},{28,24},{1,5},{5... | collective-permute-start | bytes 294920 | tf_op jit(solution)/shard_map/ppermute | solution.py:241
  118.6 12.9 %collective-permute-start.29 = (bf16[24,2048]{1,0:T(8,128)(2,1)S(1)}, bf16[24,2048]{1,0:T(8,128)(2,1)S(1)}, u32[]{:S(2)}, u32[]{:S(2)}) collective-permute-start(bf16[24,2048]{1,0:T(8,128)(2,1)S(1)} %get-tuple-element.154), channel_id=1, source_target_pairs={{0,20},{4,16},{8,28},{12,24},{16,4},{20,0},{24,12},{28,8},{1,21},{... | collective-permute-start | bytes 294920 | tf_op jit(solution)/shard_map/ppermute | solution.py:241
  118.6 12.9 %collective-permute-start.30 = (bf16[24,2048]{1,0:T(8,128)(2,1)S(1)}, bf16[24,2048]{1,0:T(8,128)(2,1)S(1)}, u32[]{:S(2)}, u32[]{:S(2)}) collective-permute-start(bf16[24,2048]{1,0:T(8,128)(2,1)S(1)} %get-tuple-element.155), channel_id=1, source_target_pairs={{0,8},{4,12},{8,0},{12,4},{16,24},{20,28},{24,16},{28,20},{1,9},{5... | collective-permute-start | bytes 294920 | tf_op jit(solution)/shard_map/ppermute | solution.py:241
  122.6 8.9 %collective-permute-start.31 = (bf16[24,2048]{1,0:T(8,128)(2,1)S(1)}, bf16[24,2048]{1,0:T(8,128)(2,1)S(1)}, u32[]{:S(2)}, u32[]{:S(2)}) collective-permute-start(bf16[24,2048]{1,0:T(8,128)(2,1)S(1)} %get-tuple-element.156), channel_id=1, source_target_pairs={{0,24},{4,28},{8,16},{12,20},{16,8},{20,12},{24,0},{28,4},{1,25},{... | collective-permute-start | bytes 294920 | tf_op jit(solution)/shard_map/ppermute | solution.py:241
  122.6 10.2 %collective-permute-start.32 = (bf16[24,2048]{1,0:T(8,128)(2,1)S(1)}, bf16[24,2048]{1,0:T(8,128)(2,1)S(1)}, u32[]{:S(2)}, u32[]{:S(2)}) collective-permute-start(bf16[24,2048]{1,0:T(8,128)(2,1)S(1)} %get-tuple-element.157), channel_id=1, source_target_pairs={{0,12},{4,8},{8,4},{12,0},{16,28},{20,24},{24,20},{28,16},{1,13},{... | collective-permute-start | bytes 294920 | tf_op jit(solution)/shard_map/ppermute | solution.py:241
  123.3 9.5 %collective-permute-start.33 = (bf16[24,2048]{1,0:T(8,128)(2,1)S(1)}, bf16[24,2048]{1,0:T(8,128)(2,1)S(1)}, u32[]{:S(2)}, u32[]{:S(2)}) collective-permute-start(bf16[24,2048]{1,0:T(8,128)(2,1)S(1)} %get-tuple-element.158), channel_id=1, source_target_pairs={{0,28},{4,24},{8,20},{12,16},{16,12},{20,8},{24,4},{28,0},{1,29},{... | collective-permute-start | bytes 294920 | tf_op jit(solution)/shard_map/ppermute | solution.py:241
  (9 other events, 199.8 us)

commit v6 on v5

--- a/solution.py
+++ b/solution.py
@@ -82,9 +82,16 @@
     return parts[0] if len(parts) == 1 else jnp.concatenate(parts, axis=0)
 
 
-def forward(weight, x):
-    part = weight.shape[0] // 3
-    both = dot(weight[: 2 * part], x, NT)
+def parted(weights, count):
+    if len(weights) == 2 * count:
+        return weights[:count], weights[count:]
+    part = weights[0].shape[0] // 3
+    return [w.at[: 2 * part] for w in weights], [w.at[2 * part :] for w in weights]
+
+
+def forward(high, x):
+    both = dot(high[...], x, NT)
+    part = both.shape[0] // 2
     gate, up = both[:part], both[part:]
     sig = jax.nn.sigmoid(gate)
     silu = gate * sig
@@ -100,18 +107,17 @@
             (send_ref if r % 2 else keep_ref)[rows, cols] = value
 
 
-def turn(weight, g, a, b):
-    part = weight.shape[0] // 3
-    dh = dot(weight[2 * part :], g, NT)
+def turn(low, g, a, b):
+    dh = dot(low[...], g, NT)
     both = jnp.concatenate(((dh * a).astype(BF16), (dh * b).astype(BF16)), axis=0)
     return both.T
 
 
-def input_gradient(turned, weights, cols):
-    wide = weights[0].shape[0] // 3 * 2
+def input_gradient(turned, highs, cols):
+    wide = highs[0].shape[0]
     total = None
-    for r, weight in enumerate(weights):
-        term = dot(turned[:, r * wide : (r + 1) * wide], weight[:wide, cols], NN)
+    for r, high in enumerate(highs):
+        term = dot(turned[:, r * wide : (r + 1) * wide], high[:, cols], NN)
         total = term if total is None else total + term
     return total
 
@@ -120,34 +126,35 @@
     blocks, weights = refs[:nb], refs[nb : nb + nw]
     send_ref, keep_ref, partial_ref, hidden, turned = refs[nb + nw :]
     x, g = halves(blocks, 0), halves(blocks, 1)
-    wide = weights[0].shape[0] // 3 * 2
+    highs, lows = parted(weights, nw)
+    wide = highs[0].shape[0]
     for r in range(nw):
-        hidden[r], a, b = forward(weights[r], x)
-        turned[:, r * wide : (r + 1) * wide] = turn(weights[r], g, a, b)
+        hidden[r], a, b = forward(highs[r], x)
+        turned[:, r * wide : (r + 1) * wide] = turn(lows[r], g, a, b)
     weight_gradient(hidden, g, send_ref, keep_ref)
     for cols in columns(g.shape[1]):
-        partial_ref[:, cols] = input_gradient(turned, weights, cols)
+        partial_ref[:, cols] = input_gradient(turned, highs, cols)
 
 
 def hidden_kernel(nb, nw, *refs):
-    blocks, weights = refs[:nb], refs[nb : nb + nw]
+    blocks, highs = refs[:nb], refs[nb : nb + nw]
     send_ref, keep_ref, a_ref, b_ref, hidden = refs[nb + nw :]
     x, g = halves(blocks, 0), halves(blocks, 1)
     for r in range(nw):
-        hidden[r], a_ref[r], b_ref[r] = forward(weights[r], x)
+        hidden[r], a_ref[r], b_ref[r] = forward(highs[r], x)
     weight_gradient(hidden, g, send_ref, keep_ref)
 
 
 def back_kernel(nb, nw, *refs):
-    blocks, weights = refs[:nb], refs[nb : nb + nw]
-    a_ref, b_ref, partial_ref = refs[nb + nw : nb + nw + 3]
-    outs, turned = refs[nb + nw + 3 : -1], refs[-1]
+    blocks, (highs, lows) = refs[:nb], parted(refs[nb : nb + 2 * nw], nw)
+    a_ref, b_ref, partial_ref = refs[nb + 2 * nw : nb + 2 * nw + 3]
+    outs, turned = refs[nb + 2 * nw + 3 : -1], refs[-1]
     g = halves(blocks, 1)
-    wide = weights[0].shape[0] // 3 * 2
+    wide = highs[0].shape[0]
     for r in range(nw):
-        turned[:, r * wide : (r + 1) * wide] = turn(weights[r], g, a_ref[r], b_ref[r])
+        turned[:, r * wide : (r + 1) * wide] = turn(lows[r], g, a_ref[r], b_ref[r])
     for cols in columns(g.shape[1]):
-        total = (partial_ref[:, cols] + input_gradient(turned, weights, cols)).astype(BF16)
+        total = (partial_ref[:, cols] + input_gradient(turned, highs, cols)).astype(BF16)
         start = 0
         for out in outs:
             out[:, cols] = total[start : start + out.shape[0]]
@@ -306,13 +313,11 @@
     for mask in [1 << i for i in range(1, m.bit_length() - 1)][::-1]:
         for r in sorted(held):
             held[r | mask] = swap(held[r], "slot", mask)
-    middle = nb // 2
-    neighbour, blocks[middle] = lax.optimization_barrier((joined, blocks[middle]))
-    near = [joined, swap(neighbour, "slot", 1)]
-    came, held = lax.optimization_barrier((blocks[1:], [held[r] for r in range(2, m, 2)]))
-    blocks[1:] = came
-    far = [w for v in held for w in (v, swap(v, "slot", 1))]
-    nf = len(far)
+    near = [joined, swap(joined, "slot", 1)]
+    blocks[1:], held = after(blocks[1:], [held[r] for r in range(2, m, 2)])
+    high = [w for v in held for w in (v[: 2 * part], swap(v[: 2 * part], "slot", 1))]
+    low = [w for v in held for w in (v[2 * part :], swap(v[2 * part :], "slot", 1))]
+    nf = len(high)
 
     send, kept, partial = call(
         functools.partial(near_kernel, nb, 2),
@@ -323,11 +328,11 @@
         flops=24 * rows * width * part,
     )
     first = [kept, swap(send, "slot", 1)]
-    far, partial = lax.optimization_barrier((far, partial))
+    high, partial = after(high, partial)
     send, keep, a, b = call(
         functools.partial(hidden_kernel, nb, nf),
         [shape((nf // 2 * part, width), BF16)] * 2 + [shape((nf, part, rows), F32)] * 2,
-        (*blocks, *far),
+        (*blocks, *high),
         scratch=[pltpu.VMEM((nf, part, rows), BF16)],
         name="far_units",
         flops=6 * rows * width * part * nf,
@@ -336,7 +341,7 @@
     dx = call(
         functools.partial(back_kernel, nb, nf),
         [shape((r.shape[0] // 2, width), BF16) for r in blocks],
-        (*blocks, *far, a, b, partial),
+        (*blocks, *high, *low, a, b, partial),
         scratch=[pltpu.VMEM((rows, nf * 2 * part), BF16)],
         name="input_gradient",
         flops=6 * rows * width * part * nf,

time: 134 us -> 132 us (0.985)
  waiting for transfers between devices: 56.9 us -> 53.3 us
    ppermute x34 -> x35, waiting for transfers between devices: 56.9 us -> 53.3 us  [swap(): return lax.ppermute(x, axis, [(i, i ^ mask) for i in range(size)])]
    ppermute x34 -> x35, starting transfers between devices: 57.5 us -> 58.8 us  [swap(): return lax.ppermute(x, axis, [(i, i ^ mask) for i in range(size)])]
  transfers between devices with their start and end apart: 34 -> 35, of which waited for: 10 -> 10; matrix products, arithmetic and copies ran while one was open for 0% -> 0% of each run, Pallas kernels for 10% -> 11%
where the time goes in v6:
time: 132 us
  starting transfers between devices  58.8 us (45%)
  waiting for transfers between devices  53.3 us (40%)
  Pallas kernels  16.5 us (12%)
  other arithmetic  1.97 us (1%)
    ppermute x35, starting transfers between devices, swap(): return lax.ppermute(x, axis, [(i, i ^ mask) for i in range(size)])  58.8 us
    ppermute x35, waiting for transfers between devices, swap(): return lax.ppermute(x, axis, [(i, i ^ mask) for i in range(size)])  53.3 us
    pallas_call x10, Pallas kernels, call(): pl.pallas_call(kernel, out_shape=tuple(outs), in_specs=[pl.BlockSpec(memo...  16.5 us
  transfers between devices with their start and end apart: 35, of which 10 were waited for; matrix products, arithmetic and copies ran while one was open for 0% of the time, Pallas kernels for 11%

profile of v6, /device:TPU:0, one launch (start us, length us, event | category | flops | bytes accessed | tf_op | source)
XLA Modules:
  0.0 131.7 jit_solution(13589601946587306137)
XLA Ops:
  0.7 2.0 %pad_maximum_fusion.refs_8_ = bf16[576,2048]{1,0:T(8,128)(2,1)S(1)} fusion(bf16[192,2048]{1,0:T(8,128)(2,1)} %bitcast.10, bf16[192,2048]{1,0:T(8,128)(2,1)} %bitcast.11, bf16[192,2048]{1,0:T(8,128)(2,1)} %bitcast.12), kind=kLoop, calls=%fused_computation | loop fusion | flops 7077888 | bytes 4718592 | tf_op jit(solution)/shard_map/concatenate | solution.py:293
  2.6 3.0 %collective-permute-start.7 = (bf16[576,2048]{1,0:T(8,128)(2,1)S(1)}, bf16[576,2048]{1,0:T(8,128)(2,1)S(1)}, u32[]{:S(2)}, u32[]{:S(2)}) collective-permute-start(bf16[576,2048]{1,0:T(8,128)(2,1)S(1)} %pad_maximum_fusion.refs_8_), channel_id=1, source_target_pairs={{0,2},{1,3},{2,0},{3,1},{4,6},{5,7},{6,4},{7,5},{8,10},{9,11},{10,... | collective-permute-start | bytes 7077896 | tf_op jit(solution)/shard_map/ppermute | solution.py:248
  6.5 2.7 %collective-permute-start = (bf16[64,2048]{1,0:T(8,128)(2,1)S(1)}, bf16[64,2048]{1,0:T(8,128)(2,1)S(1)}, u32[]{:S(2)}, u32[]{:S(2)}) collective-permute-start(bf16[64,2048]{1,0:T(8,128)(2,1)S(1)} %get-tuple-element.82), channel_id=1, source_target_pairs={{0,16},{4,20},{8,24},{12,28},{16,0},{20,4},{24,8},{28,12},{1,17},{... | collective-permute-start | bytes 786440 | tf_op jit(solution)/shard_map/ppermute | solution.py:248
  9.2 1.5 %collective-permute-start.1 = (bf16[64,2048]{1,0:T(8,128)(2,1)S(1)}, bf16[64,2048]{1,0:T(8,128)(2,1)S(1)}, u32[]{:S(2)}, u32[]{:S(2)}) collective-permute-start(bf16[64,2048]{1,0:T(8,128)(2,1)S(1)} %get-tuple-element.83), channel_id=1, source_target_pairs={{0,4},{4,0},{8,12},{12,8},{16,20},{20,16},{24,28},{28,24},{1,5},{5... | collective-permute-start | bytes 786440 | tf_op jit(solution)/shard_map/ppermute | solution.py:248
  11.0 16.8 %collective-permute-done.refs_1_ = bf16[64,2048]{1,0:T(8,128)(2,1)S(1)} collective-permute-done((bf16[64,2048]{1,0:T(8,128)(2,1)S(1)}, bf16[64,2048]{1,0:T(8,128)(2,1)S(1)}, u32[]{:S(2)}, u32[]{:S(2)}) %collective-permute-start) | collective-permute-done | bytes 262176 | tf_op jit(solution)/shard_map/ppermute | solution.py:248
  28.1 2.8 %collective-permute-start.4 = (bf16[64,2048]{1,0:T(8,128)(2,1)S(1)}, bf16[64,2048]{1,0:T(8,128)(2,1)S(1)}, u32[]{:S(2)}, u32[]{:S(2)}) collective-permute-start(bf16[64,2048]{1,0:T(8,128)(2,1)S(1)} %get-tuple-element.86), channel_id=1, source_target_pairs={{0,24},{4,28},{8,16},{12,20},{16,8},{20,12},{24,0},{28,4},{1,25},{... | collective-permute-start | bytes 786440 | tf_op jit(solution)/shard_map/ppermute | solution.py:248
  30.9 3.5 %collective-permute-done.2.refs_3_ = bf16[64,2048]{1,0:T(8,128)(2,1)S(1)} collective-permute-done((bf16[64,2048]{1,0:T(8,128)(2,1)S(1)}, bf16[64,2048]{1,0:T(8,128)(2,1)S(1)}, u32[]{:S(2)}, u32[]{:S(2)}) %collective-permute-start.2) | collective-permute-done | bytes 262176 | tf_op jit(solution)/shard_map/ppermute | solution.py:248
  34.7 9.6 %collective-permute-done.3.refs_4_ = bf16[64,2048]{1,0:T(8,128)(2,1)S(1)} collective-permute-done((bf16[64,2048]{1,0:T(8,128)(2,1)S(1)}, bf16[64,2048]{1,0:T(8,128)(2,1)S(1)}, u32[]{:S(2)}, u32[]{:S(2)}) %collective-permute-start.3) | collective-permute-done | bytes 262176 | tf_op jit(solution)/shard_map/ppermute | solution.py:248
  44.4 4.4 %collective-permute-start.6 = (bf16[64,2048]{1,0:T(8,128)(2,1)S(1)}, bf16[64,2048]{1,0:T(8,128)(2,1)S(1)}, u32[]{:S(2)}, u32[]{:S(2)}) collective-permute-start(bf16[64,2048]{1,0:T(8,128)(2,1)S(1)} %get-tuple-element.88), channel_id=1, source_target_pairs={{0,28},{4,24},{8,20},{12,16},{16,12},{20,8},{24,4},{28,0},{1,29},{... | collective-permute-start | bytes 786440 | tf_op jit(solution)/shard_map/ppermute | solution.py:248
  48.8 7.7 %collective-permute-done.5.refs_6_ = bf16[64,2048]{1,0:T(8,128)(2,1)S(1)} collective-permute-done((bf16[64,2048]{1,0:T(8,128)(2,1)S(1)}, bf16[64,2048]{1,0:T(8,128)(2,1)S(1)}, u32[]{:S(2)}, u32[]{:S(2)}) %collective-permute-start.5) | collective-permute-done | bytes 262176 | tf_op jit(solution)/shard_map/ppermute | solution.py:248
  57.8 3.1 %near_units.1 = (bf16[192,2048]{1,0:T(8,128)(2,1)S(1)}, bf16[192,2048]{1,0:T(8,128)(2,1)S(1)}, f32[256,2048]{1,0:T(8,128)S(1)}) custom-call(bf16[64,2048]{1,0:T(8,128)(2,1)S(1)} %get-tuple-element.81.refs_0_, bf16[64,2048]{1,0:T(8,128)(2,1)S(1)} %collective-permute-done.refs_1_, bf16[64,2048]{1,0:T(8,128)(2,1)S(1)} %collective-permute-done.1.refs_2_, ...), custom_call_target="tpu_custom_call" | custom-call | flops 2415919104 | bytes 10485760 | tf_op jit(solution)/shard_map/near_units/pallas_call | solution.py:29
  60.9 1.6 %far_units.1 = (bf16[192,2048]{1,0:T(8,128)(2,1)S(1)}, bf16[192,2048]{1,0:T(8,128)(2,1)S(1)}, f32[2,192,256]{2,1,0:T(8,128)S(1)}, f32[2,192,256]{2,1,0:T(8,128)S(1)}) custom-call(bf16[64,2048]{1,0:T(8,128)(2,1)S(1)} %get-tuple-element.81.refs_0_, bf16[64,2048]{1,0:T(8,128)(2,1)S(1)} %collective-permute-done.refs_1_, ...), custom_call_target="tpu_custom_call" | custom-call | flops 1207959552 | bytes 7602176 | tf_op jit(solution)/shard_map/far_units/pallas_call | solution.py:29
  62.6 2.1 %input_gradient.1 = (bf16[32,2048]{1,0:T(8,128)(2,1)S(1)}, bf16[32,2048]{1,0:T(8,128)(2,1)S(1)}, bf16[32,2048]{1,0:T(8,128)(2,1)S(1)}, bf16[32,2048]{1,0:T(8,128...) custom-call(bf16[64,2048]{1,0:T(8,128)(2,1)S(1)} %get-tuple-element., ...), custom_call_target="tpu_custom_call" | custom-call | flops 1207959552 | bytes 10747904 | tf_op jit(solution)/shard_map/input_gradient/pallas_call | solution.py:29
  65.1 1.8 %collective-permute-start.15 = (bf16[192,2048]{1,0:T(8,128)(2,1)S(1)}, bf16[192,2048]{1,0:T(8,128)(2,1)S(1)}, u32[]{:S(2)}, u32[]{:S(2)}) collective-permute-start(bf16[192,2048]{1,0:T(8,128)(2,1)S(1)} %add_pair.1), channel_id=1, source_target_pairs={{0,2},{1,3},{2,0},{3,1},{4,6},{5,7},{6,4},{7,5},{8,10},{9,11},{10,... | collective-permute-start | bytes 2359304 | tf_op jit(solution)/shard_map/ppermute | solution.py:248
  67.1 3.3 %collective-permute-start.12 = (bf16[32,2048]{1,0:T(8,128)(2,1)S(1)}, bf16[32,2048]{1,0:T(8,128)(2,1)S(1)}, u32[]{:S(2)}, u32[]{:S(2)}) collective-permute-start(bf16[32,2048]{1,0:T(8,128)(2,1)S(1)} %get-tuple-element.113), channel_id=1, source_target_pairs={{0,16},{4,20},{8,24},{12,28},{16,0},{20,4},{24,8},{28,12},{1,17},{... | collective-permute-start | bytes 393224 | tf_op jit(solution)/shard_map/ppermute | solution.py:248
  70.9 3.6 %collective-permute-start.14 = (bf16[32,2048]{1,0:T(8,128)(2,1)S(1)}, bf16[32,2048]{1,0:T(8,128)(2,1)S(1)}, u32[]{:S(2)}, u32[]{:S(2)}) collective-permute-start(bf16[32,2048]{1,0:T(8,128)(2,1)S(1)} %get-tuple-element.115), channel_id=1, source_target_pairs={{0,24},{4,28},{8,16},{12,20},{16,8},{20,12},{24,0},{28,4},{1,25},{... | collective-permute-start | bytes 393224 | tf_op jit(solution)/shard_map/ppermute | solution.py:248
  74.5 8.6 %collective-permute-done.12.refs_1_ = bf16[32,2048]{1,0:T(8,128)(2,1)S(1)} collective-permute-done((bf16[32,2048]{1,0:T(8,128)(2,1)S(1)}, bf16[32,2048]{1,0:T(8,128)(2,1)S(1)}, u32[]{:S(2)}, u32[]{:S(2)}) %collective-permute-start.12) | collective-permute-done | bytes 131104 | tf_op jit(solution)/shard_map/ppermute | solution.py:248
  83.2 3.3 %collective-permute-done.13.refs_2_ = bf16[32,2048]{1,0:T(8,128)(2,1)S(1)} collective-permute-done((bf16[32,2048]{1,0:T(8,128)(2,1)S(1)}, bf16[32,2048]{1,0:T(8,128)(2,1)S(1)}, u32[]{:S(2)}, u32[]{:S(2)}) %collective-permute-start.13) | collective-permute-done | bytes 131104 | tf_op jit(solution)/shard_map/ppermute | solution.py:248
  87.0 3.0 %collective-permute-start.20 = (bf16[24,2048]{1,0:T(8,128)(2,1)S(1)}, bf16[24,2048]{1,0:T(8,128)(2,1)S(1)}, u32[]{:S(2)}, u32[]{:S(2)}) collective-permute-start(bf16[24,2048]{1,0:T(8,128)(2,1)S(1)} %get-tuple-element.128), channel_id=1, source_target_pairs={{0,24},{4,28},{8,16},{12,20},{16,8},{20,12},{24,0},{28,4},{1,25},{... | collective-permute-start | bytes 294920 | tf_op jit(solution)/shard_map/ppermute | solution.py:248
  91.2 1.4 %collective-permute-start.23 = (bf16[24,2048]{1,0:T(8,128)(2,1)S(1)}, bf16[24,2048]{1,0:T(8,128)(2,1)S(1)}, u32[]{:S(2)}, u32[]{:S(2)}) collective-permute-start(bf16[24,2048]{1,0:T(8,128)(2,1)S(1)} %get-tuple-element.132), channel_id=1, source_target_pairs={{0,4},{4,0},{8,12},{12,8},{16,20},{20,16},{24,28},{28,24},{1,5},{5... | collective-permute-start | bytes 294920 | tf_op jit(solution)/shard_map/ppermute | solution.py:248
  93.1 1.6 %collective-permute-start.25 = (bf16[24,2048]{1,0:T(8,128)(2,1)S(1)}, bf16[24,2048]{1,0:T(8,128)(2,1)S(1)}, u32[]{:S(2)}, u32[]{:S(2)}) collective-permute-start(bf16[24,2048]{1,0:T(8,128)(2,1)S(1)} %get-tuple-element.134), channel_id=1, source_target_pairs={{0,12},{4,8},{8,4},{12,0},{16,28},{20,24},{24,20},{28,16},{1,13},{... | collective-permute-start | bytes 294920 | tf_op jit(solution)/shard_map/ppermute | solution.py:248
  94.7 5.8 %collective-permute-start.26 = (bf16[24,2048]{1,0:T(8,128)(2,1)S(1)}, bf16[24,2048]{1,0:T(8,128)(2,1)S(1)}, u32[]{:S(2)}, u32[]{:S(2)}) collective-permute-start(bf16[24,2048]{1,0:T(8,128)(2,1)S(1)} %get-tuple-element.135), channel_id=1, source_target_pairs={{0,20},{4,16},{8,28},{12,24},{16,4},{20,0},{24,12},{28,8},{1,21},{... | collective-permute-start | bytes 294920 | tf_op jit(solution)/shard_map/ppermute | solution.py:248
  100.5 3.1 %collective-permute-start.27 = (bf16[24,2048]{1,0:T(8,128)(2,1)S(1)}, bf16[24,2048]{1,0:T(8,128)(2,1)S(1)}, u32[]{:S(2)}, u32[]{:S(2)}) collective-permute-start(bf16[24,2048]{1,0:T(8,128)(2,1)S(1)} %get-tuple-element.137), channel_id=1, source_target_pairs={{0,28},{4,24},{8,20},{12,16},{16,12},{20,8},{24,4},{28,0},{1,29},{... | collective-permute-start | bytes 294920 | tf_op jit(solution)/shard_map/ppermute | solution.py:248
  104.6 2.4 %collective-permute-start.18 = (bf16[32,2048]{1,0:T(8,128)(2,1)S(1)}, bf16[32,2048]{1,0:T(8,128)(2,1)S(1)}, u32[]{:S(2)}, u32[]{:S(2)}) collective-permute-start(bf16[32,2048]{1,0:T(8,128)(2,1)S(1)} %get-tuple-element.123), channel_id=1, source_target_pairs={{0,12},{4,8},{8,4},{12,0},{16,28},{20,24},{24,20},{28,16},{1,13},{... | collective-permute-start | bytes 393224 | tf_op jit(solution)/shard_map/ppermute | solution.py:248
  107.1 2.2 %collective-permute-start.21 = (bf16[32,2048]{1,0:T(8,128)(2,1)S(1)}, bf16[32,2048]{1,0:T(8,128)(2,1)S(1)}, u32[]{:S(2)}, u32[]{:S(2)}) collective-permute-start(bf16[32,2048]{1,0:T(8,128)(2,1)S(1)} %get-tuple-element.129), channel_id=1, source_target_pairs={{0,28},{4,24},{8,20},{12,16},{16,12},{20,8},{24,4},{28,0},{1,29},{... | collective-permute-start | bytes 393224 | tf_op jit(solution)/shard_map/ppermute | solution.py:248
  109.3 2.4 %new_rows.1 = (bf16[24,2048]{1,0:T(8,128)(2,1)S(1)}, bf16[24,2048]{1,0:T(8,128)(2,1)S(1)}, bf16[24,2048]{1,0:T(8,128)(2,1)S(1)}, bf16[24,2048]{1,0:T(8,128)(2,1)...) custom-call(s32[8]{0:T(128)S(1)} %copy-done.6, ...), custom_call_target="tpu_custom_call" | custom-call | flops 2000000000 | bytes 5111840 | tf_op jit(solution)/shard_map/new_rows/pallas_call | solution.py:29
  111.8 2.2 %collective-permute-start.28 = (bf16[24,2048]{1,0:T(8,128)(2,1)S(1)}, bf16[24,2048]{1,0:T(8,128)(2,1)S(1)}, u32[]{:S(2)}, u32[]{:S(2)}) collective-permute-start(bf16[24,2048]{1,0:T(8,128)(2,1)S(1)} %get-tuple-element.148), channel_id=1, source_target_pairs={{0,16},{4,20},{8,24},{12,28},{16,0},{20,4},{24,8},{28,12},{1,17},{... | collective-permute-start | bytes 294920 | tf_op jit(solution)/shard_map/ppermute | solution.py:248
  113.9 2.6 %collective-permute-done.21.refs_7_ = bf16[32,2048]{1,0:T(8,128)(2,1)S(1)} collective-permute-done((bf16[32,2048]{1,0:T(8,128)(2,1)S(1)}, bf16[32,2048]{1,0:T(8,128)(2,1)S(1)}, u32[]{:S(2)}, u32[]{:S(2)}) %collective-permute-start.21) | collective-permute-done | bytes 131104 | tf_op jit(solution)/shard_map/ppermute | solution.py:248
  116.5 1.3 %collective-permute-start.29 = (bf16[24,2048]{1,0:T(8,128)(2,1)S(1)}, bf16[24,2048]{1,0:T(8,128)(2,1)S(1)}, u32[]{:S(2)}, u32[]{:S(2)}) collective-permute-start(bf16[24,2048]{1,0:T(8,128)(2,1)S(1)} %get-tuple-element.149), channel_id=1, source_target_pairs={{0,4},{4,0},{8,12},{12,8},{16,20},{20,16},{24,28},{28,24},{1,5},{5... | collective-permute-start | bytes 294920 | tf_op jit(solution)/shard_map/ppermute | solution.py:248
  117.9 3.2 %collective-permute-start.31 = (bf16[24,2048]{1,0:T(8,128)(2,1)S(1)}, bf16[24,2048]{1,0:T(8,128)(2,1)S(1)}, u32[]{:S(2)}, u32[]{:S(2)}) collective-permute-start(bf16[24,2048]{1,0:T(8,128)(2,1)S(1)} %get-tuple-element.151), channel_id=1, source_target_pairs={{0,8},{4,12},{8,0},{12,4},{16,24},{20,28},{24,16},{28,20},{1,9},{5... | collective-permute-start | bytes 294920 | tf_op jit(solution)/shard_map/ppermute | solution.py:248
  122.4 3.1 %collective-permute-start.34 = (bf16[24,2048]{1,0:T(8,128)(2,1)S(1)}, bf16[24,2048]{1,0:T(8,128)(2,1)S(1)}, u32[]{:S(2)}, u32[]{:S(2)}) collective-permute-start(bf16[24,2048]{1,0:T(8,128)(2,1)S(1)} %get-tuple-element.154), channel_id=1, source_target_pairs={{0,28},{4,24},{8,20},{12,16},{16,12},{20,8},{24,4},{28,0},{1,29},{... | collective-permute-start | bytes 294920 | tf_op jit(solution)/shard_map/ppermute | solution.py:248
  125.5 3.6 %new_state.1 = (f32[6,24,2048]{2,1,0:T(8,128)}, f32[6,24,2048]{2,1,0:T(8,128)}, f32[6,24,2048]{2,1,0:T(8,128)}) custom-call(s32[8]{0:T(128)S(1)} %copy-done.6, bf16[24,2048]{1,0:T(8,128)(2,1)S(1)} %get-tuple-element.130.refs_0_, bf16[24,2048]{1,0:T(8,128)(2,1)S(1)} %collective-permute-done.22.refs_1_, bf16[24,2048]{1,0:T(8,128)(2,1)S(1)} %collective-permute-done.23.refs_2_, ...), custom_call_target="tpu_custom_call" | custom-call | bytes 7864352 | tf_op jit(solution)/shard_map/new_state/pallas_call | solution.py:29
  (65 shorter events, 11.3 us)
Async XLA Ops:
  2.6 54.3 %collective-permute-start.7 = (bf16[576,2048]{1,0:T(8,128)(2,1)S(1)}, bf16[576,2048]{1,0:T(8,128)(2,1)S(1)}, u32[]{:S(2)}, u32[]{:S(2)}) collective-permute-start(bf16[576,2048]{1,0:T(8,128)(2,1)S(1)} %pad_maximum_fusion.refs_8_), channel_id=1, source_target_pairs={{0,2},{1,3},{2,0},{3,1},{4,6},{5,7},{6,4},{7,5},{8,10},{9,11},{10,... | collective-permute-start | bytes 7077896 | tf_op jit(solution)/shard_map/ppermute | solution.py:248
  5.6 52.1 %collective-permute-start.9 = (bf16[576,2048]{1,0:T(8,128)(2,1)S(1)}, bf16[576,2048]{1,0:T(8,128)(2,1)S(1)}, u32[]{:S(2)}, u32[]{:S(2)}) collective-permute-start(bf16[576,2048]{1,0:T(8,128)(2,1)S(1)} %pad_maximum_fusion.refs_8_), channel_id=1, source_target_pairs={{0,1},{1,0},{2,3},{3,2},{4,5},{5,4},{6,7},{7,6},{8,9},{9,8},{10,11... | collective-permute-start | bytes 7077896 | tf_op jit(solution)/shard_map/ppermute | solution.py:248
  6.5 21.3 %collective-permute-start = (bf16[64,2048]{1,0:T(8,128)(2,1)S(1)}, bf16[64,2048]{1,0:T(8,128)(2,1)S(1)}, u32[]{:S(2)}, u32[]{:S(2)}) collective-permute-start(bf16[64,2048]{1,0:T(8,128)(2,1)S(1)} %get-tuple-element.82), channel_id=1, source_target_pairs={{0,16},{4,20},{8,24},{12,28},{16,0},{20,4},{24,8},{28,12},{1,17},{... | collective-permute-start | bytes 786440 | tf_op jit(solution)/shard_map/ppermute | solution.py:248
  9.2 19.0 %collective-permute-start.1 = (bf16[64,2048]{1,0:T(8,128)(2,1)S(1)}, bf16[64,2048]{1,0:T(8,128)(2,1)S(1)}, u32[]{:S(2)}, u32[]{:S(2)}) collective-permute-start(bf16[64,2048]{1,0:T(8,128)(2,1)S(1)} %get-tuple-element.83), channel_id=1, source_target_pairs={{0,4},{4,0},{8,12},{12,8},{16,20},{20,16},{24,28},{28,24},{1,5},{5... | collective-permute-start | bytes 786440 | tf_op jit(solution)/shard_map/ppermute | solution.py:248
  10.7 23.7 %collective-permute-start.2 = (bf16[64,2048]{1,0:T(8,128)(2,1)S(1)}, bf16[64,2048]{1,0:T(8,128)(2,1)S(1)}, u32[]{:S(2)}, u32[]{:S(2)}) collective-permute-start(bf16[64,2048]{1,0:T(8,128)(2,1)S(1)} %get-tuple-element.84), channel_id=1, source_target_pairs={{0,20},{4,16},{8,28},{12,24},{16,4},{20,0},{24,12},{28,8},{1,21},{... | collective-permute-start | bytes 786440 | tf_op jit(solution)/shard_map/ppermute | solution.py:248
  27.8 16.6 %collective-permute-start.3 = (bf16[64,2048]{1,0:T(8,128)(2,1)S(1)}, bf16[64,2048]{1,0:T(8,128)(2,1)S(1)}, u32[]{:S(2)}, u32[]{:S(2)}) collective-permute-start(bf16[64,2048]{1,0:T(8,128)(2,1)S(1)} %get-tuple-element.85), channel_id=1, source_target_pairs={{0,8},{4,12},{8,0},{12,4},{16,24},{20,28},{24,16},{28,20},{1,9},{5... | collective-permute-start | bytes 786440 | tf_op jit(solution)/shard_map/ppermute | solution.py:248
  28.1 20.7 %collective-permute-start.4 = (bf16[64,2048]{1,0:T(8,128)(2,1)S(1)}, bf16[64,2048]{1,0:T(8,128)(2,1)S(1)}, u32[]{:S(2)}, u32[]{:S(2)}) collective-permute-start(bf16[64,2048]{1,0:T(8,128)(2,1)S(1)} %get-tuple-element.86), channel_id=1, source_target_pairs={{0,24},{4,28},{8,16},{12,20},{16,8},{20,12},{24,0},{28,4},{1,25},{... | collective-permute-start | bytes 786440 | tf_op jit(solution)/shard_map/ppermute | solution.py:248
  34.4 22.0 %collective-permute-start.5 = (bf16[64,2048]{1,0:T(8,128)(2,1)S(1)}, bf16[64,2048]{1,0:T(8,128)(2,1)S(1)}, u32[]{:S(2)}, u32[]{:S(2)}) collective-permute-start(bf16[64,2048]{1,0:T(8,128)(2,1)S(1)} %get-tuple-element.87), channel_id=1, source_target_pairs={{0,12},{4,8},{8,4},{12,0},{16,28},{20,24},{24,20},{28,16},{1,13},{... | collective-permute-start | bytes 786440 | tf_op jit(solution)/shard_map/ppermute | solution.py:248
  44.4 12.1 %collective-permute-start.6 = (bf16[64,2048]{1,0:T(8,128)(2,1)S(1)}, bf16[64,2048]{1,0:T(8,128)(2,1)S(1)}, u32[]{:S(2)}, u32[]{:S(2)}) collective-permute-start(bf16[64,2048]{1,0:T(8,128)(2,1)S(1)} %get-tuple-element.88), channel_id=1, source_target_pairs={{0,28},{4,24},{8,20},{12,16},{16,12},{20,8},{24,4},{28,0},{1,29},{... | collective-permute-start | bytes 786440 | tf_op jit(solution)/shard_map/ppermute | solution.py:248
  65.1 21.4 %collective-permute-start.15 = (bf16[192,2048]{1,0:T(8,128)(2,1)S(1)}, bf16[192,2048]{1,0:T(8,128)(2,1)S(1)}, u32[]{:S(2)}, u32[]{:S(2)}) collective-permute-start(bf16[192,2048]{1,0:T(8,128)(2,1)S(1)} %add_pair.1), channel_id=1, source_target_pairs={{0,2},{1,3},{2,0},{3,1},{4,6},{5,7},{6,4},{7,5},{8,10},{9,11},{10,... | collective-permute-start | bytes 2359304 | tf_op jit(solution)/shard_map/ppermute | solution.py:248
  66.9 19.6 %collective-permute-start.19 = (bf16[192,2048]{1,0:T(8,128)(2,1)S(1)}, bf16[192,2048]{1,0:T(8,128)(2,1)S(1)}, u32[]{:S(2)}, u32[]{:S(2)}) collective-permute-start(bf16[192,2048]{1,0:T(8,128)(2,1)S(1)} %get-tuple-element.126), channel_id=1, source_target_pairs={{0,1},{1,0},{2,3},{3,2},{4,5},{5,4},{6,7},{7,6},{8,9},{9,8},{10,11... | collective-permute-start | bytes 2359304 | tf_op jit(solution)/shard_map/ppermute | solution.py:248
  67.1 16.1 %collective-permute-start.12 = (bf16[32,2048]{1,0:T(8,128)(2,1)S(1)}, bf16[32,2048]{1,0:T(8,128)(2,1)S(1)}, u32[]{:S(2)}, u32[]{:S(2)}) collective-permute-start(bf16[32,2048]{1,0:T(8,128)(2,1)S(1)} %get-tuple-element.113), channel_id=1, source_target_pairs={{0,16},{4,20},{8,24},{12,28},{16,0},{20,4},{24,8},{28,12},{1,17},{... | collective-permute-start | bytes 393224 | tf_op jit(solution)/shard_map/ppermute | solution.py:248
  70.4 16.1 %collective-permute-start.13 = (bf16[32,2048]{1,0:T(8,128)(2,1)S(1)}, bf16[32,2048]{1,0:T(8,128)(2,1)S(1)}, u32[]{:S(2)}, u32[]{:S(2)}) collective-permute-start(bf16[32,2048]{1,0:T(8,128)(2,1)S(1)} %get-tuple-element.114), channel_id=1, source_target_pairs={{0,20},{4,16},{8,28},{12,24},{16,4},{20,0},{24,12},{28,8},{1,21},{... | collective-permute-start | bytes 393224 | tf_op jit(solution)/shard_map/ppermute | solution.py:248
  70.9 15.5 %collective-permute-start.14 = (bf16[32,2048]{1,0:T(8,128)(2,1)S(1)}, bf16[32,2048]{1,0:T(8,128)(2,1)S(1)}, u32[]{:S(2)}, u32[]{:S(2)}) collective-permute-start(bf16[32,2048]{1,0:T(8,128)(2,1)S(1)} %get-tuple-element.115), channel_id=1, source_target_pairs={{0,24},{4,28},{8,16},{12,20},{16,8},{20,12},{24,0},{28,4},{1,25},{... | collective-permute-start | bytes 393224 | tf_op jit(solution)/shard_map/ppermute | solution.py:248
  87.0 7.6 %collective-permute-start.20 = (bf16[24,2048]{1,0:T(8,128)(2,1)S(1)}, bf16[24,2048]{1,0:T(8,128)(2,1)S(1)}, u32[]{:S(2)}, u32[]{:S(2)}) collective-permute-start(bf16[24,2048]{1,0:T(8,128)(2,1)S(1)} %get-tuple-element.128), channel_id=1, source_target_pairs={{0,24},{4,28},{8,16},{12,20},{16,8},{20,12},{24,0},{28,4},{1,25},{... | collective-permute-start | bytes 294920 | tf_op jit(solution)/shard_map/ppermute | solution.py:248
  90.1 10.4 %collective-permute-start.22 = (bf16[24,2048]{1,0:T(8,128)(2,1)S(1)}, bf16[24,2048]{1,0:T(8,128)(2,1)S(1)}, u32[]{:S(2)}, u32[]{:S(2)}) collective-permute-start(bf16[24,2048]{1,0:T(8,128)(2,1)S(1)} %get-tuple-element.131), channel_id=1, source_target_pairs={{0,16},{4,20},{8,24},{12,28},{16,0},{20,4},{24,8},{28,12},{1,17},{... | collective-permute-start | bytes 294920 | tf_op jit(solution)/shard_map/ppermute | solution.py:248
  91.2 12.4 %collective-permute-start.23 = (bf16[24,2048]{1,0:T(8,128)(2,1)S(1)}, bf16[24,2048]{1,0:T(8,128)(2,1)S(1)}, u32[]{:S(2)}, u32[]{:S(2)}) collective-permute-start(bf16[24,2048]{1,0:T(8,128)(2,1)S(1)} %get-tuple-element.132), channel_id=1, source_target_pairs={{0,4},{4,0},{8,12},{12,8},{16,20},{20,16},{24,28},{28,24},{1,5},{5... | collective-permute-start | bytes 294920 | tf_op jit(solution)/shard_map/ppermute | solution.py:248
  92.6 12.0 %collective-permute-start.24 = (bf16[24,2048]{1,0:T(8,128)(2,1)S(1)}, bf16[24,2048]{1,0:T(8,128)(2,1)S(1)}, u32[]{:S(2)}, u32[]{:S(2)}) collective-permute-start(bf16[24,2048]{1,0:T(8,128)(2,1)S(1)} %get-tuple-element.133), channel_id=1, source_target_pairs={{0,8},{4,12},{8,0},{12,4},{16,24},{20,28},{24,16},{28,20},{1,9},{5... | collective-permute-start | bytes 294920 | tf_op jit(solution)/shard_map/ppermute | solution.py:248
  93.1 11.6 %collective-permute-start.25 = (bf16[24,2048]{1,0:T(8,128)(2,1)S(1)}, bf16[24,2048]{1,0:T(8,128)(2,1)S(1)}, u32[]{:S(2)}, u32[]{:S(2)}) collective-permute-start(bf16[24,2048]{1,0:T(8,128)(2,1)S(1)} %get-tuple-element.134), channel_id=1, source_target_pairs={{0,12},{4,8},{8,4},{12,0},{16,28},{20,24},{24,20},{28,16},{1,13},{... | collective-permute-start | bytes 294920 | tf_op jit(solution)/shard_map/ppermute | solution.py:248
  94.7 12.4 %collective-permute-start.26 = (bf16[24,2048]{1,0:T(8,128)(2,1)S(1)}, bf16[24,2048]{1,0:T(8,128)(2,1)S(1)}, u32[]{:S(2)}, u32[]{:S(2)}) collective-permute-start(bf16[24,2048]{1,0:T(8,128)(2,1)S(1)} %get-tuple-element.135), channel_id=1, source_target_pairs={{0,20},{4,16},{8,28},{12,24},{16,4},{20,0},{24,12},{28,8},{1,21},{... | collective-permute-start | bytes 294920 | tf_op jit(solution)/shard_map/ppermute | solution.py:248
  100.5 8.9 %collective-permute-start.27 = (bf16[24,2048]{1,0:T(8,128)(2,1)S(1)}, bf16[24,2048]{1,0:T(8,128)(2,1)S(1)}, u32[]{:S(2)}, u32[]{:S(2)}) collective-permute-start(bf16[24,2048]{1,0:T(8,128)(2,1)S(1)} %get-tuple-element.137), channel_id=1, source_target_pairs={{0,28},{4,24},{8,20},{12,16},{16,12},{20,8},{24,4},{28,0},{1,29},{... | collective-permute-start | bytes 294920 | tf_op jit(solution)/shard_map/ppermute | solution.py:248
  103.6 14.3 %collective-permute-start.16 = (bf16[32,2048]{1,0:T(8,128)(2,1)S(1)}, bf16[32,2048]{1,0:T(8,128)(2,1)S(1)}, u32[]{:S(2)}, u32[]{:S(2)}) collective-permute-start(bf16[32,2048]{1,0:T(8,128)(2,1)S(1)} %get-tuple-element.121), channel_id=1, source_target_pairs={{0,4},{4,0},{8,12},{12,8},{16,20},{20,16},{24,28},{28,24},{1,5},{5... | collective-permute-start | bytes 393224 | tf_op jit(solution)/shard_map/ppermute | solution.py:248
  104.6 13.3 %collective-permute-start.17 = (bf16[32,2048]{1,0:T(8,128)(2,1)S(1)}, bf16[32,2048]{1,0:T(8,128)(2,1)S(1)}, u32[]{:S(2)}, u32[]{:S(2)}) collective-permute-start(bf16[32,2048]{1,0:T(8,128)(2,1)S(1)} %get-tuple-element.122), channel_id=1, source_target_pairs={{0,8},{4,12},{8,0},{12,4},{16,24},{20,28},{24,16},{28,20},{1,9},{5... | collective-permute-start | bytes 393224 | tf_op jit(solution)/shard_map/ppermute | solution.py:248
  104.6 16.5 %collective-permute-start.18 = (bf16[32,2048]{1,0:T(8,128)(2,1)S(1)}, bf16[32,2048]{1,0:T(8,128)(2,1)S(1)}, u32[]{:S(2)}, u32[]{:S(2)}) collective-permute-start(bf16[32,2048]{1,0:T(8,128)(2,1)S(1)} %get-tuple-element.123), channel_id=1, source_target_pairs={{0,12},{4,8},{8,4},{12,0},{16,28},{20,24},{24,20},{28,16},{1,13},{... | collective-permute-start | bytes 393224 | tf_op jit(solution)/shard_map/ppermute | solution.py:248
  107.1 9.5 %collective-permute-start.21 = (bf16[32,2048]{1,0:T(8,128)(2,1)S(1)}, bf16[32,2048]{1,0:T(8,128)(2,1)S(1)}, u32[]{:S(2)}, u32[]{:S(2)}) collective-permute-start(bf16[32,2048]{1,0:T(8,128)(2,1)S(1)} %get-tuple-element.129), channel_id=1, source_target_pairs={{0,28},{4,24},{8,20},{12,16},{16,12},{20,8},{24,4},{28,0},{1,29},{... | collective-permute-start | bytes 393224 | tf_op jit(solution)/shard_map/ppermute | solution.py:248
  111.8 10.6 %collective-permute-start.28 = (bf16[24,2048]{1,0:T(8,128)(2,1)S(1)}, bf16[24,2048]{1,0:T(8,128)(2,1)S(1)}, u32[]{:S(2)}, u32[]{:S(2)}) collective-permute-start(bf16[24,2048]{1,0:T(8,128)(2,1)S(1)} %get-tuple-element.148), channel_id=1, source_target_pairs={{0,16},{4,20},{8,24},{12,28},{16,0},{20,4},{24,8},{28,12},{1,17},{... | collective-permute-start | bytes 294920 | tf_op jit(solution)/shard_map/ppermute | solution.py:248
  116.5 5.9 %collective-permute-start.29 = (bf16[24,2048]{1,0:T(8,128)(2,1)S(1)}, bf16[24,2048]{1,0:T(8,128)(2,1)S(1)}, u32[]{:S(2)}, u32[]{:S(2)}) collective-permute-start(bf16[24,2048]{1,0:T(8,128)(2,1)S(1)} %get-tuple-element.149), channel_id=1, source_target_pairs={{0,4},{4,0},{8,12},{12,8},{16,20},{20,16},{24,28},{28,24},{1,5},{5... | collective-permute-start | bytes 294920 | tf_op jit(solution)/shard_map/ppermute | solution.py:248
  117.9 12.3 %collective-permute-start.30 = (bf16[24,2048]{1,0:T(8,128)(2,1)S(1)}, bf16[24,2048]{1,0:T(8,128)(2,1)S(1)}, u32[]{:S(2)}, u32[]{:S(2)}) collective-permute-start(bf16[24,2048]{1,0:T(8,128)(2,1)S(1)} %get-tuple-element.150), channel_id=1, source_target_pairs={{0,20},{4,16},{8,28},{12,24},{16,4},{20,0},{24,12},{28,8},{1,21},{... | collective-permute-start | bytes 294920 | tf_op jit(solution)/shard_map/ppermute | solution.py:248
  117.9 12.3 %collective-permute-start.31 = (bf16[24,2048]{1,0:T(8,128)(2,1)S(1)}, bf16[24,2048]{1,0:T(8,128)(2,1)S(1)}, u32[]{:S(2)}, u32[]{:S(2)}) collective-permute-start(bf16[24,2048]{1,0:T(8,128)(2,1)S(1)} %get-tuple-element.151), channel_id=1, source_target_pairs={{0,8},{4,12},{8,0},{12,4},{16,24},{20,28},{24,16},{28,20},{1,9},{5... | collective-permute-start | bytes 294920 | tf_op jit(solution)/shard_map/ppermute | solution.py:248
  121.1 9.1 %collective-permute-start.32 = (bf16[24,2048]{1,0:T(8,128)(2,1)S(1)}, bf16[24,2048]{1,0:T(8,128)(2,1)S(1)}, u32[]{:S(2)}, u32[]{:S(2)}) collective-permute-start(bf16[24,2048]{1,0:T(8,128)(2,1)S(1)} %get-tuple-element.152), channel_id=1, source_target_pairs={{0,24},{4,28},{8,16},{12,20},{16,8},{20,12},{24,0},{28,4},{1,25},{... | collective-permute-start | bytes 294920 | tf_op jit(solution)/shard_map/ppermute | solution.py:248
  122.4 8.3 %collective-permute-start.33 = (bf16[24,2048]{1,0:T(8,128)(2,1)S(1)}, bf16[24,2048]{1,0:T(8,128)(2,1)S(1)}, u32[]{:S(2)}, u32[]{:S(2)}) collective-permute-start(bf16[24,2048]{1,0:T(8,128)(2,1)S(1)} %get-tuple-element.153), channel_id=1, source_target_pairs={{0,12},{4,8},{8,4},{12,0},{16,28},{20,24},{24,20},{28,16},{1,13},{... | collective-permute-start | bytes 294920 | tf_op jit(solution)/shard_map/ppermute | solution.py:248
  122.4 8.3 %collective-permute-start.34 = (bf16[24,2048]{1,0:T(8,128)(2,1)S(1)}, bf16[24,2048]{1,0:T(8,128)(2,1)S(1)}, u32[]{:S(2)}, u32[]{:S(2)}) collective-permute-start(bf16[24,2048]{1,0:T(8,128)(2,1)S(1)} %get-tuple-element.154), channel_id=1, source_target_pairs={{0,28},{4,24},{8,20},{12,16},{16,12},{20,8},{24,4},{28,0},{1,29},{... | collective-permute-start | bytes 294920 | tf_op jit(solution)/shard_map/ppermute | solution.py:248
  (10 other events, 204.4 us)

commit v7 on v6

--- a/solution.py
+++ b/solution.py
@@ -12,7 +12,7 @@
 NT = (((1,), (1,)), ((), ()))
 TN = (((0,), (0,)), ((), ()))
 NN = (((1,), (0,)), ((), ()))
-COLUMNS = 512
+COLUMNS = 1024
 PIECES = 6
 OUT = 3
 NEWFLOPS = 2 * 10**9

time: 132 us -> 132 us (level)
  no operation moved by 1% of the time
where the time goes in v7:
time: 132 us
  starting transfers between devices  58.8 us (45%)
  waiting for transfers between devices  53.3 us (40%)
  Pallas kernels  16.5 us (12%)
  other arithmetic  1.97 us (1%)
    ppermute x35, starting transfers between devices, swap(): return lax.ppermute(x, axis, [(i, i ^ mask) for i in range(size)])  58.8 us
    ppermute x35, waiting for transfers between devices, swap(): return lax.ppermute(x, axis, [(i, i ^ mask) for i in range(size)])  53.3 us
    pallas_call x10, Pallas kernels, call(): pl.pallas_call(kernel, out_shape=tuple(outs), in_specs=[pl.BlockSpec(memo...  16.5 us
  transfers between devices with their start and end apart: 35, of which 10 were waited for; matrix products, arithmetic and copies ran while one was open for 0% of the time, Pallas kernels for 11%

profile of v7, /device:TPU:0, one launch (start us, length us, event | category | flops | bytes accessed | tf_op | source)
XLA Modules:
  0.0 131.7 jit_solution(17725701558596941643)
XLA Ops:
  0.7 2.0 %pad_maximum_fusion.refs_8_ = bf16[576,2048]{1,0:T(8,128)(2,1)S(1)} fusion(bf16[192,2048]{1,0:T(8,128)(2,1)} %bitcast.10, bf16[192,2048]{1,0:T(8,128)(2,1)} %bitcast.11, bf16[192,2048]{1,0:T(8,128)(2,1)} %bitcast.12), kind=kLoop, calls=%fused_computation | loop fusion | flops 7077888 | bytes 4718592 | tf_op jit(solution)/shard_map/concatenate | solution.py:293
  2.6 3.0 %collective-permute-start.7 = (bf16[576,2048]{1,0:T(8,128)(2,1)S(1)}, bf16[576,2048]{1,0:T(8,128)(2,1)S(1)}, u32[]{:S(2)}, u32[]{:S(2)}) collective-permute-start(bf16[576,2048]{1,0:T(8,128)(2,1)S(1)} %pad_maximum_fusion.refs_8_), channel_id=1, source_target_pairs={{0,2},{1,3},{2,0},{3,1},{4,6},{5,7},{6,4},{7,5},{8,10},{9,11},{10,... | collective-permute-start | bytes 7077896 | tf_op jit(solution)/shard_map/ppermute | solution.py:248
  6.5 2.7 %collective-permute-start = (bf16[64,2048]{1,0:T(8,128)(2,1)S(1)}, bf16[64,2048]{1,0:T(8,128)(2,1)S(1)}, u32[]{:S(2)}, u32[]{:S(2)}) collective-permute-start(bf16[64,2048]{1,0:T(8,128)(2,1)S(1)} %get-tuple-element.82), channel_id=1, source_target_pairs={{0,16},{4,20},{8,24},{12,28},{16,0},{20,4},{24,8},{28,12},{1,17},{... | collective-permute-start | bytes 786440 | tf_op jit(solution)/shard_map/ppermute | solution.py:248
  9.2 1.5 %collective-permute-start.1 = (bf16[64,2048]{1,0:T(8,128)(2,1)S(1)}, bf16[64,2048]{1,0:T(8,128)(2,1)S(1)}, u32[]{:S(2)}, u32[]{:S(2)}) collective-permute-start(bf16[64,2048]{1,0:T(8,128)(2,1)S(1)} %get-tuple-element.83), channel_id=1, source_target_pairs={{0,4},{4,0},{8,12},{12,8},{16,20},{20,16},{24,28},{28,24},{1,5},{5... | collective-permute-start | bytes 786440 | tf_op jit(solution)/shard_map/ppermute | solution.py:248
  11.0 16.8 %collective-permute-done.refs_1_ = bf16[64,2048]{1,0:T(8,128)(2,1)S(1)} collective-permute-done((bf16[64,2048]{1,0:T(8,128)(2,1)S(1)}, bf16[64,2048]{1,0:T(8,128)(2,1)S(1)}, u32[]{:S(2)}, u32[]{:S(2)}) %collective-permute-start) | collective-permute-done | bytes 262176 | tf_op jit(solution)/shard_map/ppermute | solution.py:248
  28.1 2.8 %collective-permute-start.4 = (bf16[64,2048]{1,0:T(8,128)(2,1)S(1)}, bf16[64,2048]{1,0:T(8,128)(2,1)S(1)}, u32[]{:S(2)}, u32[]{:S(2)}) collective-permute-start(bf16[64,2048]{1,0:T(8,128)(2,1)S(1)} %get-tuple-element.86), channel_id=1, source_target_pairs={{0,24},{4,28},{8,16},{12,20},{16,8},{20,12},{24,0},{28,4},{1,25},{... | collective-permute-start | bytes 786440 | tf_op jit(solution)/shard_map/ppermute | solution.py:248
  30.9 3.5 %collective-permute-done.2.refs_3_ = bf16[64,2048]{1,0:T(8,128)(2,1)S(1)} collective-permute-done((bf16[64,2048]{1,0:T(8,128)(2,1)S(1)}, bf16[64,2048]{1,0:T(8,128)(2,1)S(1)}, u32[]{:S(2)}, u32[]{:S(2)}) %collective-permute-start.2) | collective-permute-done | bytes 262176 | tf_op jit(solution)/shard_map/ppermute | solution.py:248
  34.7 9.6 %collective-permute-done.3.refs_4_ = bf16[64,2048]{1,0:T(8,128)(2,1)S(1)} collective-permute-done((bf16[64,2048]{1,0:T(8,128)(2,1)S(1)}, bf16[64,2048]{1,0:T(8,128)(2,1)S(1)}, u32[]{:S(2)}, u32[]{:S(2)}) %collective-permute-start.3) | collective-permute-done | bytes 262176 | tf_op jit(solution)/shard_map/ppermute | solution.py:248
  44.4 4.4 %collective-permute-start.6 = (bf16[64,2048]{1,0:T(8,128)(2,1)S(1)}, bf16[64,2048]{1,0:T(8,128)(2,1)S(1)}, u32[]{:S(2)}, u32[]{:S(2)}) collective-permute-start(bf16[64,2048]{1,0:T(8,128)(2,1)S(1)} %get-tuple-element.88), channel_id=1, source_target_pairs={{0,28},{4,24},{8,20},{12,16},{16,12},{20,8},{24,4},{28,0},{1,29},{... | collective-permute-start | bytes 786440 | tf_op jit(solution)/shard_map/ppermute | solution.py:248
  48.8 7.7 %collective-permute-done.5.refs_6_ = bf16[64,2048]{1,0:T(8,128)(2,1)S(1)} collective-permute-done((bf16[64,2048]{1,0:T(8,128)(2,1)S(1)}, bf16[64,2048]{1,0:T(8,128)(2,1)S(1)}, u32[]{:S(2)}, u32[]{:S(2)}) %collective-permute-start.5) | collective-permute-done | bytes 262176 | tf_op jit(solution)/shard_map/ppermute | solution.py:248
  57.8 3.1 %near_units.1 = (bf16[192,2048]{1,0:T(8,128)(2,1)S(1)}, bf16[192,2048]{1,0:T(8,128)(2,1)S(1)}, f32[256,2048]{1,0:T(8,128)S(1)}) custom-call(bf16[64,2048]{1,0:T(8,128)(2,1)S(1)} %get-tuple-element.81.refs_0_, bf16[64,2048]{1,0:T(8,128)(2,1)S(1)} %collective-permute-done.refs_1_, bf16[64,2048]{1,0:T(8,128)(2,1)S(1)} %collective-permute-done.1.refs_2_, ...), custom_call_target="tpu_custom_call" | custom-call | flops 2415919104 | bytes 10485760 | tf_op jit(solution)/shard_map/near_units/pallas_call | solution.py:29
  60.9 1.6 %far_units.1 = (bf16[192,2048]{1,0:T(8,128)(2,1)S(1)}, bf16[192,2048]{1,0:T(8,128)(2,1)S(1)}, f32[2,192,256]{2,1,0:T(8,128)S(1)}, f32[2,192,256]{2,1,0:T(8,128)S(1)}) custom-call(bf16[64,2048]{1,0:T(8,128)(2,1)S(1)} %get-tuple-element.81.refs_0_, bf16[64,2048]{1,0:T(8,128)(2,1)S(1)} %collective-permute-done.refs_1_, ...), custom_call_target="tpu_custom_call" | custom-call | flops 1207959552 | bytes 7602176 | tf_op jit(solution)/shard_map/far_units/pallas_call | solution.py:29
  62.6 2.1 %input_gradient.1 = (bf16[32,2048]{1,0:T(8,128)(2,1)S(1)}, bf16[32,2048]{1,0:T(8,128)(2,1)S(1)}, bf16[32,2048]{1,0:T(8,128)(2,1)S(1)}, bf16[32,2048]{1,0:T(8,128...) custom-call(bf16[64,2048]{1,0:T(8,128)(2,1)S(1)} %get-tuple-element., ...), custom_call_target="tpu_custom_call" | custom-call | flops 1207959552 | bytes 10747904 | tf_op jit(solution)/shard_map/input_gradient/pallas_call | solution.py:29
  65.1 1.8 %collective-permute-start.15 = (bf16[192,2048]{1,0:T(8,128)(2,1)S(1)}, bf16[192,2048]{1,0:T(8,128)(2,1)S(1)}, u32[]{:S(2)}, u32[]{:S(2)}) collective-permute-start(bf16[192,2048]{1,0:T(8,128)(2,1)S(1)} %add_pair.1), channel_id=1, source_target_pairs={{0,2},{1,3},{2,0},{3,1},{4,6},{5,7},{6,4},{7,5},{8,10},{9,11},{10,... | collective-permute-start | bytes 2359304 | tf_op jit(solution)/shard_map/ppermute | solution.py:248
  67.1 3.3 %collective-permute-start.12 = (bf16[32,2048]{1,0:T(8,128)(2,1)S(1)}, bf16[32,2048]{1,0:T(8,128)(2,1)S(1)}, u32[]{:S(2)}, u32[]{:S(2)}) collective-permute-start(bf16[32,2048]{1,0:T(8,128)(2,1)S(1)} %get-tuple-element.113), channel_id=1, source_target_pairs={{0,16},{4,20},{8,24},{12,28},{16,0},{20,4},{24,8},{28,12},{1,17},{... | collective-permute-start | bytes 393224 | tf_op jit(solution)/shard_map/ppermute | solution.py:248
  70.9 3.6 %collective-permute-start.14 = (bf16[32,2048]{1,0:T(8,128)(2,1)S(1)}, bf16[32,2048]{1,0:T(8,128)(2,1)S(1)}, u32[]{:S(2)}, u32[]{:S(2)}) collective-permute-start(bf16[32,2048]{1,0:T(8,128)(2,1)S(1)} %get-tuple-element.115), channel_id=1, source_target_pairs={{0,24},{4,28},{8,16},{12,20},{16,8},{20,12},{24,0},{28,4},{1,25},{... | collective-permute-start | bytes 393224 | tf_op jit(solution)/shard_map/ppermute | solution.py:248
  74.5 8.6 %collective-permute-done.12.refs_1_ = bf16[32,2048]{1,0:T(8,128)(2,1)S(1)} collective-permute-done((bf16[32,2048]{1,0:T(8,128)(2,1)S(1)}, bf16[32,2048]{1,0:T(8,128)(2,1)S(1)}, u32[]{:S(2)}, u32[]{:S(2)}) %collective-permute-start.12) | collective-permute-done | bytes 131104 | tf_op jit(solution)/shard_map/ppermute | solution.py:248
  83.2 3.3 %collective-permute-done.13.refs_2_ = bf16[32,2048]{1,0:T(8,128)(2,1)S(1)} collective-permute-done((bf16[32,2048]{1,0:T(8,128)(2,1)S(1)}, bf16[32,2048]{1,0:T(8,128)(2,1)S(1)}, u32[]{:S(2)}, u32[]{:S(2)}) %collective-permute-start.13) | collective-permute-done | bytes 131104 | tf_op jit(solution)/shard_map/ppermute | solution.py:248
  87.0 3.0 %collective-permute-start.20 = (bf16[24,2048]{1,0:T(8,128)(2,1)S(1)}, bf16[24,2048]{1,0:T(8,128)(2,1)S(1)}, u32[]{:S(2)}, u32[]{:S(2)}) collective-permute-start(bf16[24,2048]{1,0:T(8,128)(2,1)S(1)} %get-tuple-element.128), channel_id=1, source_target_pairs={{0,24},{4,28},{8,16},{12,20},{16,8},{20,12},{24,0},{28,4},{1,25},{... | collective-permute-start | bytes 294920 | tf_op jit(solution)/shard_map/ppermute | solution.py:248
  91.2 1.4 %collective-permute-start.23 = (bf16[24,2048]{1,0:T(8,128)(2,1)S(1)}, bf16[24,2048]{1,0:T(8,128)(2,1)S(1)}, u32[]{:S(2)}, u32[]{:S(2)}) collective-permute-start(bf16[24,2048]{1,0:T(8,128)(2,1)S(1)} %get-tuple-element.132), channel_id=1, source_target_pairs={{0,4},{4,0},{8,12},{12,8},{16,20},{20,16},{24,28},{28,24},{1,5},{5... | collective-permute-start | bytes 294920 | tf_op jit(solution)/shard_map/ppermute | solution.py:248
  93.1 1.6 %collective-permute-start.25 = (bf16[24,2048]{1,0:T(8,128)(2,1)S(1)}, bf16[24,2048]{1,0:T(8,128)(2,1)S(1)}, u32[]{:S(2)}, u32[]{:S(2)}) collective-permute-start(bf16[24,2048]{1,0:T(8,128)(2,1)S(1)} %get-tuple-element.134), channel_id=1, source_target_pairs={{0,12},{4,8},{8,4},{12,0},{16,28},{20,24},{24,20},{28,16},{1,13},{... | collective-permute-start | bytes 294920 | tf_op jit(solution)/shard_map/ppermute | solution.py:248
  94.7 5.8 %collective-permute-start.26 = (bf16[24,2048]{1,0:T(8,128)(2,1)S(1)}, bf16[24,2048]{1,0:T(8,128)(2,1)S(1)}, u32[]{:S(2)}, u32[]{:S(2)}) collective-permute-start(bf16[24,2048]{1,0:T(8,128)(2,1)S(1)} %get-tuple-element.135), channel_id=1, source_target_pairs={{0,20},{4,16},{8,28},{12,24},{16,4},{20,0},{24,12},{28,8},{1,21},{... | collective-permute-start | bytes 294920 | tf_op jit(solution)/shard_map/ppermute | solution.py:248
  100.5 3.1 %collective-permute-start.27 = (bf16[24,2048]{1,0:T(8,128)(2,1)S(1)}, bf16[24,2048]{1,0:T(8,128)(2,1)S(1)}, u32[]{:S(2)}, u32[]{:S(2)}) collective-permute-start(bf16[24,2048]{1,0:T(8,128)(2,1)S(1)} %get-tuple-element.137), channel_id=1, source_target_pairs={{0,28},{4,24},{8,20},{12,16},{16,12},{20,8},{24,4},{28,0},{1,29},{... | collective-permute-start | bytes 294920 | tf_op jit(solution)/shard_map/ppermute | solution.py:248
  104.6 2.4 %collective-permute-start.18 = (bf16[32,2048]{1,0:T(8,128)(2,1)S(1)}, bf16[32,2048]{1,0:T(8,128)(2,1)S(1)}, u32[]{:S(2)}, u32[]{:S(2)}) collective-permute-start(bf16[32,2048]{1,0:T(8,128)(2,1)S(1)} %get-tuple-element.123), channel_id=1, source_target_pairs={{0,12},{4,8},{8,4},{12,0},{16,28},{20,24},{24,20},{28,16},{1,13},{... | collective-permute-start | bytes 393224 | tf_op jit(solution)/shard_map/ppermute | solution.py:248
  107.1 2.2 %collective-permute-start.21 = (bf16[32,2048]{1,0:T(8,128)(2,1)S(1)}, bf16[32,2048]{1,0:T(8,128)(2,1)S(1)}, u32[]{:S(2)}, u32[]{:S(2)}) collective-permute-start(bf16[32,2048]{1,0:T(8,128)(2,1)S(1)} %get-tuple-element.129), channel_id=1, source_target_pairs={{0,28},{4,24},{8,20},{12,16},{16,12},{20,8},{24,4},{28,0},{1,29},{... | collective-permute-start | bytes 393224 | tf_op jit(solution)/shard_map/ppermute | solution.py:248
  109.3 2.4 %new_rows.1 = (bf16[24,2048]{1,0:T(8,128)(2,1)S(1)}, bf16[24,2048]{1,0:T(8,128)(2,1)S(1)}, bf16[24,2048]{1,0:T(8,128)(2,1)S(1)}, bf16[24,2048]{1,0:T(8,128)(2,1)...) custom-call(s32[8]{0:T(128)S(1)} %copy-done.6, ...), custom_call_target="tpu_custom_call" | custom-call | flops 2000000000 | bytes 5111840 | tf_op jit(solution)/shard_map/new_rows/pallas_call | solution.py:29
  111.8 2.2 %collective-permute-start.28 = (bf16[24,2048]{1,0:T(8,128)(2,1)S(1)}, bf16[24,2048]{1,0:T(8,128)(2,1)S(1)}, u32[]{:S(2)}, u32[]{:S(2)}) collective-permute-start(bf16[24,2048]{1,0:T(8,128)(2,1)S(1)} %get-tuple-element.148), channel_id=1, source_target_pairs={{0,16},{4,20},{8,24},{12,28},{16,0},{20,4},{24,8},{28,12},{1,17},{... | collective-permute-start | bytes 294920 | tf_op jit(solution)/shard_map/ppermute | solution.py:248
  113.9 2.6 %collective-permute-done.21.refs_7_ = bf16[32,2048]{1,0:T(8,128)(2,1)S(1)} collective-permute-done((bf16[32,2048]{1,0:T(8,128)(2,1)S(1)}, bf16[32,2048]{1,0:T(8,128)(2,1)S(1)}, u32[]{:S(2)}, u32[]{:S(2)}) %collective-permute-start.21) | collective-permute-done | bytes 131104 | tf_op jit(solution)/shard_map/ppermute | solution.py:248
  116.5 1.4 %collective-permute-start.29 = (bf16[24,2048]{1,0:T(8,128)(2,1)S(1)}, bf16[24,2048]{1,0:T(8,128)(2,1)S(1)}, u32[]{:S(2)}, u32[]{:S(2)}) collective-permute-start(bf16[24,2048]{1,0:T(8,128)(2,1)S(1)} %get-tuple-element.149), channel_id=1, source_target_pairs={{0,4},{4,0},{8,12},{12,8},{16,20},{20,16},{24,28},{28,24},{1,5},{5... | collective-permute-start | bytes 294920 | tf_op jit(solution)/shard_map/ppermute | solution.py:248
  117.9 3.2 %collective-permute-start.31 = (bf16[24,2048]{1,0:T(8,128)(2,1)S(1)}, bf16[24,2048]{1,0:T(8,128)(2,1)S(1)}, u32[]{:S(2)}, u32[]{:S(2)}) collective-permute-start(bf16[24,2048]{1,0:T(8,128)(2,1)S(1)} %get-tuple-element.151), channel_id=1, source_target_pairs={{0,8},{4,12},{8,0},{12,4},{16,24},{20,28},{24,16},{28,20},{1,9},{5... | collective-permute-start | bytes 294920 | tf_op jit(solution)/shard_map/ppermute | solution.py:248
  122.4 3.1 %collective-permute-start.34 = (bf16[24,2048]{1,0:T(8,128)(2,1)S(1)}, bf16[24,2048]{1,0:T(8,128)(2,1)S(1)}, u32[]{:S(2)}, u32[]{:S(2)}) collective-permute-start(bf16[24,2048]{1,0:T(8,128)(2,1)S(1)} %get-tuple-element.154), channel_id=1, source_target_pairs={{0,28},{4,24},{8,20},{12,16},{16,12},{20,8},{24,4},{28,0},{1,29},{... | collective-permute-start | bytes 294920 | tf_op jit(solution)/shard_map/ppermute | solution.py:248
  125.5 3.6 %new_state.1 = (f32[6,24,2048]{2,1,0:T(8,128)}, f32[6,24,2048]{2,1,0:T(8,128)}, f32[6,24,2048]{2,1,0:T(8,128)}) custom-call(s32[8]{0:T(128)S(1)} %copy-done.6, bf16[24,2048]{1,0:T(8,128)(2,1)S(1)} %get-tuple-element.130.refs_0_, bf16[24,2048]{1,0:T(8,128)(2,1)S(1)} %collective-permute-done.22.refs_1_, bf16[24,2048]{1,0:T(8,128)(2,1)S(1)} %collective-permute-done.23.refs_2_, ...), custom_call_target="tpu_custom_call" | custom-call | bytes 7864352 | tf_op jit(solution)/shard_map/new_state/pallas_call | solution.py:29
  (65 shorter events, 11.3 us)
Async XLA Ops:
  2.6 54.3 %collective-permute-start.7 = (bf16[576,2048]{1,0:T(8,128)(2,1)S(1)}, bf16[576,2048]{1,0:T(8,128)(2,1)S(1)}, u32[]{:S(2)}, u32[]{:S(2)}) collective-permute-start(bf16[576,2048]{1,0:T(8,128)(2,1)S(1)} %pad_maximum_fusion.refs_8_), channel_id=1, source_target_pairs={{0,2},{1,3},{2,0},{3,1},{4,6},{5,7},{6,4},{7,5},{8,10},{9,11},{10,... | collective-permute-start | bytes 7077896 | tf_op jit(solution)/shard_map/ppermute | solution.py:248
  5.6 52.1 %collective-permute-start.9 = (bf16[576,2048]{1,0:T(8,128)(2,1)S(1)}, bf16[576,2048]{1,0:T(8,128)(2,1)S(1)}, u32[]{:S(2)}, u32[]{:S(2)}) collective-permute-start(bf16[576,2048]{1,0:T(8,128)(2,1)S(1)} %pad_maximum_fusion.refs_8_), channel_id=1, source_target_pairs={{0,1},{1,0},{2,3},{3,2},{4,5},{5,4},{6,7},{7,6},{8,9},{9,8},{10,11... | collective-permute-start | bytes 7077896 | tf_op jit(solution)/shard_map/ppermute | solution.py:248
  6.5 21.3 %collective-permute-start = (bf16[64,2048]{1,0:T(8,128)(2,1)S(1)}, bf16[64,2048]{1,0:T(8,128)(2,1)S(1)}, u32[]{:S(2)}, u32[]{:S(2)}) collective-permute-start(bf16[64,2048]{1,0:T(8,128)(2,1)S(1)} %get-tuple-element.82), channel_id=1, source_target_pairs={{0,16},{4,20},{8,24},{12,28},{16,0},{20,4},{24,8},{28,12},{1,17},{... | collective-permute-start | bytes 786440 | tf_op jit(solution)/shard_map/ppermute | solution.py:248
  9.2 19.0 %collective-permute-start.1 = (bf16[64,2048]{1,0:T(8,128)(2,1)S(1)}, bf16[64,2048]{1,0:T(8,128)(2,1)S(1)}, u32[]{:S(2)}, u32[]{:S(2)}) collective-permute-start(bf16[64,2048]{1,0:T(8,128)(2,1)S(1)} %get-tuple-element.83), channel_id=1, source_target_pairs={{0,4},{4,0},{8,12},{12,8},{16,20},{20,16},{24,28},{28,24},{1,5},{5... | collective-permute-start | bytes 786440 | tf_op jit(solution)/shard_map/ppermute | solution.py:248
  10.7 23.7 %collective-permute-start.2 = (bf16[64,2048]{1,0:T(8,128)(2,1)S(1)}, bf16[64,2048]{1,0:T(8,128)(2,1)S(1)}, u32[]{:S(2)}, u32[]{:S(2)}) collective-permute-start(bf16[64,2048]{1,0:T(8,128)(2,1)S(1)} %get-tuple-element.84), channel_id=1, source_target_pairs={{0,20},{4,16},{8,28},{12,24},{16,4},{20,0},{24,12},{28,8},{1,21},{... | collective-permute-start | bytes 786440 | tf_op jit(solution)/shard_map/ppermute | solution.py:248
  27.8 16.6 %collective-permute-start.3 = (bf16[64,2048]{1,0:T(8,128)(2,1)S(1)}, bf16[64,2048]{1,0:T(8,128)(2,1)S(1)}, u32[]{:S(2)}, u32[]{:S(2)}) collective-permute-start(bf16[64,2048]{1,0:T(8,128)(2,1)S(1)} %get-tuple-element.85), channel_id=1, source_target_pairs={{0,8},{4,12},{8,0},{12,4},{16,24},{20,28},{24,16},{28,20},{1,9},{5... | collective-permute-start | bytes 786440 | tf_op jit(solution)/shard_map/ppermute | solution.py:248
  28.1 20.7 %collective-permute-start.4 = (bf16[64,2048]{1,0:T(8,128)(2,1)S(1)}, bf16[64,2048]{1,0:T(8,128)(2,1)S(1)}, u32[]{:S(2)}, u32[]{:S(2)}) collective-permute-start(bf16[64,2048]{1,0:T(8,128)(2,1)S(1)} %get-tuple-element.86), channel_id=1, source_target_pairs={{0,24},{4,28},{8,16},{12,20},{16,8},{20,12},{24,0},{28,4},{1,25},{... | collective-permute-start | bytes 786440 | tf_op jit(solution)/shard_map/ppermute | solution.py:248
  34.4 22.0 %collective-permute-start.5 = (bf16[64,2048]{1,0:T(8,128)(2,1)S(1)}, bf16[64,2048]{1,0:T(8,128)(2,1)S(1)}, u32[]{:S(2)}, u32[]{:S(2)}) collective-permute-start(bf16[64,2048]{1,0:T(8,128)(2,1)S(1)} %get-tuple-element.87), channel_id=1, source_target_pairs={{0,12},{4,8},{8,4},{12,0},{16,28},{20,24},{24,20},{28,16},{1,13},{... | collective-permute-start | bytes 786440 | tf_op jit(solution)/shard_map/ppermute | solution.py:248
  44.4 12.1 %collective-permute-start.6 = (bf16[64,2048]{1,0:T(8,128)(2,1)S(1)}, bf16[64,2048]{1,0:T(8,128)(2,1)S(1)}, u32[]{:S(2)}, u32[]{:S(2)}) collective-permute-start(bf16[64,2048]{1,0:T(8,128)(2,1)S(1)} %get-tuple-element.88), channel_id=1, source_target_pairs={{0,28},{4,24},{8,20},{12,16},{16,12},{20,8},{24,4},{28,0},{1,29},{... | collective-permute-start | bytes 786440 | tf_op jit(solution)/shard_map/ppermute | solution.py:248
  65.1 21.4 %collective-permute-start.15 = (bf16[192,2048]{1,0:T(8,128)(2,1)S(1)}, bf16[192,2048]{1,0:T(8,128)(2,1)S(1)}, u32[]{:S(2)}, u32[]{:S(2)}) collective-permute-start(bf16[192,2048]{1,0:T(8,128)(2,1)S(1)} %add_pair.1), channel_id=1, source_target_pairs={{0,2},{1,3},{2,0},{3,1},{4,6},{5,7},{6,4},{7,5},{8,10},{9,11},{10,... | collective-permute-start | bytes 2359304 | tf_op jit(solution)/shard_map/ppermute | solution.py:248
  66.9 19.6 %collective-permute-start.19 = (bf16[192,2048]{1,0:T(8,128)(2,1)S(1)}, bf16[192,2048]{1,0:T(8,128)(2,1)S(1)}, u32[]{:S(2)}, u32[]{:S(2)}) collective-permute-start(bf16[192,2048]{1,0:T(8,128)(2,1)S(1)} %get-tuple-element.126), channel_id=1, source_target_pairs={{0,1},{1,0},{2,3},{3,2},{4,5},{5,4},{6,7},{7,6},{8,9},{9,8},{10,11... | collective-permute-start | bytes 2359304 | tf_op jit(solution)/shard_map/ppermute | solution.py:248
  67.1 16.1 %collective-permute-start.12 = (bf16[32,2048]{1,0:T(8,128)(2,1)S(1)}, bf16[32,2048]{1,0:T(8,128)(2,1)S(1)}, u32[]{:S(2)}, u32[]{:S(2)}) collective-permute-start(bf16[32,2048]{1,0:T(8,128)(2,1)S(1)} %get-tuple-element.113), channel_id=1, source_target_pairs={{0,16},{4,20},{8,24},{12,28},{16,0},{20,4},{24,8},{28,12},{1,17},{... | collective-permute-start | bytes 393224 | tf_op jit(solution)/shard_map/ppermute | solution.py:248
  70.4 16.1 %collective-permute-start.13 = (bf16[32,2048]{1,0:T(8,128)(2,1)S(1)}, bf16[32,2048]{1,0:T(8,128)(2,1)S(1)}, u32[]{:S(2)}, u32[]{:S(2)}) collective-permute-start(bf16[32,2048]{1,0:T(8,128)(2,1)S(1)} %get-tuple-element.114), channel_id=1, source_target_pairs={{0,20},{4,16},{8,28},{12,24},{16,4},{20,0},{24,12},{28,8},{1,21},{... | collective-permute-start | bytes 393224 | tf_op jit(solution)/shard_map/ppermute | solution.py:248
  70.9 15.5 %collective-permute-start.14 = (bf16[32,2048]{1,0:T(8,128)(2,1)S(1)}, bf16[32,2048]{1,0:T(8,128)(2,1)S(1)}, u32[]{:S(2)}, u32[]{:S(2)}) collective-permute-start(bf16[32,2048]{1,0:T(8,128)(2,1)S(1)} %get-tuple-element.115), channel_id=1, source_target_pairs={{0,24},{4,28},{8,16},{12,20},{16,8},{20,12},{24,0},{28,4},{1,25},{... | collective-permute-start | bytes 393224 | tf_op jit(solution)/shard_map/ppermute | solution.py:248
  87.0 7.6 %collective-permute-start.20 = (bf16[24,2048]{1,0:T(8,128)(2,1)S(1)}, bf16[24,2048]{1,0:T(8,128)(2,1)S(1)}, u32[]{:S(2)}, u32[]{:S(2)}) collective-permute-start(bf16[24,2048]{1,0:T(8,128)(2,1)S(1)} %get-tuple-element.128), channel_id=1, source_target_pairs={{0,24},{4,28},{8,16},{12,20},{16,8},{20,12},{24,0},{28,4},{1,25},{... | collective-permute-start | bytes 294920 | tf_op jit(solution)/shard_map/ppermute | solution.py:248
  90.1 10.4 %collective-permute-start.22 = (bf16[24,2048]{1,0:T(8,128)(2,1)S(1)}, bf16[24,2048]{1,0:T(8,128)(2,1)S(1)}, u32[]{:S(2)}, u32[]{:S(2)}) collective-permute-start(bf16[24,2048]{1,0:T(8,128)(2,1)S(1)} %get-tuple-element.131), channel_id=1, source_target_pairs={{0,16},{4,20},{8,24},{12,28},{16,0},{20,4},{24,8},{28,12},{1,17},{... | collective-permute-start | bytes 294920 | tf_op jit(solution)/shard_map/ppermute | solution.py:248
  91.2 12.4 %collective-permute-start.23 = (bf16[24,2048]{1,0:T(8,128)(2,1)S(1)}, bf16[24,2048]{1,0:T(8,128)(2,1)S(1)}, u32[]{:S(2)}, u32[]{:S(2)}) collective-permute-start(bf16[24,2048]{1,0:T(8,128)(2,1)S(1)} %get-tuple-element.132), channel_id=1, source_target_pairs={{0,4},{4,0},{8,12},{12,8},{16,20},{20,16},{24,28},{28,24},{1,5},{5... | collective-permute-start | bytes 294920 | tf_op jit(solution)/shard_map/ppermute | solution.py:248
  92.6 12.0 %collective-permute-start.24 = (bf16[24,2048]{1,0:T(8,128)(2,1)S(1)}, bf16[24,2048]{1,0:T(8,128)(2,1)S(1)}, u32[]{:S(2)}, u32[]{:S(2)}) collective-permute-start(bf16[24,2048]{1,0:T(8,128)(2,1)S(1)} %get-tuple-element.133), channel_id=1, source_target_pairs={{0,8},{4,12},{8,0},{12,4},{16,24},{20,28},{24,16},{28,20},{1,9},{5... | collective-permute-start | bytes 294920 | tf_op jit(solution)/shard_map/ppermute | solution.py:248
  93.1 11.6 %collective-permute-start.25 = (bf16[24,2048]{1,0:T(8,128)(2,1)S(1)}, bf16[24,2048]{1,0:T(8,128)(2,1)S(1)}, u32[]{:S(2)}, u32[]{:S(2)}) collective-permute-start(bf16[24,2048]{1,0:T(8,128)(2,1)S(1)} %get-tuple-element.134), channel_id=1, source_target_pairs={{0,12},{4,8},{8,4},{12,0},{16,28},{20,24},{24,20},{28,16},{1,13},{... | collective-permute-start | bytes 294920 | tf_op jit(solution)/shard_map/ppermute | solution.py:248
  94.7 12.4 %collective-permute-start.26 = (bf16[24,2048]{1,0:T(8,128)(2,1)S(1)}, bf16[24,2048]{1,0:T(8,128)(2,1)S(1)}, u32[]{:S(2)}, u32[]{:S(2)}) collective-permute-start(bf16[24,2048]{1,0:T(8,128)(2,1)S(1)} %get-tuple-element.135), channel_id=1, source_target_pairs={{0,20},{4,16},{8,28},{12,24},{16,4},{20,0},{24,12},{28,8},{1,21},{... | collective-permute-start | bytes 294920 | tf_op jit(solution)/shard_map/ppermute | solution.py:248
  100.5 8.9 %collective-permute-start.27 = (bf16[24,2048]{1,0:T(8,128)(2,1)S(1)}, bf16[24,2048]{1,0:T(8,128)(2,1)S(1)}, u32[]{:S(2)}, u32[]{:S(2)}) collective-permute-start(bf16[24,2048]{1,0:T(8,128)(2,1)S(1)} %get-tuple-element.137), channel_id=1, source_target_pairs={{0,28},{4,24},{8,20},{12,16},{16,12},{20,8},{24,4},{28,0},{1,29},{... | collective-permute-start | bytes 294920 | tf_op jit(solution)/shard_map/ppermute | solution.py:248
  103.6 14.3 %collective-permute-start.16 = (bf16[32,2048]{1,0:T(8,128)(2,1)S(1)}, bf16[32,2048]{1,0:T(8,128)(2,1)S(1)}, u32[]{:S(2)}, u32[]{:S(2)}) collective-permute-start(bf16[32,2048]{1,0:T(8,128)(2,1)S(1)} %get-tuple-element.121), channel_id=1, source_target_pairs={{0,4},{4,0},{8,12},{12,8},{16,20},{20,16},{24,28},{28,24},{1,5},{5... | collective-permute-start | bytes 393224 | tf_op jit(solution)/shard_map/ppermute | solution.py:248
  104.6 13.3 %collective-permute-start.17 = (bf16[32,2048]{1,0:T(8,128)(2,1)S(1)}, bf16[32,2048]{1,0:T(8,128)(2,1)S(1)}, u32[]{:S(2)}, u32[]{:S(2)}) collective-permute-start(bf16[32,2048]{1,0:T(8,128)(2,1)S(1)} %get-tuple-element.122), channel_id=1, source_target_pairs={{0,8},{4,12},{8,0},{12,4},{16,24},{20,28},{24,16},{28,20},{1,9},{5... | collective-permute-start | bytes 393224 | tf_op jit(solution)/shard_map/ppermute | solution.py:248
  104.6 16.5 %collective-permute-start.18 = (bf16[32,2048]{1,0:T(8,128)(2,1)S(1)}, bf16[32,2048]{1,0:T(8,128)(2,1)S(1)}, u32[]{:S(2)}, u32[]{:S(2)}) collective-permute-start(bf16[32,2048]{1,0:T(8,128)(2,1)S(1)} %get-tuple-element.123), channel_id=1, source_target_pairs={{0,12},{4,8},{8,4},{12,0},{16,28},{20,24},{24,20},{28,16},{1,13},{... | collective-permute-start | bytes 393224 | tf_op jit(solution)/shard_map/ppermute | solution.py:248
  107.1 9.5 %collective-permute-start.21 = (bf16[32,2048]{1,0:T(8,128)(2,1)S(1)}, bf16[32,2048]{1,0:T(8,128)(2,1)S(1)}, u32[]{:S(2)}, u32[]{:S(2)}) collective-permute-start(bf16[32,2048]{1,0:T(8,128)(2,1)S(1)} %get-tuple-element.129), channel_id=1, source_target_pairs={{0,28},{4,24},{8,20},{12,16},{16,12},{20,8},{24,4},{28,0},{1,29},{... | collective-permute-start | bytes 393224 | tf_op jit(solution)/shard_map/ppermute | solution.py:248
  111.8 10.6 %collective-permute-start.28 = (bf16[24,2048]{1,0:T(8,128)(2,1)S(1)}, bf16[24,2048]{1,0:T(8,128)(2,1)S(1)}, u32[]{:S(2)}, u32[]{:S(2)}) collective-permute-start(bf16[24,2048]{1,0:T(8,128)(2,1)S(1)} %get-tuple-element.148), channel_id=1, source_target_pairs={{0,16},{4,20},{8,24},{12,28},{16,0},{20,4},{24,8},{28,12},{1,17},{... | collective-permute-start | bytes 294920 | tf_op jit(solution)/shard_map/ppermute | solution.py:248
  116.5 5.9 %collective-permute-start.29 = (bf16[24,2048]{1,0:T(8,128)(2,1)S(1)}, bf16[24,2048]{1,0:T(8,128)(2,1)S(1)}, u32[]{:S(2)}, u32[]{:S(2)}) collective-permute-start(bf16[24,2048]{1,0:T(8,128)(2,1)S(1)} %get-tuple-element.149), channel_id=1, source_target_pairs={{0,4},{4,0},{8,12},{12,8},{16,20},{20,16},{24,28},{28,24},{1,5},{5... | collective-permute-start | bytes 294920 | tf_op jit(solution)/shard_map/ppermute | solution.py:248
  117.9 12.3 %collective-permute-start.30 = (bf16[24,2048]{1,0:T(8,128)(2,1)S(1)}, bf16[24,2048]{1,0:T(8,128)(2,1)S(1)}, u32[]{:S(2)}, u32[]{:S(2)}) collective-permute-start(bf16[24,2048]{1,0:T(8,128)(2,1)S(1)} %get-tuple-element.150), channel_id=1, source_target_pairs={{0,20},{4,16},{8,28},{12,24},{16,4},{20,0},{24,12},{28,8},{1,21},{... | collective-permute-start | bytes 294920 | tf_op jit(solution)/shard_map/ppermute | solution.py:248
  117.9 12.3 %collective-permute-start.31 = (bf16[24,2048]{1,0:T(8,128)(2,1)S(1)}, bf16[24,2048]{1,0:T(8,128)(2,1)S(1)}, u32[]{:S(2)}, u32[]{:S(2)}) collective-permute-start(bf16[24,2048]{1,0:T(8,128)(2,1)S(1)} %get-tuple-element.151), channel_id=1, source_target_pairs={{0,8},{4,12},{8,0},{12,4},{16,24},{20,28},{24,16},{28,20},{1,9},{5... | collective-permute-start | bytes 294920 | tf_op jit(solution)/shard_map/ppermute | solution.py:248
  121.1 9.1 %collective-permute-start.32 = (bf16[24,2048]{1,0:T(8,128)(2,1)S(1)}, bf16[24,2048]{1,0:T(8,128)(2,1)S(1)}, u32[]{:S(2)}, u32[]{:S(2)}) collective-permute-start(bf16[24,2048]{1,0:T(8,128)(2,1)S(1)} %get-tuple-element.152), channel_id=1, source_target_pairs={{0,24},{4,28},{8,16},{12,20},{16,8},{20,12},{24,0},{28,4},{1,25},{... | collective-permute-start | bytes 294920 | tf_op jit(solution)/shard_map/ppermute | solution.py:248
  122.4 8.3 %collective-permute-start.33 = (bf16[24,2048]{1,0:T(8,128)(2,1)S(1)}, bf16[24,2048]{1,0:T(8,128)(2,1)S(1)}, u32[]{:S(2)}, u32[]{:S(2)}) collective-permute-start(bf16[24,2048]{1,0:T(8,128)(2,1)S(1)} %get-tuple-element.153), channel_id=1, source_target_pairs={{0,12},{4,8},{8,4},{12,0},{16,28},{20,24},{24,20},{28,16},{1,13},{... | collective-permute-start | bytes 294920 | tf_op jit(solution)/shard_map/ppermute | solution.py:248
  122.4 8.3 %collective-permute-start.34 = (bf16[24,2048]{1,0:T(8,128)(2,1)S(1)}, bf16[24,2048]{1,0:T(8,128)(2,1)S(1)}, u32[]{:S(2)}, u32[]{:S(2)}) collective-permute-start(bf16[24,2048]{1,0:T(8,128)(2,1)S(1)} %get-tuple-element.154), channel_id=1, source_target_pairs={{0,28},{4,24},{8,20},{12,16},{16,12},{20,8},{24,4},{28,0},{1,29},{... | collective-permute-start | bytes 294920 | tf_op jit(solution)/shard_map/ppermute | solution.py:248
  (10 other events, 204.4 us)
